TPU v7x, 256 devices: a whole 4x4x8 slice. The times are simulated.
256 devices in a mesh: row: 16 (over y, x), col: 16 (over z, core).
Axes of the slice: x: 4, y: 4, z: 8, core: 2. Of those that a mesh axis runs over, the one named last changes fastest.
Arguments:
- rhs_one: bfloat16 [16, 16, 2, 256, 512], P('row', 'col'), may hold values from -6 to 6
- inv_one: bfloat16 [16, 16, 2, 256, 256], P('row', 'col'), as said below
- rhs_two: bfloat16 [16, 16, 1, 256, 512], P('row', 'col'), may hold values from -6 to 6
- inv_two: bfloat16 [16, 16, 1, 256, 256], P('row', 'col'), as said below
- blocks: bfloat16 [16, 16, 80, 256, 256], P('row', 'col'), may hold values from -0.0390625 to 0.0390625
- block_rows: int32 [16, 16, 80], P('row', 'col'), may hold values from 0 to 15
- block_cols: int32 [16, 16, 80], P('row', 'col'), may hold values from 0 to 31
Outputs:
- solved_one: bfloat16 [16, 16, 2, 256, 512], P('row', 'col')
- solved_two: bfloat16 [16, 16, 1, 256, 512], P('row', 'col')
Inputs may be any that keep to these rules, and one draw needn't show every extreme that they name: `inv_one`: each 256 by 256 block is lower triangular with diagonal entries from 0.5 to 1.5. `inv_two`: each 256 by 256 block is lower triangular with diagonal entries from 0.5 to 1.5.
All inputs are finite; a program needn't handle non-finite values.
Results may differ from a plain program's by a relative error of at most 0.0055.
Values may be sent and summed in bfloat16 or wider, within the bound.
No kernel may reach another device: no remote copies, remote signals or barrier semaphores. Data moves between devices by JAX's collectives and lax.ppermute only.
A program may use at most 128 MiB of HBM per device.

v0:
```python
import jax
import jax.numpy as jnp
from jax import lax
from jax.sharding import PartitionSpec as P

GROUP = 16


def apply_inverse(inverse, values):
    return jnp.einsum("qvw,qwr->qvr", inverse, values, preferred_element_type=jnp.float32).astype(
        jnp.bfloat16
    )


def local(rhs_one, inv_one, rhs_two, inv_two, blocks, block_rows, block_cols):
    solved_one = apply_inverse(inv_one[0, 0], rhs_one[0, 0])
    column = lax.all_gather(solved_one, "row", axis=0, tiled=True)
    owners = rhs_two.shape[2]
    peers = lax.axis_size("col")
    targets_all = peers * owners
    block_count = blocks.shape[2]
    block_width = blocks.shape[3]
    sources_all = column.shape[0]
    rhs_count = column.shape[2]
    groups = block_count // GROUP
    factor_groups = blocks[0, 0].reshape(groups, GROUP, block_width, block_width)
    row_groups = block_rows[0, 0].reshape(groups, GROUP)
    col_groups = block_cols[0, 0].reshape(groups, GROUP)
    flat_column = column.reshape(sources_all, block_width * rhs_count)
    source_labels = jnp.arange(sources_all, dtype=jnp.int32)
    target_labels = jnp.arange(targets_all, dtype=jnp.int32)

    def accumulate(running, bundle):
        factor, targets, sources = bundle
        picker = (sources[:, None] == source_labels[None, :]).astype(jnp.bfloat16)
        picked = jnp.dot(picker, flat_column, preferred_element_type=jnp.float32).astype(
            jnp.bfloat16
        )
        picked = picked.reshape(GROUP, block_width, rhs_count)
        product = jnp.einsum("kvw,kwr->kvr", factor, picked, preferred_element_type=jnp.float32)
        selector = (target_labels[:, None] == targets[None, :]).astype(jnp.float32)
        added = jnp.dot(
            selector,
            product.reshape(GROUP, block_width * rhs_count),
            precision=lax.Precision.HIGHEST,
        )
        return (running + added, None)

    initial = jnp.zeros((targets_all, block_width * rhs_count), jnp.float32)
    flat_sums, unused = lax.scan(accumulate, initial, (factor_groups, row_groups, col_groups))
    partial_sums = flat_sums.reshape(targets_all, block_width, rhs_count)
    summed = lax.psum_scatter(partial_sums, "col", scatter_dimension=0, tiled=True)
    residual = (rhs_two[0, 0].astype(jnp.float32) - summed).astype(jnp.bfloat16)
    solved_two = apply_inverse(inv_two[0, 0], residual)
    return (solved_one[None, None], solved_two[None, None])


def solution(mesh):
    in_specs = (
        P("row", "col", None, None, None),
        P("row", "col", None, None, None),
        P("row", "col", None, None, None),
        P("row", "col", None, None, None),
        P("row", "col", None, None, None),
        P("row", "col", None),
        P("row", "col", None),
    )
    out_specs = (P("row", "col", None, None, None), P("row", "col", None, None, None))
    return jax.shard_map(local, mesh=mesh, in_specs=in_specs, out_specs=out_specs, check_vma=False)
```

profile of v0, /device:TPU:1, one launch (start us, length us, event | category | flops | bytes accessed | tf_op | source)
XLA Modules:
  0.0 301.2 jit_solution(12375283930900828143)
XLA Ops:
  7.2 0.0 copy-start
  7.2 0.0 all-gather.2.cloned.1.call-start
  7.2 1.0 copy-done
  8.2 2.0 convolution_convert_fusion.1
  10.3 0.0 all-gather.2.cloned.1.call-update
  10.3 0.0 reduce-scatter.2.cloned.1.call-start
  10.3 0.5 broadcast.14
  10.9 1.3 reduce.6
  12.2 1.3 reduce.7
  13.4 0.1 reshape_squeeze.11
  13.5 0.1 reshape_squeeze.9
  13.6 77.0 %all-gather.2.cloned.1.call-done = bf16[32,256,512]{2,1,0:T(8,128)(2,1)} async-done(((bf16[2,256,512]{2,1,0:T(8,128)(2,1)}), bf16[32,256,512]{2,1,0:T(8,128)(2,1)}) %all-gather.2.cloned.1.call-update) | async-done | bytes 8388624 | tf_op jit(solution)/shard_map/all_gather | solution.py:17
  90.6 11.4 %copy.13 = bf16[4,8,256,512]{3,1,2,0:T(8,128)(2,1)} copy(bf16[4,8,256,512]{3,2,1,0:T(8,128)(2,1)} %bitcast.68) | data formatting | bytes 16777216
  102.0 111.1 %while.11 = (s32[]{:T(128)}, f32[16,131072]{1,0:T(8,128)}, s32[5,16]{1,0:T(8,128)S(1)}, bf16[5,16,256,256]{3,2,1,0:T(8,128)(2,1)}, s32[5,16]{1,0:T(8,128)S(1)}, ...) while((s32[]{:T(128)}, f32[16,131072]{1,0:T(8,128)}, s32[5,16]{1,0:T(8,128)S(1)}, ...), condition=%wide.region_1.2_spmd.clone, body=%wide.region_0.1_spmd.clone.sunk | while | flops 1616904960 | bytes 77595112 | solution.py:50
  102.0 4.7 %convolution_convert_fusion.4 = bf16[16,131072]{1,0:T(8,128)(2,1)S(1)} fusion(bf16[32,131072]{1,0:T(8,128)(2,1)} %get-tuple-element.150, s32[16]{0:T(128)S(1)} %get-tuple-element.127), kind=kOutput, calls=%fused_computation.3.clone.1 | convolution fusion | flops 136315392 | bytes 12582976 | tf_op jit(solution)/shard_map/while/body/eval_jaxpr/dot_general | solution.py:36
  106.7 1.4 copy.17
  108.2 2.9 fusion.34
  111.0 4.9 %copy.18 = f32[2,8,256,512]{3,1,2,0:T(8,128)S(1)} copy(f32[2,8,256,512]{3,2,1,0:T(8,128)S(1)} %bitcast.61) | data formatting | bytes 16777216 | tf_op jit(solution)/shard_map/while
  115.9 6.6 %convolution_add_fusion.2 = f32[16,131072]{1,0:T(8,128)} fusion(f32[16,131072]{1,0:T(8,128)S(1)} %bitcast.60, f32[16,131072]{1,0:T(8,128)} %get-tuple-element.138, pred[]{:T(512)S(6)} %compare.3, s32[16]{0:T(128)S(1)} %get-tuple-element.128), kind=kOutput, calls=%fused_computation.2.clone.1 | convolution fusion | flops 406847744 | bytes 25165888 | tf_op jit(solution)/shard_map/while/body/eval_jaxpr/dot_general | solution.py:42
  122.5 4.7 %convolution_convert_fusion.4 = bf16[16,131072]{1,0:T(8,128)(2,1)S(1)} fusion(bf16[32,131072]{1,0:T(8,128)(2,1)} %get-tuple-element.150, s32[16]{0:T(128)S(1)} %get-tuple-element.127), kind=kOutput, calls=%fused_computation.3.clone.1 | convolution fusion | flops 136315392 | bytes 12582976 | tf_op jit(solution)/shard_map/while/body/eval_jaxpr/dot_general | solution.py:36
  127.2 1.4 copy.17
  128.6 2.9 fusion.34
  131.5 4.9 %copy.18 = f32[2,8,256,512]{3,1,2,0:T(8,128)S(1)} copy(f32[2,8,256,512]{3,2,1,0:T(8,128)S(1)} %bitcast.61) | data formatting | bytes 16777216 | tf_op jit(solution)/shard_map/while
  136.4 8.8 %convolution_add_fusion.2 = f32[16,131072]{1,0:T(8,128)} fusion(f32[16,131072]{1,0:T(8,128)S(1)} %bitcast.60, f32[16,131072]{1,0:T(8,128)} %get-tuple-element.138, pred[]{:T(512)S(6)} %compare.3, s32[16]{0:T(128)S(1)} %get-tuple-element.128), kind=kOutput, calls=%fused_computation.2.clone.1 | convolution fusion | flops 406847744 | bytes 25165888 | tf_op jit(solution)/shard_map/while/body/eval_jaxpr/dot_general | solution.py:42
  145.2 4.7 %convolution_convert_fusion.4 = bf16[16,131072]{1,0:T(8,128)(2,1)S(1)} fusion(bf16[32,131072]{1,0:T(8,128)(2,1)} %get-tuple-element.150, s32[16]{0:T(128)S(1)} %get-tuple-element.127), kind=kOutput, calls=%fused_computation.3.clone.1 | convolution fusion | flops 136315392 | bytes 12582976 | tf_op jit(solution)/shard_map/while/body/eval_jaxpr/dot_general | solution.py:36
  149.8 1.4 copy.17
  151.3 2.9 fusion.34
  154.1 4.9 %copy.18 = f32[2,8,256,512]{3,1,2,0:T(8,128)S(1)} copy(f32[2,8,256,512]{3,2,1,0:T(8,128)S(1)} %bitcast.61) | data formatting | bytes 16777216 | tf_op jit(solution)/shard_map/while
  159.0 8.8 %convolution_add_fusion.2 = f32[16,131072]{1,0:T(8,128)} fusion(f32[16,131072]{1,0:T(8,128)S(1)} %bitcast.60, f32[16,131072]{1,0:T(8,128)} %get-tuple-element.138, pred[]{:T(512)S(6)} %compare.3, s32[16]{0:T(128)S(1)} %get-tuple-element.128), kind=kOutput, calls=%fused_computation.2.clone.1 | convolution fusion | flops 406847744 | bytes 25165888 | tf_op jit(solution)/shard_map/while/body/eval_jaxpr/dot_general | solution.py:42
  167.8 4.7 %convolution_convert_fusion.4 = bf16[16,131072]{1,0:T(8,128)(2,1)S(1)} fusion(bf16[32,131072]{1,0:T(8,128)(2,1)} %get-tuple-element.150, s32[16]{0:T(128)S(1)} %get-tuple-element.127), kind=kOutput, calls=%fused_computation.3.clone.1 | convolution fusion | flops 136315392 | bytes 12582976 | tf_op jit(solution)/shard_map/while/body/eval_jaxpr/dot_general | solution.py:36
  172.5 1.4 copy.17
  173.9 2.9 fusion.34
  176.8 4.9 %copy.18 = f32[2,8,256,512]{3,1,2,0:T(8,128)S(1)} copy(f32[2,8,256,512]{3,2,1,0:T(8,128)S(1)} %bitcast.61) | data formatting | bytes 16777216 | tf_op jit(solution)/shard_map/while
  181.6 8.8 %convolution_add_fusion.2 = f32[16,131072]{1,0:T(8,128)} fusion(f32[16,131072]{1,0:T(8,128)S(1)} %bitcast.60, f32[16,131072]{1,0:T(8,128)} %get-tuple-element.138, pred[]{:T(512)S(6)} %compare.3, s32[16]{0:T(128)S(1)} %get-tuple-element.128), kind=kOutput, calls=%fused_computation.2.clone.1 | convolution fusion | flops 406847744 | bytes 25165888 | tf_op jit(solution)/shard_map/while/body/eval_jaxpr/dot_general | solution.py:42
  190.4 4.7 %convolution_convert_fusion.4 = bf16[16,131072]{1,0:T(8,128)(2,1)S(1)} fusion(bf16[32,131072]{1,0:T(8,128)(2,1)} %get-tuple-element.150, s32[16]{0:T(128)S(1)} %get-tuple-element.127), kind=kOutput, calls=%fused_computation.3.clone.1 | convolution fusion | flops 136315392 | bytes 12582976 | tf_op jit(solution)/shard_map/while/body/eval_jaxpr/dot_general | solution.py:36
  195.1 1.4 copy.17
  196.6 2.9 fusion.34
  199.4 4.9 %copy.18 = f32[2,8,256,512]{3,1,2,0:T(8,128)S(1)} copy(f32[2,8,256,512]{3,2,1,0:T(8,128)S(1)} %bitcast.61) | data formatting | bytes 16777216 | tf_op jit(solution)/shard_map/while
  204.3 8.8 %convolution_add_fusion.2 = f32[16,131072]{1,0:T(8,128)} fusion(f32[16,131072]{1,0:T(8,128)S(1)} %bitcast.60, f32[16,131072]{1,0:T(8,128)} %get-tuple-element.138, pred[]{:T(512)S(6)} %compare.3, s32[16]{0:T(128)S(1)} %get-tuple-element.128), kind=kOutput, calls=%fused_computation.2.clone.1 | convolution fusion | flops 406847744 | bytes 25165888 | tf_op jit(solution)/shard_map/while/body/eval_jaxpr/dot_general | solution.py:42
  213.1 0.0 copy-start.1
  213.1 11.5 %copy.14 = f32[2,8,256,512]{3,2,1,0:T(8,128)} copy(f32[2,8,256,512]{3,1,2,0:T(8,128)} %bitcast.65) | data formatting | bytes 16777216
  224.6 0.0 copy-start.2
  224.6 0.0 copy-start.3
  224.6 0.0 reduce-scatter.2.cloned.1.call-update
  224.6 67.5 %reduce-scatter.2.cloned.1.call-done = f32[1,256,512]{2,1,0:T(8,128)} async-done(((f32[16,256,512]{2,1,0:T(8,128)}), f32[1,256,512]{2,1,0:T(8,128)}) %reduce-scatter.2.cloned.1.call-update) | async-done | bytes 524304 | tf_op jit(solution)/shard_map/reduce_scatter | solution.py:52
  292.1 0.0 copy-done.2
  292.1 0.0 copy-done.3
  292.1 1.3 fusion.12
  293.5 0.8 copy.10
  294.3 0.0 copy-done.1
  (6 shorter events, 0.0 us)
Async XLA Ops:
  7.2 1.1 copy-start
  7.2 83.4 %all-gather.2.cloned.1.call-start = ((), (), s32[]{:S(2)}) async-start(), calls=%async_computation.1 | async-start | bytes 8912896 | tf_op jit(solution)/shard_map/all_gather | solution.py:17
  10.3 281.8 %reduce-scatter.2.cloned.1.call-start = ((), (), s32[]{:S(2)}) async-start(), calls=%async_computation.2 | async-start | bytes 8912896 | tf_op jit(solution)/shard_map/reduce_scatter | solution.py:52
  213.1 81.2 %copy-start.1 = (bf16[1,1,2,256,512]{4,3,2,1,0:T(8,128)(2,1)S(1)}, bf16[1,1,2,256,512]{4,3,2,1,0:T(8,128)(2,1)}, u32[]{:S(2)}) copy-start(bf16[1,1,2,256,512]{4,3,2,1,0:T(8,128)(2,1)} %param.9) | copy-start | bytes 1572868
  224.6 67.5 %copy-start.2 = (bf16[1,1,1,256,512]{4,3,2,1,0:T(8,128)(2,1)S(1)}, bf16[1,1,1,256,512]{4,3,2,1,0:T(8,128)(2,1)}, u32[]{:S(2)}) copy-start(bf16[1,1,1,256,512]{4,3,2,1,0:T(8,128)(2,1)} %param.11) | copy-start | bytes 786436
  224.6 67.5 %copy-start.3 = (bf16[1,1,1,256,256]{4,3,2,1,0:T(8,128)(2,1)S(1)}, bf16[1,1,1,256,256]{4,3,2,1,0:T(8,128)(2,1)}, u32[]{:S(2)}) copy-start(bf16[1,1,1,256,256]{4,3,2,1,0:T(8,128)(2,1)} %param.12) | copy-start | bytes 393220
Sparse Core Ops, SparseCore 0:
  11.0 79.5 all-gather.1
  224.8 67.3 reduce-scatter.1
where the time goes:
time: 304 us; the launch traced here: 301 us
  waiting for transfers between devices  145 us (48%)
  matrix products  82.8 us (27%)
  local copies, waits for them, and re-layouts  57 us (19%)
  between operations  14.1 us (5%)
    all_gather x1, waiting for transfers between devices, local(): column = lax.all_gather(solved_one, 'row', axis=0, tiled=True)  77 us
    reduce_scatter x1, waiting for transfers between devices, local(): lax.psum_scatter(partial_sums, 'col', scatter_dimension=0, tiled=True)  67.5 us
    dot_general x5, matrix products, accumulate(): jnp.dot(selector, product.reshape(GROUP, block_width * rhs_count), precis...  41.8 us
    while x10, local copies, waits for them, and re-layouts  31.5 us
    unnamed x12, local copies, waits for them, and re-layouts  25.3 us
    dot_general x5, matrix products, accumulate(): jnp.dot(picker, flat_column, preferred_element_type=jnp.float32)  23.4 us
    dot_general x5, matrix products, accumulate(): jnp.einsum('kvw,kwr->kvr', factor, picked, preferred_element_type=jnp.flo...  14.2 us
  transfers between devices with their start and end apart: 2, of which 2 were waited for; matrix products, arithmetic and copies ran while one was open for 1% of the time, Pallas kernels for 0%

commit v1 on v0

v1 whole, which is shorter than its diff:
```python
import functools

import jax
import jax.numpy as jnp
from jax import lax
from jax.experimental import pallas as pl
from jax.experimental.pallas import tpu as pltpu
from jax.sharding import PartitionSpec as P

WIDTHS = (512,)
STEP = 8
BOTH = ("row", "col")
VMEM_LIMIT = 48 * 1024 * 1024
F32 = jnp.float32
BF16 = jnp.bfloat16


def whole(memory=pltpu.VMEM):
    return pl.BlockSpec(memory_space=memory)


def shape(dims, dtype=BF16):
    return jax.ShapeDtypeStruct(dims, dtype)


def params():
    return pltpu.CompilerParams(vmem_limit_bytes=VMEM_LIMIT)


def ring_pairs(axis, steps):
    pairs = []
    for y in range(4):
        for x in range(4):
            for z in range(8):
                for core in range(2):
                    way = steps if core == 0 else -steps
                    to_y, to_x, to_z = y, x, z
                    if axis == "x":
                        to_x = (x + way) % 4
                    elif axis == "y":
                        to_y = (y + way) % 4
                    else:
                        to_z = (z + way) % 8
                    pairs.append(((y * 4 + x) * 16 + z * 2 + core, (to_y * 4 + to_x) * 16 + to_z * 2 + core))
    return pairs


def move(value, axis, steps):
    return lax.ppermute(value, BOTH, ring_pairs(axis, steps))


def swap_cores(value):
    return lax.ppermute(value, "col", [(i, i ^ 1) for i in range(16)])


def solve_one_kernel(widths, rhs, inverse, solved, *parts):
    for q in range(2):
        value = jnp.dot(inverse[q], rhs[q], preferred_element_type=F32).astype(BF16)
        solved[q] = value
        start = 0
        for i, width in enumerate(widths):
            parts[2 * i + q][0] = value[:, start : start + width]
            start += width


def solve_one(rhs, inverse, widths):
    outs = [shape(rhs.shape)]
    for width in widths:
        outs += [shape((1, rhs.shape[1], width))] * 2
    return pl.pallas_call(
        functools.partial(solve_one_kernel, widths),
        out_shape=outs,
        in_specs=[whole()] * 2,
        out_specs=[whole()] * len(outs),
        compiler_params=params(),
    )(rhs, inverse)


def couple_kernel(places, source_slot, target_slot, blocks, *refs):
    count = len(places)
    pieces = refs[:count]
    keep, send, sources, total, sems = refs[count:]
    step = pl.program_id(0)

    @pl.when(step == 0)
    def _():
        copies = []
        for i, (piece, (start, size)) in enumerate(zip(pieces, places)):
            copies.append(pltpu.make_async_copy(piece, sources.at[pl.ds(start, size)], sems.at[i]))
            copies[-1].start()
        total[...] = jnp.zeros_like(total)
        for copy in copies:
            copy.wait()

    for j in range(STEP):
        index = step * STEP + j
        product = jnp.dot(blocks[j], sources[source_slot[index]], preferred_element_type=F32)
        total[target_slot[index]] += product

    @pl.when(step == pl.num_programs(0) - 1)
    def _():
        keep[...] = total[:8]
        send[...] = total[8:].astype(BF16)


def couple(source_slot, target_slot, blocks, pieces, places):
    count, rows, _ = blocks.shape
    width = pieces[0].shape[-1]
    return pl.pallas_call(
        functools.partial(couple_kernel, places),
        out_shape=[shape((8, rows, width), F32), shape((8, rows, width))],
        grid_spec=pltpu.PrefetchScalarGridSpec(
            num_scalar_prefetch=2,
            grid=(count // STEP,),
            in_specs=[pl.BlockSpec((STEP, rows, rows), lambda i, *_: (i, 0, 0))] + [whole(pl.ANY)] * len(pieces),
            out_specs=[pl.BlockSpec((8, rows, width), lambda i, *_: (0, 0, 0))] * 2,
            scratch_shapes=[
                pltpu.VMEM((32, rows, width), BF16),
                pltpu.VMEM((16, rows, width), F32),
                pltpu.SemaphoreType.DMA((len(pieces),)),
            ],
        ),
        compiler_params=params(),
        cost_estimate=pl.CostEstimate(
            flops=2 * count * rows * rows * width, bytes_accessed=2 * count * rows * rows, transcendentals=0
        ),
    )(source_slot, target_slot, blocks, *pieces)


def first_kernel(keep, other, near_fwd, near_bwd, far_fwd, far_bwd, kept):
    def part(u):
        return keep[u] + other[u].astype(F32)

    near_fwd[0] = part(1).astype(BF16)
    near_fwd[1] = part(3).astype(BF16)
    near_bwd[0] = part(7).astype(BF16)
    near_bwd[1] = part(5).astype(BF16)
    half = far_fwd.shape[0]
    middle = part(4).astype(BF16)
    far_fwd[...] = middle[:half]
    far_bwd[...] = middle[half:]
    kept[0] = part(0)
    kept[1] = part(2)
    kept[2] = part(6)


def second_kernel(kept, fwd, bwd, far_fwd, far_bwd, out_fwd, out_bwd, own):
    half = far_fwd.shape[0]
    ahead = kept[1] + fwd[1].astype(F32)
    out_fwd[:half] = (ahead[:half] + far_fwd[...].astype(F32)).astype(BF16)
    out_fwd[half:] = ahead[half:].astype(BF16)
    behind = kept[2] + bwd[1].astype(F32)
    out_bwd[:half] = behind[:half].astype(BF16)
    out_bwd[half:] = (behind[half:] + far_bwd[...].astype(F32)).astype(BF16)
    own[...] = kept[0] + fwd[0].astype(F32) + bwd[0].astype(F32)


def last_kernel(own, fwd, bwd, rhs, inverse, solved):
    coupled = own[...] + (fwd[...].astype(F32) + bwd[...].astype(F32))
    residual = (rhs[...].astype(F32) - coupled).astype(BF16)
    solved[...] = jnp.dot(inverse[...], residual, preferred_element_type=F32).astype(BF16)


def call(kernel, outs, *args):
    return pl.pallas_call(
        kernel,
        out_shape=outs,
        in_specs=[whole()] * len(args),
        out_specs=[whole()] * len(outs),
        compiler_params=params(),
    )(*args)


def gather(part, first, second):
    fwd = move(part, first, 1)
    bwd = move(part, first, -1)
    far = move(part, first, 2)
    line = jnp.concatenate([part, bwd, far, fwd], 0)
    from_fwd = move(line, second, 1)
    from_bwd = move(line, second, -1)
    on_fwd = move(from_fwd[:2], second, 1)
    on_bwd = move(from_bwd[2:], second, -1)
    pieces = [line, from_bwd, on_fwd, on_bwd, from_fwd]
    places = [(0, 4), (4, 4), (8, 2), (10, 2), (12, 4)]
    return pieces, places


def local(rhs_one, inv_one, rhs_two, inv_two, blocks, block_rows, block_cols):
    rows = rhs_one.shape[3]
    row = lax.axis_index("row")
    col = lax.axis_index("col")
    core = col % 2
    sign = 1 - 2 * core
    here_y, here_x, here_z = row // 4, row % 4, col // 2

    target = block_rows[0, 0]
    parity = target % 2
    steps = ((1 - 2 * parity) * (target // 2 - here_z)) % 8
    target_slot = jnp.where(parity == core, 0, 8) + steps
    source = block_cols[0, 0]
    place = source // 2
    from_y = (sign * (place // 4 - here_y)) % 4
    from_x = (sign * (place % 4 - here_x)) % 4
    source_slot = jnp.where(source % 2 == 0, from_y * 4 + from_x, 16 + from_x * 4 + from_y)

    solved_one, *parts = solve_one(rhs_one[0, 0], inv_one[0, 0], WIDTHS)
    columns = []
    start = 0
    for i, width in enumerate(WIDTHS):
        pieces, places = gather(parts[2 * i], "x", "y")
        more, more_places = gather(parts[2 * i + 1], "y", "x")
        places = places + [(16 + s, n) for s, n in more_places]
        keep, send = couple(source_slot, target_slot, blocks[0, 0], pieces + more, places)
        other = swap_cores(send)
        half = shape((rows // 2, width))
        near = shape((2, rows, width))
        near_fwd, near_bwd, far_fwd, far_bwd, kept = call(
            first_kernel, [near, near, half, half, shape((3, rows, width), F32)], keep, other
        )
        near_fwd = move(near_fwd, "z", 1)
        near_bwd = move(near_bwd, "z", -1)
        far_fwd = move(far_fwd, "z", 2)
        far_bwd = move(far_bwd, "z", -2)
        one = shape((rows, width))
        out_fwd, out_bwd, own = call(
            second_kernel, [one, one, shape((rows, width), F32)], kept, near_fwd, near_bwd, far_fwd, far_bwd
        )
        out_fwd = move(out_fwd, "z", 2)
        out_bwd = move(out_bwd, "z", -2)
        (column,) = call(
            last_kernel, [one], own, out_fwd, out_bwd, rhs_two[0, 0, 0, :, start : start + width], inv_two[0, 0, 0]
        )
        columns.append(column)
        start += width
    solved_two = columns[0] if len(columns) == 1 else jnp.concatenate(columns, 1)
    return (solved_one[None, None], solved_two[None, None, None])


def solution(mesh):
    in_specs = (
        P("row", "col", None, None, None),
        P("row", "col", None, None, None),
        P("row", "col", None, None, None),
        P("row", "col", None, None, None),
        P("row", "col", None, None, None),
        P("row", "col", None),
        P("row", "col", None),
    )
    out_specs = (P("row", "col", None, None, None), P("row", "col", None, None, None))
    return jax.shard_map(local, mesh=mesh, in_specs=in_specs, out_specs=out_specs, check_vma=False)
```

time: 304 us -> 134 us (0.44)
  matrix products: 82.8 us -> 0 us
  waiting for transfers between devices: 145 us -> 69.3 us
  local copies, waits for them, and re-layouts: 57 us -> 5.61 us
  starting transfers between devices: 0.08 us -> 35 us
  Pallas kernels: 0 us -> 22 us
  between operations: 14.1 us -> 0.86 us
    dot_general x17 -> x0, matrix products: 82.8 us -> none  [the longest x5 41.8 us: accumulate(): jnp.dot(selector, product.reshape(GROUP, block_width * rhs_count), precis...]
    all_gather x1 -> x0, waiting for transfers between devices: 77 us -> none  [local(): column = lax.all_gather(solved_one, 'row', axis=0, tiled=True)]
    ppermute x0 -> x21, waiting for transfers between devices: none -> 69.3 us  [the longest x20 65.3 us: move(): return lax.ppermute(value, BOTH, ring_pairs(axis, steps))]
    reduce_scatter x1 -> x0, waiting for transfers between devices: 67.5 us -> none  [local(): lax.psum_scatter(partial_sums, 'col', scatter_dimension=0, tiled=True)]
    ppermute x0 -> x21, starting transfers between devices: none -> 35 us  [the longest x20 33.5 us: move(): return lax.ppermute(value, BOTH, ring_pairs(axis, steps))]
    while x10 -> x0, local copies, waits for them, and re-layouts: 31.5 us -> none
    unnamed x12 -> x24, local copies, waits for them, and re-layouts: 25.3 us -> 2.13 us
    pallas_call x0 -> x5, Pallas kernels: none -> 22 us  [the longest x1 17.2 us: couple(): pl.pallas_call(functools.partial(couple_kernel, places), out_shape=[shape...]
  transfers between devices with their start and end apart: 2 -> 21, of which waited for: 2 -> 9; matrix products, arithmetic and copies ran while one was open for 1% -> 3% of each run, Pallas kernels for 0% -> 0%
where the time goes in v1:
time: 134 us; the launch traced here: 133 us
  waiting for transfers between devices  69.3 us (52%)
  starting transfers between devices  35 us (26%)
  Pallas kernels  22 us (16%)
  local copies, waits for them, and re-layouts  5.61 us (4%)
    ppermute x20, waiting for transfers between devices, move(): return lax.ppermute(value, BOTH, ring_pairs(axis, steps))  65.3 us
    ppermute x20, starting transfers between devices, move(): return lax.ppermute(value, BOTH, ring_pairs(axis, steps))  33.5 us
    pallas_call x1, Pallas kernels, couple(): pl.pallas_call(functools.partial(couple_kernel, places), out_shape=[shape...  17.2 us
    ppermute x1, waiting for transfers between devices, swap_cores(): return lax.ppermute(value, 'col', [(i, i ^ 1) for i in range(16)])  4 us
    pallas_call x3, Pallas kernels, call(): pl.pallas_call(kernel, out_shape=outs, in_specs=[whole()] * len(args), ou...  3.73 us
  transfers between devices with their start and end apart: 21, of which 9 were waited for; matrix products, arithmetic and copies ran while one was open for 3% of the time, Pallas kernels for 0%

profile of v1, /device:TPU:1, one launch (start us, length us, event | category | flops | bytes accessed | tf_op | source)
XLA Modules:
  0.0 132.9 jit_solution(1949171098067960430)
XLA Ops:
  0.6 0.0 copy-start
  0.6 1.0 copy-done
  1.7 0.9 copy-done.1
  2.6 1.1 shard_map.86
  3.7 2.1 %collective-permute-start.7 = (bf16[1,256,512]{2,1,0:T(8,128)(2,1)S(1)}, bf16[1,256,512]{2,1,0:T(8,128)(2,1)S(1)}, u32[]{:S(2)}, u32[]{:S(2)}) collective-permute-start(bf16[1,256,512]{2,1,0:T(8,128)(2,1)S(1)} %get-tuple-element.17), channel_id=1, source_target_pairs={{0,192},{1,65},{2,194},{3,67},{4,196},{5,69},{6,198},{7,71},{8,200... | collective-permute-start | bytes 786440 | tf_op jit(solution)/shard_map/ppermute | solution.py:49
  5.8 2.5 %collective-permute-start.2 = (bf16[1,256,512]{2,1,0:T(8,128)(2,1)S(1)}, bf16[1,256,512]{2,1,0:T(8,128)(2,1)S(1)}, u32[]{:S(2)}, u32[]{:S(2)}) collective-permute-start(bf16[1,256,512]{2,1,0:T(8,128)(2,1)S(1)} %get-tuple-element.16), channel_id=1, source_target_pairs={{0,16},{1,49},{2,18},{3,51},{4,20},{5,53},{6,22},{7,55},{8,24},{9,... | collective-permute-start | bytes 786440 | tf_op jit(solution)/shard_map/ppermute | solution.py:49
  8.3 0.5 collective-permute-start.1
  8.8 1.4 %collective-permute-start.9 = (bf16[1,256,512]{2,1,0:T(8,128)(2,1)S(1)}, bf16[1,256,512]{2,1,0:T(8,128)(2,1)S(1)}, u32[]{:S(2)}, u32[]{:S(2)}) collective-permute-start(bf16[1,256,512]{2,1,0:T(8,128)(2,1)S(1)} %get-tuple-element.17), channel_id=1, source_target_pairs={{0,64},{1,193},{2,66},{3,195},{4,68},{5,197},{6,70},{7,199},{8,72}... | collective-permute-start | bytes 786440 | tf_op jit(solution)/shard_map/ppermute | solution.py:49
  10.3 1.6 %collective-permute-start.8 = (bf16[1,256,512]{2,1,0:T(8,128)(2,1)S(1)}, bf16[1,256,512]{2,1,0:T(8,128)(2,1)S(1)}, u32[]{:S(2)}, u32[]{:S(2)}) collective-permute-start(bf16[1,256,512]{2,1,0:T(8,128)(2,1)S(1)} %get-tuple-element.17), channel_id=1, source_target_pairs={{0,128},{1,129},{2,130},{3,131},{4,132},{5,133},{6,134},{7,135},{8... | collective-permute-start | bytes 786440 | tf_op jit(solution)/shard_map/ppermute | solution.py:49
  12.0 0.0 collective-permute-done.7
  12.0 0.7 collective-permute-start
  12.7 5.8 %collective-permute-done.8 = bf16[1,256,512]{2,1,0:T(8,128)(2,1)S(1)} collective-permute-done((bf16[1,256,512]{2,1,0:T(8,128)(2,1)S(1)}, bf16[1,256,512]{2,1,0:T(8,128)(2,1)S(1)}, u32[]{:S(2)}, u32[]{:S(2)}) %collective-permute-start.8) | collective-permute-done | bytes 262176 | tf_op jit(solution)/shard_map/ppermute | solution.py:49
  18.5 0.0 collective-permute-done.9
  18.5 0.0 copy-start.6
  18.5 4.2 %collective-permute-start.11 = (bf16[4,256,512]{2,1,0:T(8,128)(2,1)S(1)}, bf16[4,256,512]{2,1,0:T(8,128)(2,1)S(1)}, u32[]{:S(2)}, u32[]{:S(2)}) collective-permute-start(bf16[4,256,512]{2,1,0:T(8,128)(2,1)S(1)} %constant_dynamic-update-slice_fusion.4.refs_5_), channel_id=1, source_target_pairs={{0,16},{1,49},{2,18},{3,51},{4,20},{5,53},{6,22},{7,55},{8,24},{9,... | collective-permute-start | bytes 3145736 | tf_op jit(solution)/shard_map/ppermute | solution.py:49
  22.7 0.0 collective-permute-start.10
  22.8 0.0 collective-permute-done
  22.8 0.0 collective-permute-done.1
  22.8 0.0 collective-permute-done.2
  22.9 0.0 copy-start.7
  22.9 0.0 copy-start.8
  22.9 3.2 %collective-permute-start.4 = (bf16[4,256,512]{2,1,0:T(8,128)(2,1)S(1)}, bf16[4,256,512]{2,1,0:T(8,128)(2,1)S(1)}, u32[]{:S(2)}, u32[]{:S(2)}) collective-permute-start(bf16[4,256,512]{2,1,0:T(8,128)(2,1)S(1)} %constant_dynamic-update-slice_fusion.refs_0_), channel_id=1, source_target_pairs={{0,64},{1,193},{2,66},{3,195},{4,68},{5,197},{6,70},{7,199},{8,72}... | collective-permute-start | bytes 3145736 | tf_op jit(solution)/shard_map/ppermute | solution.py:49
  26.1 0.0 collective-permute-start.3
  26.1 19.4 %collective-permute-done.11.refs_9_ = bf16[4,256,512]{2,1,0:T(8,128)(2,1)S(1)} collective-permute-done((bf16[4,256,512]{2,1,0:T(8,128)(2,1)S(1)}, bf16[4,256,512]{2,1,0:T(8,128)(2,1)S(1)}, u32[]{:S(2)}, u32[]{:S(2)}) %collective-permute-start.11) | collective-permute-done | bytes 1048608 | tf_op jit(solution)/shard_map/ppermute | solution.py:49
  45.5 0.9 slice.18
  46.4 3.4 %collective-permute-start.12 = (bf16[2,256,512]{2,1,0:T(8,128)(2,1)}, bf16[2,256,512]{2,1,0:T(8,128)(2,1)}, u32[]{:S(2)}, u32[]{:S(2)}) collective-permute-start(bf16[2,256,512]{2,1,0:T(8,128)(2,1)} %slice.18), channel_id=1, source_target_pairs={{0,16},{1,49},{2,18},{3,51},{4,20},{5,53},{6,22},{7,55},{8,24},{9,... | collective-permute-start | bytes 1572872 | tf_op jit(solution)/shard_map/ppermute | solution.py:49
  49.8 0.0 collective-permute-done.10.refs_6_
  49.8 0.9 slice.19
  50.7 0.0 collective-permute-start.13
  50.7 0.0 collective-permute-done.4.refs_4_
  50.7 0.8 slice.16
  51.5 0.0 copy-done.6
  51.5 2.7 %collective-permute-start.5 = (bf16[2,256,512]{2,1,0:T(8,128)(2,1)}, bf16[2,256,512]{2,1,0:T(8,128)(2,1)}, u32[]{:S(2)}, u32[]{:S(2)}) collective-permute-start(bf16[2,256,512]{2,1,0:T(8,128)(2,1)} %slice.16), channel_id=1, source_target_pairs={{0,64},{1,193},{2,66},{3,195},{4,68},{5,197},{6,70},{7,199},{8,72}... | collective-permute-start | bytes 1572872 | tf_op jit(solution)/shard_map/ppermute | solution.py:49
  54.2 0.0 collective-permute-done.3.refs_1_
  54.2 0.8 slice.17
  55.1 0.0 copy-done.4
  55.1 0.0 collective-permute-start.6
  55.1 0.0 copy-done.7
  55.1 0.0 copy-done.8
  55.2 1.6 %collective-permute-done.12.refs_7_ = bf16[2,256,512]{2,1,0:T(8,128)(2,1)} collective-permute-done((bf16[2,256,512]{2,1,0:T(8,128)(2,1)}, bf16[2,256,512]{2,1,0:T(8,128)(2,1)}, u32[]{:S(2)}, u32[]{:S(2)}) %collective-permute-start.12) | collective-permute-done | bytes 524320 | tf_op jit(solution)/shard_map/ppermute | solution.py:49
  56.8 9.1 %collective-permute-done.13.refs_8_ = bf16[2,256,512]{2,1,0:T(8,128)(2,1)} collective-permute-done((bf16[2,256,512]{2,1,0:T(8,128)(2,1)}, bf16[2,256,512]{2,1,0:T(8,128)(2,1)}, u32[]{:S(2)}, u32[]{:S(2)}) %collective-permute-start.13) | collective-permute-done | bytes 524320 | tf_op jit(solution)/shard_map/ppermute | solution.py:49
  65.9 0.0 collective-permute-done.5.refs_2_
  65.9 3.6 %collective-permute-done.6.refs_3_ = bf16[2,256,512]{2,1,0:T(8,128)(2,1)} collective-permute-done((bf16[2,256,512]{2,1,0:T(8,128)(2,1)}, bf16[2,256,512]{2,1,0:T(8,128)(2,1)}, u32[]{:S(2)}, u32[]{:S(2)}) %collective-permute-start.6) | collective-permute-done | bytes 524320 | tf_op jit(solution)/shard_map/ppermute | solution.py:49
  69.5 17.2 %shard_map.87 = (f32[8,256,512]{2,1,0:T(8,128)}, bf16[8,256,512]{2,1,0:T(8,128)(2,1)}) custom-call(s32[80]{0:T(128)S(1)} %get-tuple-element.28.source_slot, s32[80]{0:T(128)S(1)} %get-tuple-element.29.target_slot, bf16[80,256,256]{2,1,0:T(8,128)(2,1)} %bitcast.38, bf16[4,256,512]{2,1,0:T(8,128)(2,1)S(1)} %constant_dynamic-update-slice_fusion.refs_0_, ...), custom_call_target="tpu_custom_call" | custom-call | flops 5368709120 | bytes 10485760 | tf_op jit(solution)/shard_map/pallas_call | solution.py:109
  86.7 1.5 %collective-permute-start.14 = (bf16[8,256,512]{2,1,0:T(8,128)(2,1)}, bf16[8,256,512]{2,1,0:T(8,128)(2,1)S(1)}, u32[]{:S(2)}, u32[]{:S(2)}) collective-permute-start(bf16[8,256,512]{2,1,0:T(8,128)(2,1)} %get-tuple-element.19), channel_id=1, source_target_pairs={{0,1},{1,0},{2,3},{3,2},{4,5},{5,4},{6,7},{7,6},{8,9},{9,8},{10,11... | collective-permute-start | bytes 6291464 | tf_op jit(solution)/shard_map/ppermute | solution.py:53
  88.2 4.0 %collective-permute-done.14.other = bf16[8,256,512]{2,1,0:T(8,128)(2,1)S(1)} collective-permute-done((bf16[8,256,512]{2,1,0:T(8,128)(2,1)}, bf16[8,256,512]{2,1,0:T(8,128)(2,1)S(1)}, u32[]{:S(2)}, u32[]{:S(2)}) %collective-permute-start.14) | collective-permute-done | bytes 2097184 | tf_op jit(solution)/shard_map/ppermute | solution.py:53
  92.2 2.5 %shard_map.88 = (bf16[2,256,512]{2,1,0:T(8,128)(2,1)S(1)}, bf16[2,256,512]{2,1,0:T(8,128)(2,1)S(1)}, bf16[128,512]{1,0:T(8,128)(2,1)S(1)}, bf16[128,512]{1,0:T(8,128)(2,1)S(1)}, f32[3,256,512]{2,1,0:T(8,128)S(1)}) custom-call(f32[8,256,512]{2,1,0:T(8,128)} %get-tuple-element.18.keep, bf16[8,256,512]{2,1,0:T(8,128)(2,1)S(1)} %collective-permute-done.14.other), custom_call_target="tpu_custom_call" | custom-call | tf_op jit(solution)/shard_map/pallas_call | solution.py:165
  94.8 0.0 copy-start.2
  94.8 0.0 copy-start.3
  94.8 5.6 %collective-permute-start.15 = (bf16[2,256,512]{2,1,0:T(8,128)(2,1)S(1)}, bf16[2,256,512]{2,1,0:T(8,128)(2,1)S(1)}, u32[]{:S(2)}, u32[]{:S(2)}) collective-permute-start(bf16[2,256,512]{2,1,0:T(8,128)(2,1)S(1)} %get-tuple-element.21), channel_id=1, source_target_pairs={{0,2},{1,15},{2,4},{3,1},{4,6},{5,3},{6,8},{7,5},{8,10},{9,7},{10,... | collective-permute-start | bytes 1572872 | tf_op jit(solution)/shard_map/ppermute | solution.py:49
  100.4 0.0 collective-permute-start.16
  100.4 1.9 %collective-permute-start.17 = (bf16[128,512]{1,0:T(8,128)(2,1)S(1)}, bf16[128,512]{1,0:T(8,128)(2,1)S(1)}, u32[]{:S(2)}, u32[]{:S(2)}) collective-permute-start(bf16[128,512]{1,0:T(8,128)(2,1)S(1)} %get-tuple-element.23), channel_id=1, source_target_pairs={{0,4},{1,13},{2,6},{3,15},{4,8},{5,1},{6,10},{7,3},{8,12},{9,5},{1... | collective-permute-start | bytes 393224 | tf_op jit(solution)/shard_map/ppermute | solution.py:49
  102.3 0.5 collective-permute-start.18
  102.8 14.1 %collective-permute-done.17.far_fwd = bf16[128,512]{1,0:T(8,128)(2,1)S(1)} collective-permute-done((bf16[128,512]{1,0:T(8,128)(2,1)S(1)}, bf16[128,512]{1,0:T(8,128)(2,1)S(1)}, u32[]{:S(2)}, u32[]{:S(2)}) %collective-permute-start.17) | collective-permute-done | bytes 131104 | tf_op jit(solution)/shard_map/ppermute | solution.py:49
  116.9 1.3 %collective-permute-done.18.far_bwd = bf16[128,512]{1,0:T(8,128)(2,1)S(1)} collective-permute-done((bf16[128,512]{1,0:T(8,128)(2,1)S(1)}, bf16[128,512]{1,0:T(8,128)(2,1)S(1)}, u32[]{:S(2)}, u32[]{:S(2)}) %collective-permute-start.18) | collective-permute-done | bytes 131104 | tf_op jit(solution)/shard_map/ppermute | solution.py:49
  118.2 0.0 collective-permute-done.15.fwd
  118.2 0.0 collective-permute-done.16.bwd
  118.2 0.2 shard_map.89
  118.4 3.1 %collective-permute-start.19 = (bf16[256,512]{1,0:T(8,128)(2,1)S(1)}, bf16[256,512]{1,0:T(8,128)(2,1)S(1)}, u32[]{:S(2)}, u32[]{:S(2)}) collective-permute-start(bf16[256,512]{1,0:T(8,128)(2,1)S(1)} %get-tuple-element.26), channel_id=1, source_target_pairs={{0,4},{1,13},{2,6},{3,15},{4,8},{5,1},{6,10},{7,3},{8,12},{9,5},{1... | collective-permute-start | bytes 786440 | tf_op jit(solution)/shard_map/ppermute | solution.py:49
  121.5 0.0 collective-permute-start.20
  121.5 10.3 %collective-permute-done.19.fwd = bf16[256,512]{1,0:T(8,128)(2,1)S(1)} collective-permute-done((bf16[256,512]{1,0:T(8,128)(2,1)S(1)}, bf16[256,512]{1,0:T(8,128)(2,1)S(1)}, u32[]{:S(2)}, u32[]{:S(2)}) %collective-permute-start.19) | collective-permute-done | bytes 262176 | tf_op jit(solution)/shard_map/ppermute | solution.py:49
  131.8 0.0 collective-permute-done.20.bwd
  131.8 0.0 copy-done.3
  131.8 1.0 shard_map.90
  (14 shorter events, 0.2 us)
Async XLA Ops:
  0.6 1.0 copy-start
  1.7 0.9 copy-start.1
  3.7 8.3 %collective-permute-start.7 = (bf16[1,256,512]{2,1,0:T(8,128)(2,1)S(1)}, bf16[1,256,512]{2,1,0:T(8,128)(2,1)S(1)}, u32[]{:S(2)}, u32[]{:S(2)}) collective-permute-start(bf16[1,256,512]{2,1,0:T(8,128)(2,1)S(1)} %get-tuple-element.17), channel_id=1, source_target_pairs={{0,192},{1,65},{2,194},{3,67},{4,196},{5,69},{6,198},{7,71},{8,200... | collective-permute-start | bytes 786440 | tf_op jit(solution)/shard_map/ppermute | solution.py:49
  5.8 17.0 %collective-permute-start.2 = (bf16[1,256,512]{2,1,0:T(8,128)(2,1)S(1)}, bf16[1,256,512]{2,1,0:T(8,128)(2,1)S(1)}, u32[]{:S(2)}, u32[]{:S(2)}) collective-permute-start(bf16[1,256,512]{2,1,0:T(8,128)(2,1)S(1)} %get-tuple-element.16), channel_id=1, source_target_pairs={{0,16},{1,49},{2,18},{3,51},{4,20},{5,53},{6,22},{7,55},{8,24},{9,... | collective-permute-start | bytes 786440 | tf_op jit(solution)/shard_map/ppermute | solution.py:49
  8.3 14.5 %collective-permute-start.1 = (bf16[1,256,512]{2,1,0:T(8,128)(2,1)S(1)}, bf16[1,256,512]{2,1,0:T(8,128)(2,1)S(1)}, u32[]{:S(2)}, u32[]{:S(2)}) collective-permute-start(bf16[1,256,512]{2,1,0:T(8,128)(2,1)S(1)} %get-tuple-element.16), channel_id=1, source_target_pairs={{0,32},{1,33},{2,34},{3,35},{4,36},{5,37},{6,38},{7,39},{8,40},{9,... | collective-permute-start | bytes 786440 | tf_op jit(solution)/shard_map/ppermute | solution.py:49
  8.8 9.6 %collective-permute-start.9 = (bf16[1,256,512]{2,1,0:T(8,128)(2,1)S(1)}, bf16[1,256,512]{2,1,0:T(8,128)(2,1)S(1)}, u32[]{:S(2)}, u32[]{:S(2)}) collective-permute-start(bf16[1,256,512]{2,1,0:T(8,128)(2,1)S(1)} %get-tuple-element.17), channel_id=1, source_target_pairs={{0,64},{1,193},{2,66},{3,195},{4,68},{5,197},{6,70},{7,199},{8,72}... | collective-permute-start | bytes 786440 | tf_op jit(solution)/shard_map/ppermute | solution.py:49
  10.3 8.2 %collective-permute-start.8 = (bf16[1,256,512]{2,1,0:T(8,128)(2,1)S(1)}, bf16[1,256,512]{2,1,0:T(8,128)(2,1)S(1)}, u32[]{:S(2)}, u32[]{:S(2)}) collective-permute-start(bf16[1,256,512]{2,1,0:T(8,128)(2,1)S(1)} %get-tuple-element.17), channel_id=1, source_target_pairs={{0,128},{1,129},{2,130},{3,131},{4,132},{5,133},{6,134},{7,135},{8... | collective-permute-start | bytes 786440 | tf_op jit(solution)/shard_map/ppermute | solution.py:49
  12.0 10.8 %collective-permute-start = (bf16[1,256,512]{2,1,0:T(8,128)(2,1)S(1)}, bf16[1,256,512]{2,1,0:T(8,128)(2,1)S(1)}, u32[]{:S(2)}, u32[]{:S(2)}) collective-permute-start(bf16[1,256,512]{2,1,0:T(8,128)(2,1)S(1)} %get-tuple-element.16), channel_id=1, source_target_pairs={{0,48},{1,17},{2,50},{3,19},{4,52},{5,21},{6,54},{7,23},{8,56},{9,... | collective-permute-start | bytes 786440 | tf_op jit(solution)/shard_map/ppermute | solution.py:49
  18.5 33.0 %copy-start.6 = (bf16[4,256,512]{2,1,0:T(8,128)(2,1)}, bf16[4,256,512]{2,1,0:T(8,128)(2,1)S(1)}, u32[]{:S(2)}) copy-start(bf16[4,256,512]{2,1,0:T(8,128)(2,1)S(1)} %constant_dynamic-update-slice_fusion.4.refs_5_) | copy-start | bytes 3145732
  18.5 26.9 %collective-permute-start.11 = (bf16[4,256,512]{2,1,0:T(8,128)(2,1)S(1)}, bf16[4,256,512]{2,1,0:T(8,128)(2,1)S(1)}, u32[]{:S(2)}, u32[]{:S(2)}) collective-permute-start(bf16[4,256,512]{2,1,0:T(8,128)(2,1)S(1)} %constant_dynamic-update-slice_fusion.4.refs_5_), channel_id=1, source_target_pairs={{0,16},{1,49},{2,18},{3,51},{4,20},{5,53},{6,22},{7,55},{8,24},{9,... | collective-permute-start | bytes 3145736 | tf_op jit(solution)/shard_map/ppermute | solution.py:49
  22.7 27.0 %collective-permute-start.10 = (bf16[4,256,512]{2,1,0:T(8,128)(2,1)S(1)}, bf16[4,256,512]{2,1,0:T(8,128)(2,1)S(1)}, u32[]{:S(2)}, u32[]{:S(2)}) collective-permute-start(bf16[4,256,512]{2,1,0:T(8,128)(2,1)S(1)} %constant_dynamic-update-slice_fusion.4.refs_5_), channel_id=1, source_target_pairs={{0,48},{1,17},{2,50},{3,19},{4,52},{5,21},{6,54},{7,23},{8,56},{9,... | collective-permute-start | bytes 3145736 | tf_op jit(solution)/shard_map/ppermute | solution.py:49
  22.9 32.3 %copy-start.7 = (s32[1,1,80]{2,1,0:T(1,128)S(1)}, s32[1,1,80]{2,1,0:T(1,128)}, u32[]{:S(2)}) copy-start(s32[1,1,80]{2,1,0:T(1,128)} %param.13) | copy-start | bytes 964
  22.9 32.2 %copy-start.8 = (s32[1,1,80]{2,1,0:T(1,128)S(1)}, s32[1,1,80]{2,1,0:T(1,128)}, u32[]{:S(2)}) copy-start(s32[1,1,80]{2,1,0:T(1,128)} %param.12) | copy-start | bytes 964
  22.9 27.8 %collective-permute-start.4 = (bf16[4,256,512]{2,1,0:T(8,128)(2,1)S(1)}, bf16[4,256,512]{2,1,0:T(8,128)(2,1)S(1)}, u32[]{:S(2)}, u32[]{:S(2)}) collective-permute-start(bf16[4,256,512]{2,1,0:T(8,128)(2,1)S(1)} %constant_dynamic-update-slice_fusion.refs_0_), channel_id=1, source_target_pairs={{0,64},{1,193},{2,66},{3,195},{4,68},{5,197},{6,70},{7,199},{8,72}... | collective-permute-start | bytes 3145736 | tf_op jit(solution)/shard_map/ppermute | solution.py:49
  26.1 28.1 %collective-permute-start.3 = (bf16[4,256,512]{2,1,0:T(8,128)(2,1)S(1)}, bf16[4,256,512]{2,1,0:T(8,128)(2,1)S(1)}, u32[]{:S(2)}, u32[]{:S(2)}) collective-permute-start(bf16[4,256,512]{2,1,0:T(8,128)(2,1)S(1)} %constant_dynamic-update-slice_fusion.refs_0_), channel_id=1, source_target_pairs={{0,192},{1,65},{2,194},{3,67},{4,196},{5,69},{6,198},{7,71},{8,200... | collective-permute-start | bytes 3145736 | tf_op jit(solution)/shard_map/ppermute | solution.py:49
  45.5 9.6 %copy-start.4 = (bf16[4,256,512]{2,1,0:T(8,128)(2,1)}, bf16[4,256,512]{2,1,0:T(8,128)(2,1)S(1)}, u32[]{:S(2)}) copy-start(bf16[4,256,512]{2,1,0:T(8,128)(2,1)S(1)} %collective-permute-done.11.refs_9_) | copy-start | bytes 3145732
  46.4 10.4 %collective-permute-start.12 = (bf16[2,256,512]{2,1,0:T(8,128)(2,1)}, bf16[2,256,512]{2,1,0:T(8,128)(2,1)}, u32[]{:S(2)}, u32[]{:S(2)}) collective-permute-start(bf16[2,256,512]{2,1,0:T(8,128)(2,1)} %slice.18), channel_id=1, source_target_pairs={{0,16},{1,49},{2,18},{3,51},{4,20},{5,53},{6,22},{7,55},{8,24},{9,... | collective-permute-start | bytes 1572872 | tf_op jit(solution)/shard_map/ppermute | solution.py:49
  49.8 5.3 %copy-start.5 = (bf16[4,256,512]{2,1,0:T(8,128)(2,1)}, bf16[4,256,512]{2,1,0:T(8,128)(2,1)S(1)}, u32[]{:S(2)}) copy-start(bf16[4,256,512]{2,1,0:T(8,128)(2,1)S(1)} %collective-permute-done.10.refs_6_) | copy-start | bytes 3145732
  50.7 15.3 %collective-permute-start.13 = (bf16[2,256,512]{2,1,0:T(8,128)(2,1)}, bf16[2,256,512]{2,1,0:T(8,128)(2,1)}, u32[]{:S(2)}, u32[]{:S(2)}) collective-permute-start(bf16[2,256,512]{2,1,0:T(8,128)(2,1)} %slice.19), channel_id=1, source_target_pairs={{0,48},{1,17},{2,50},{3,19},{4,52},{5,21},{6,54},{7,23},{8,56},{9,... | collective-permute-start | bytes 1572872 | tf_op jit(solution)/shard_map/ppermute | solution.py:49
  51.5 14.4 %collective-permute-start.5 = (bf16[2,256,512]{2,1,0:T(8,128)(2,1)}, bf16[2,256,512]{2,1,0:T(8,128)(2,1)}, u32[]{:S(2)}, u32[]{:S(2)}) collective-permute-start(bf16[2,256,512]{2,1,0:T(8,128)(2,1)} %slice.16), channel_id=1, source_target_pairs={{0,64},{1,193},{2,66},{3,195},{4,68},{5,197},{6,70},{7,199},{8,72}... | collective-permute-start | bytes 1572872 | tf_op jit(solution)/shard_map/ppermute | solution.py:49
  55.1 14.5 %collective-permute-start.6 = (bf16[2,256,512]{2,1,0:T(8,128)(2,1)}, bf16[2,256,512]{2,1,0:T(8,128)(2,1)}, u32[]{:S(2)}, u32[]{:S(2)}) collective-permute-start(bf16[2,256,512]{2,1,0:T(8,128)(2,1)} %slice.17), channel_id=1, source_target_pairs={{0,192},{1,65},{2,194},{3,67},{4,196},{5,69},{6,198},{7,71},{8,200... | collective-permute-start | bytes 1572872 | tf_op jit(solution)/shard_map/ppermute | solution.py:49
  86.7 5.5 %collective-permute-start.14 = (bf16[8,256,512]{2,1,0:T(8,128)(2,1)}, bf16[8,256,512]{2,1,0:T(8,128)(2,1)S(1)}, u32[]{:S(2)}, u32[]{:S(2)}) collective-permute-start(bf16[8,256,512]{2,1,0:T(8,128)(2,1)} %get-tuple-element.19), channel_id=1, source_target_pairs={{0,1},{1,0},{2,3},{3,2},{4,5},{5,4},{6,7},{7,6},{8,9},{9,8},{10,11... | collective-permute-start | bytes 6291464 | tf_op jit(solution)/shard_map/ppermute | solution.py:53
  94.8 37.1 %copy-start.2 = (bf16[1,1,1,256,512]{4,3,2,1,0:T(8,128)(2,1)S(1)}, bf16[1,1,1,256,512]{4,3,2,1,0:T(8,128)(2,1)}, u32[]{:S(2)}) copy-start(bf16[1,1,1,256,512]{4,3,2,1,0:T(8,128)(2,1)} %param.9) | copy-start | bytes 786436
  94.8 37.1 %copy-start.3 = (bf16[1,1,1,256,256]{4,3,2,1,0:T(8,128)(2,1)S(1)}, bf16[1,1,1,256,256]{4,3,2,1,0:T(8,128)(2,1)}, u32[]{:S(2)}) copy-start(bf16[1,1,1,256,256]{4,3,2,1,0:T(8,128)(2,1)} %param.10) | copy-start | bytes 393220
  94.8 23.4 %collective-permute-start.15 = (bf16[2,256,512]{2,1,0:T(8,128)(2,1)S(1)}, bf16[2,256,512]{2,1,0:T(8,128)(2,1)S(1)}, u32[]{:S(2)}, u32[]{:S(2)}) collective-permute-start(bf16[2,256,512]{2,1,0:T(8,128)(2,1)S(1)} %get-tuple-element.21), channel_id=1, source_target_pairs={{0,2},{1,15},{2,4},{3,1},{4,6},{5,3},{6,8},{7,5},{8,10},{9,7},{10,... | collective-permute-start | bytes 1572872 | tf_op jit(solution)/shard_map/ppermute | solution.py:49
  100.4 17.8 %collective-permute-start.16 = (bf16[2,256,512]{2,1,0:T(8,128)(2,1)S(1)}, bf16[2,256,512]{2,1,0:T(8,128)(2,1)S(1)}, u32[]{:S(2)}, u32[]{:S(2)}) collective-permute-start(bf16[2,256,512]{2,1,0:T(8,128)(2,1)S(1)} %get-tuple-element.22), channel_id=1, source_target_pairs={{0,14},{1,3},{2,0},{3,5},{4,2},{5,7},{6,4},{7,9},{8,6},{9,11},{10,... | collective-permute-start | bytes 1572872 | tf_op jit(solution)/shard_map/ppermute | solution.py:49
  100.4 16.4 %collective-permute-start.17 = (bf16[128,512]{1,0:T(8,128)(2,1)S(1)}, bf16[128,512]{1,0:T(8,128)(2,1)S(1)}, u32[]{:S(2)}, u32[]{:S(2)}) collective-permute-start(bf16[128,512]{1,0:T(8,128)(2,1)S(1)} %get-tuple-element.23), channel_id=1, source_target_pairs={{0,4},{1,13},{2,6},{3,15},{4,8},{5,1},{6,10},{7,3},{8,12},{9,5},{1... | collective-permute-start | bytes 393224 | tf_op jit(solution)/shard_map/ppermute | solution.py:49
  102.3 15.9 %collective-permute-start.18 = (bf16[128,512]{1,0:T(8,128)(2,1)S(1)}, bf16[128,512]{1,0:T(8,128)(2,1)S(1)}, u32[]{:S(2)}, u32[]{:S(2)}) collective-permute-start(bf16[128,512]{1,0:T(8,128)(2,1)S(1)} %get-tuple-element.24), channel_id=1, source_target_pairs={{0,12},{1,5},{2,14},{3,7},{4,0},{5,9},{6,2},{7,11},{8,4},{9,13},{1... | collective-permute-start | bytes 393224 | tf_op jit(solution)/shard_map/ppermute | solution.py:49
  118.4 13.4 %collective-permute-start.19 = (bf16[256,512]{1,0:T(8,128)(2,1)S(1)}, bf16[256,512]{1,0:T(8,128)(2,1)S(1)}, u32[]{:S(2)}, u32[]{:S(2)}) collective-permute-start(bf16[256,512]{1,0:T(8,128)(2,1)S(1)} %get-tuple-element.26), channel_id=1, source_target_pairs={{0,4},{1,13},{2,6},{3,15},{4,8},{5,1},{6,10},{7,3},{8,12},{9,5},{1... | collective-permute-start | bytes 786440 | tf_op jit(solution)/shard_map/ppermute | solution.py:49
  121.5 10.4 %collective-permute-start.20 = (bf16[256,512]{1,0:T(8,128)(2,1)S(1)}, bf16[256,512]{1,0:T(8,128)(2,1)S(1)}, u32[]{:S(2)}, u32[]{:S(2)}) collective-permute-start(bf16[256,512]{1,0:T(8,128)(2,1)S(1)} %get-tuple-element.27), channel_id=1, source_target_pairs={{0,12},{1,5},{2,14},{3,7},{4,0},{5,9},{6,2},{7,11},{8,4},{9,13},{1... | collective-permute-start | bytes 786440 | tf_op jit(solution)/shard_map/ppermute | solution.py:49

commit v2 on v0

v2 whole, which is shorter than its diff:
```python
import functools

import jax
import jax.numpy as jnp
from jax import lax
from jax.experimental import pallas as pl
from jax.experimental.pallas import tpu as pltpu
from jax.sharding import PartitionSpec as P

PARTS = 1
STEP = 8
BOTH = ("row", "col")
MIB = 1024 * 1024
F32 = jnp.float32
BF16 = jnp.bfloat16


def whole(memory=pltpu.VMEM):
    return pl.BlockSpec(memory_space=memory)


def shape(dims, dtype=BF16):
    return jax.ShapeDtypeStruct(dims, dtype)


def params(mib=16):
    return pltpu.CompilerParams(vmem_limit_bytes=mib * MIB)


def ring_pairs(axis, steps):
    pairs = []
    for y in range(4):
        for x in range(4):
            for z in range(8):
                for core in range(2):
                    way = steps if core == 0 else -steps
                    to_y, to_x, to_z = y, x, z
                    if axis == "x":
                        to_x = (x + way) % 4
                    elif axis == "y":
                        to_y = (y + way) % 4
                    else:
                        to_z = (z + way) % 8
                    pairs.append(((y * 4 + x) * 16 + z * 2 + core, (to_y * 4 + to_x) * 16 + to_z * 2 + core))
    return pairs


def move(value, axis, steps):
    return lax.ppermute(value, BOTH, ring_pairs(axis, steps))


def swap_cores(value):
    return lax.ppermute(value, "col", [(i, i ^ 1) for i in range(16)])


def solve_one_kernel(rhs_hbm, inverse_hbm, solved, even, odd, rhs, inverse, sems):
    copies = []
    for q in range(2):
        copies.append(pltpu.make_async_copy(rhs_hbm.at[q], rhs.at[q], sems.at[2 * q]))
        copies.append(pltpu.make_async_copy(inverse_hbm.at[q], inverse.at[q], sems.at[2 * q + 1]))
    for copy in copies:
        copy.start()
    for q, out in enumerate((even, odd)):
        copies[2 * q].wait()
        copies[2 * q + 1].wait()
        value = jnp.dot(inverse[q], rhs[q], preferred_element_type=F32).astype(BF16)
        solved[q] = value
        width = value.shape[1] // PARTS
        for i in range(PARTS):
            out[i] = value[:, i * width : (i + 1) * width]


def solve_one(rhs, inverse):
    part = shape((PARTS, rhs.shape[1], rhs.shape[2] // PARTS))
    return pl.pallas_call(
        solve_one_kernel,
        out_shape=[shape(rhs.shape), part, part],
        in_specs=[whole(pltpu.HBM)] * 2,
        out_specs=[whole()] * 3,
        scratch_shapes=[
            pltpu.VMEM(rhs.shape, BF16),
            pltpu.VMEM(inverse.shape, BF16),
            pltpu.SemaphoreType.DMA((4,)),
        ],
        compiler_params=params(),
    )(*[pltpu.with_memory_space_constraint(value, pltpu.HBM) for value in (rhs, inverse)])


def stage_kernel(blocks_hbm, blocks, sems):
    size = blocks.shape[0] // STEP
    copies = []
    for i in range(size):
        span = pl.ds(i * STEP, STEP)
        copies.append(pltpu.make_async_copy(blocks_hbm.at[span], blocks.at[span], sems.at[i]))
        copies[-1].start()
    for copy in copies:
        copy.wait()


def stage(blocks):
    return pl.pallas_call(
        stage_kernel,
        out_shape=pltpu.VMEM(blocks.shape, blocks.dtype),
        in_specs=[whole(pl.ANY)],
        out_specs=whole(),
        scratch_shapes=[pltpu.SemaphoreType.DMA((blocks.shape[0] // STEP,))],
        compiler_params=params(4),
    )(pltpu.with_memory_space_constraint(blocks, pltpu.HBM))


def couple_kernel(slots, count, chosen, source_slot, target_slot, blocks, *refs):
    pieces = refs[:slots]
    total, send, sources, sems = refs[slots:]
    copies = []
    for i, piece in enumerate(pieces):
        copies.append(pltpu.make_async_copy(piece, sources.at[pl.ds(4 * i, 4)], sems.at[i]))
        copies[-1].start()
    total[...] = jnp.zeros_like(total)
    for copy in copies:
        copy.wait()

    def products(group, carry):
        for j in range(STEP):
            index = group * STEP + j
            product = jnp.dot(blocks[chosen[index]], sources[source_slot[index]], preferred_element_type=F32)
            total[target_slot[index]] += product
        return carry

    lax.fori_loop(0, (count[0] + STEP - 1) // STEP, products, 0)
    send[...] = total[8:16].astype(BF16)


def couple(picked, blocks, pieces):
    count, rows, _ = blocks.shape
    width = pieces[0].shape[-1]
    return pl.pallas_call(
        functools.partial(couple_kernel, len(pieces)),
        out_shape=[pltpu.VMEM((17, rows, width), F32), shape((8, rows, width))],
        in_specs=[whole(pltpu.SMEM)] * 4 + [whole()] + [whole(pl.ANY)] * len(pieces),
        out_specs=[whole()] * 2,
        scratch_shapes=[
            pltpu.VMEM((4 * len(pieces), rows, width), BF16),
            pltpu.SemaphoreType.DMA((len(pieces),)),
        ],
        compiler_params=params(16),
        cost_estimate=pl.CostEstimate(
            flops=2 * count * rows * rows * width, bytes_accessed=2 * count * rows * rows, transcendentals=0
        ),
    )(*picked, pltpu.with_memory_space_constraint(blocks, pltpu.VMEM), *pieces)


def pick(wanted, source_slot, target_slot):
    size = wanted.shape[0]
    index = jnp.arange(size, dtype=jnp.int32)
    place = jnp.cumsum(wanted.astype(jnp.int32)) - 1
    hits = wanted[None, :] & (place[None, :] == index[:, None])
    gathered = lambda values: jnp.sum(jnp.where(hits, values[None, :], 0), axis=1, dtype=jnp.int32)
    found = jnp.sum(wanted, dtype=jnp.int32)
    target = jnp.where(index < found, gathered(target_slot), 16)
    return found.reshape(1), gathered(index), gathered(source_slot), target


ORDER = (1, 3, 7, 5, 4, 2, 6, 0)
PLACES = tuple(ORDER.index(u) for u in range(8))


def merge_kernel(keep, other, base):
    base[...] = keep[:8] + other[...].astype(F32)


def first_kernel(bases, keep, other, *refs):
    base = refs[:bases]
    fwd, bwd, far, held = refs[bases:]

    def part(place):
        value = keep[place] + other[place].astype(F32)
        return value + base[0][place] if bases else value

    fwd[0] = part(0).astype(BF16)
    fwd[1] = part(1).astype(BF16)
    bwd[0] = part(2).astype(BF16)
    bwd[1] = part(3).astype(BF16)
    far[...] = part(4).astype(BF16)
    for i in range(3):
        held[i] = part(5 + i)


def second_kernel(held, fwd, bwd, far, out_fwd, out_bwd, own):
    out_fwd[...] = (held[0] + (fwd[1].astype(F32) + far[...].astype(F32))).astype(BF16)
    out_bwd[...] = (held[1] + bwd[1].astype(F32)).astype(BF16)
    own[...] = held[2] + (fwd[0].astype(F32) + bwd[0].astype(F32))


def last_kernel(own, fwd, bwd, rhs, inverse, solved):
    coupled = own[...] + (fwd[...].astype(F32) + bwd[...].astype(F32))
    residual = (rhs[...].astype(F32) - coupled).astype(BF16)
    solved[...] = jnp.dot(inverse[...], residual, preferred_element_type=F32).astype(BF16)


def call(kernel, outs, *args):
    return pl.pallas_call(
        kernel,
        out_shape=outs,
        in_specs=[whole()] * len(args),
        out_specs=[whole()] * len(outs),
        compiler_params=params(),
    )(*args)


def after(value, *others):
    return lax.optimization_barrier((value, *others))[0]


def line_of(part, axis):
    fwd = move(part, axis, 1)
    bwd = move(part, axis, -1)
    far = move(part, axis, 2)
    return [jnp.stack([part[i], bwd[i], far[i], fwd[i]]) for i in range(PARTS)]


def reduce_along_z(base, keep, other):
    _, rows, width = other.shape
    one = shape((rows, width))
    two = shape((2, rows, width))
    kernel = functools.partial(first_kernel, len(base))
    fwd, bwd, far, held = call(kernel, [two, two, one, shape((3, rows, width), F32)], keep, other, *base)
    fwd = move(fwd, "z", 1)
    bwd = move(bwd, "z", -1)
    far = move(far, "z", 2)
    sent = (fwd, bwd, far)
    out_fwd, out_bwd, own = call(second_kernel, [one, one, shape((rows, width), F32)], held, fwd, bwd, far)
    out_fwd = move(out_fwd, "z", 2)
    out_bwd = move(out_bwd, "z", -2)
    return (own, out_fwd, out_bwd), sent


def local(rhs_one, inv_one, rhs_two, inv_two, blocks, block_rows, block_cols):
    rows = rhs_one.shape[3]
    row = lax.axis_index("row")
    col = lax.axis_index("col")
    core = col % 2
    sign = 1 - 2 * core
    here_y, here_x, here_z = row // 4, row % 4, col // 2

    target = block_rows[0, 0]
    parity = target % 2
    steps = ((1 - 2 * parity) * (target // 2 - here_z)) % 8
    target_slot = jnp.where(parity == core, 0, 8) + jnp.array(PLACES, jnp.int32)[steps]
    source = block_cols[0, 0]
    place = source // 2
    from_y = (sign * (place // 4 - here_y)) % 4
    from_x = (sign * (place % 4 - here_x)) % 4
    even = source % 2 == 0
    near = jnp.where(even, from_x, from_y)
    distant = jnp.where(even, from_y, from_x)
    later = distant == 2
    early_slot = jnp.where(even, 0, 12) + jnp.where(distant == 3, 2, distant) * 4 + near
    early_picked = pick(jnp.logical_not(later), early_slot, target_slot)
    later_picked = pick(later, jnp.where(even, 0, 4) + near, target_slot)
    all_slot = jnp.where(later, jnp.where(even, 24, 28) + near, early_slot)
    all_picked = (jnp.full((1,), target.shape[0], jnp.int32), jnp.arange(target.shape[0], dtype=jnp.int32), all_slot, target_slot)

    solved_one, even, odd = solve_one(rhs_one[0, 0], inv_one[0, 0])
    lines = list(zip(line_of(even, "x"), line_of(odd, "y")))
    factor = stage(blocks[0, 0])
    axes = ("y", "x")
    both = range(2)
    sums = []

    if PARTS == 2:
        line = lines[0]
        fwd = [move(line[q], axes[q], 1) for q in both]
        bwd = [move(line[q], axes[q], -1) for q in both]
        far = [move(fwd[q], axes[q], 1) for q in both]
        line = lines[1]
        next_fwd = [move(after(line[q], *bwd), axes[q], 1) for q in both]
        next_bwd = [move(after(line[q], *bwd), axes[q], -1) for q in both]
        pieces = [lines[0][0], bwd[0], fwd[0], lines[0][1], bwd[1], fwd[1], far[0], far[1]]
        keep, send = couple(all_picked, factor, pieces)
        far = [move(after(next_fwd[q], send), axes[q], 1) for q in both]
        fwd, bwd = next_fwd, next_bwd
        done, sent = reduce_along_z([], keep, swap_cores(send))
        sums.append(done)
    else:
        line = lines[0]
        fwd = [move(line[q], axes[q], 1) for q in both]
        bwd = [move(line[q], axes[q], -1) for q in both]
        far = [move(fwd[q], axes[q], 1) for q in both]
        sent = ()

    pieces = [line[0], bwd[0], fwd[0], line[1], bwd[1], fwd[1]]
    keep, send = couple(early_picked, factor, pieces)
    (base,) = call(merge_kernel, [shape(send.shape, F32)], keep, swap_cores(send))
    keep, send = couple(later_picked, factor, [after(far[0], *sent), far[1]])
    done, _ = reduce_along_z([base], keep, swap_cores(send))
    sums.append(done)

    width = rhs_two.shape[4] // PARTS
    columns = []
    for i, done in enumerate(sums):
        rhs = rhs_two[0, 0, 0, :, i * width : (i + 1) * width]
        columns += call(last_kernel, [shape((rows, width))], *done, rhs, inv_two[0, 0, 0])
    solved_two = jnp.concatenate(columns, 1)
    return (solved_one[None, None], solved_two[None, None, None])


def solution(mesh):
    in_specs = (
        P("row", "col", None, None, None),
        P("row", "col", None, None, None),
        P("row", "col", None, None, None),
        P("row", "col", None, None, None),
        P("row", "col", None, None, None),
        P("row", "col", None),
        P("row", "col", None),
    )
    out_specs = (P("row", "col", None, None, None), P("row", "col", None, None, None))
    return jax.shard_map(local, mesh=mesh, in_specs=in_specs, out_specs=out_specs, check_vma=False)
```

time: 304 us -> 121 us (0.40)
  waiting for transfers between devices: 145 us -> 47.4 us
  matrix products: 82.8 us -> 0 us
  local copies, waits for them, and re-layouts: 57 us -> 2.9 us
  starting transfers between devices: 0.08 us -> 42.3 us
  Pallas kernels: 0 us -> 22.1 us
  between operations: 14.1 us -> 0.82 us
    dot_general x17 -> x0, matrix products: 82.8 us -> none  [the longest x5 41.8 us: accumulate(): jnp.dot(selector, product.reshape(GROUP, block_width * rhs_count), precis...]
    all_gather x1 -> x0, waiting for transfers between devices: 77 us -> none  [local(): column = lax.all_gather(solved_one, 'row', axis=0, tiled=True)]
    reduce_scatter x1 -> x0, waiting for transfers between devices: 67.5 us -> none  [local(): lax.psum_scatter(partial_sums, 'col', scatter_dimension=0, tiled=True)]
    ppermute x0 -> x19, waiting for transfers between devices: none -> 47.4 us  [the longest x17 44 us: move(): return lax.ppermute(value, BOTH, ring_pairs(axis, steps))]
    ppermute x0 -> x19, starting transfers between devices: none -> 42.3 us  [the longest x17 34.1 us: move(): return lax.ppermute(value, BOTH, ring_pairs(axis, steps))]
    while x10 -> x0, local copies, waits for them, and re-layouts: 31.5 us -> none
    unnamed x12, local copies, waits for them, and re-layouts: 25.3 us -> 2.02 us
    pallas_call x0 -> x8, Pallas kernels: none -> 22.1 us  [the longest x2 13.7 us: couple(): pl.pallas_call(functools.partial(couple_kernel, len(pieces)), out_shape=[...]
  transfers between devices with their start and end apart: 2 -> 19, of which waited for: 2 -> 11; matrix products, arithmetic and copies ran while one was open for 1% -> 5% of each run, Pallas kernels for 0% -> 15%
where the time goes in v2:
time: 121 us; the launch traced here: 119 us
  waiting for transfers between devices  47.4 us (39%)
  starting transfers between devices  42.3 us (35%)
  Pallas kernels  22.1 us (18%)
  other arithmetic  3.56 us (3%)
  local copies, waits for them, and re-layouts  2.9 us (2%)
    ppermute x17, waiting for transfers between devices, move(): return lax.ppermute(value, BOTH, ring_pairs(axis, steps))  44 us
    ppermute x17, starting transfers between devices, move(): return lax.ppermute(value, BOTH, ring_pairs(axis, steps))  34.1 us
    pallas_call x2, Pallas kernels, couple(): pl.pallas_call(functools.partial(couple_kernel, len(pieces)), out_shape=[...  13.7 us
    ppermute x2, starting transfers between devices, swap_cores(): return lax.ppermute(value, 'col', [(i, i ^ 1) for i in range(16)])  8.24 us
    pallas_call x1, Pallas kernels, stage(): pl.pallas_call(stage_kernel, out_shape=pltpu.VMEM(blocks.shape, blocks.dt...  4.09 us
    ppermute x2, waiting for transfers between devices, swap_cores(): return lax.ppermute(value, 'col', [(i, i ^ 1) for i in range(16)])  3.44 us
  transfers between devices with their start and end apart: 19, of which 11 were waited for; matrix products, arithmetic and copies ran while one was open for 5% of the time, Pallas kernels for 15%

profile of v2, /device:TPU:1, one launch (start us, length us, event | category | flops | bytes accessed | tf_op | source)
XLA Modules:
  0.0 119.1 jit_solution(10378643213601877045)
XLA Ops:
  0.6 0.0 copy-start.2
  0.6 2.3 %shard_map.95 = (bf16[2,256,512]{2,1,0:T(8,128)(2,1)}, bf16[1,256,512]{2,1,0:T(8,128)(2,1)S(1)}, bf16[1,256,512]{2,1,0:T(8,128)(2,1)S(1)}) custom-call(bf16[2,256,512]{2,1,0:T(8,128)(2,1)} %bitcast.32, bf16[2,256,256]{2,1,0:T(8,128)(2,1)} %bitcast.33), custom_call_target="tpu_custom_call" | custom-call | tf_op jit(solution)/shard_map/pallas_call | solution.py:75
  2.9 2.1 %collective-permute-start = (bf16[1,256,512]{2,1,0:T(8,128)(2,1)S(1)}, bf16[1,256,512]{2,1,0:T(8,128)(2,1)}, u32[]{:S(2)}, u32[]{:S(2)}) collective-permute-start(bf16[1,256,512]{2,1,0:T(8,128)(2,1)S(1)} %get-tuple-element.17), channel_id=1, source_target_pairs={{0,48},{1,17},{2,50},{3,19},{4,52},{5,21},{6,54},{7,23},{8,56},{9,... | collective-permute-start | bytes 786440 | tf_op jit(solution)/shard_map/ppermute | solution.py:49
  5.0 2.4 %collective-permute-start.1 = (bf16[1,256,512]{2,1,0:T(8,128)(2,1)S(1)}, bf16[1,256,512]{2,1,0:T(8,128)(2,1)}, u32[]{:S(2)}, u32[]{:S(2)}) collective-permute-start(bf16[1,256,512]{2,1,0:T(8,128)(2,1)S(1)} %get-tuple-element.17), channel_id=1, source_target_pairs={{0,32},{1,33},{2,34},{3,35},{4,36},{5,37},{6,38},{7,39},{8,40},{9,... | collective-permute-start | bytes 786440 | tf_op jit(solution)/shard_map/ppermute | solution.py:49
  7.5 1.1 collective-permute-start.2
  8.6 1.3 %collective-permute-start.5 = (bf16[1,256,512]{2,1,0:T(8,128)(2,1)S(1)}, bf16[1,256,512]{2,1,0:T(8,128)(2,1)S(1)}, u32[]{:S(2)}, u32[]{:S(2)}) collective-permute-start(bf16[1,256,512]{2,1,0:T(8,128)(2,1)S(1)} %get-tuple-element.18), channel_id=1, source_target_pairs={{0,192},{1,65},{2,194},{3,67},{4,196},{5,69},{6,198},{7,71},{8,200... | collective-permute-start | bytes 786440 | tf_op jit(solution)/shard_map/ppermute | solution.py:49
  9.9 2.6 %collective-permute-start.6 = (bf16[1,256,512]{2,1,0:T(8,128)(2,1)S(1)}, bf16[1,256,512]{2,1,0:T(8,128)(2,1)S(1)}, u32[]{:S(2)}, u32[]{:S(2)}) collective-permute-start(bf16[1,256,512]{2,1,0:T(8,128)(2,1)S(1)} %get-tuple-element.18), channel_id=1, source_target_pairs={{0,128},{1,129},{2,130},{3,131},{4,132},{5,133},{6,134},{7,135},{8... | collective-permute-start | bytes 786440 | tf_op jit(solution)/shard_map/ppermute | solution.py:49
  12.6 0.7 copy.26
  13.3 0.1 fusion.34
  13.5 0.7 select_add_fusion
  14.2 0.0 collective-permute-done
  14.2 1.1 collective-permute-start.7
  15.4 1.0 constant_dynamic-update-slice_fusion.2
  16.3 0.5 collective-permute-done.1
  16.8 1.0 constant_dynamic-update-slice_fusion.1
  17.8 0.4 collective-permute-done.2
  18.3 3.5 %collective-permute-start.3 = (bf16[4,256,512]{2,1,0:T(8,128)(2,1)S(1)}, bf16[4,256,512]{2,1,0:T(8,128)(2,1)}, u32[]{:S(2)}, u32[]{:S(2)}) collective-permute-start(bf16[4,256,512]{2,1,0:T(8,128)(2,1)S(1)} %constant_dynamic-update-slice_fusion.refs_0_), channel_id=1, source_target_pairs={{0,64},{1,193},{2,66},{3,195},{4,68},{5,197},{6,70},{7,199},{8,72}... | collective-permute-start | bytes 3145736 | tf_op jit(solution)/shard_map/ppermute | solution.py:49
  21.8 0.0 collective-permute-done.5
  21.8 0.4 collective-permute-done.6
  22.2 1.5 %collective-permute-done.7 = bf16[1,256,512]{2,1,0:T(8,128)(2,1)S(1)} collective-permute-done((bf16[1,256,512]{2,1,0:T(8,128)(2,1)S(1)}, bf16[1,256,512]{2,1,0:T(8,128)(2,1)S(1)}, u32[]{:S(2)}, u32[]{:S(2)}) %collective-permute-start.7) | collective-permute-done | bytes 262176 | tf_op jit(solution)/shard_map/ppermute | solution.py:49
  23.7 1.6 %collective-permute-start.8 = (bf16[4,256,512]{2,1,0:T(8,128)(2,1)S(1)}, bf16[4,256,512]{2,1,0:T(8,128)(2,1)}, u32[]{:S(2)}, u32[]{:S(2)}) collective-permute-start(bf16[4,256,512]{2,1,0:T(8,128)(2,1)S(1)} %constant_dynamic-update-slice_fusion.4.refs_3_), channel_id=1, source_target_pairs={{0,16},{1,49},{2,18},{3,51},{4,20},{5,53},{6,22},{7,55},{8,24},{9,... | collective-permute-start | bytes 3145736 | tf_op jit(solution)/shard_map/ppermute | solution.py:49
  25.3 0.0 copy-done.2
  25.3 0.1 copy.30
  25.4 0.2 select_reduce_fusion
  25.6 0.6 collective-permute-start.11
  26.1 0.4 collective-permute-start.12
  26.6 0.1 compare_reduce_fusion
  26.7 0.1 reduce-window.17
  26.8 0.1 reduce-window.16
  26.9 4.1 %shard_map.96.blocks = bf16[80,256,256]{2,1,0:T(8,128)(2,1)S(1)} custom-call(bf16[80,256,256]{2,1,0:T(8,128)(2,1)} %bitcast.31), custom_call_target="tpu_custom_call" | custom-call | tf_op jit(solution)/shard_map/pallas_call | solution.py:101
  31.0 0.1 add_reduce_fusion
  31.1 0.2 select_reduce_fusion.1
  31.3 12.2 %collective-permute-done.8.refs_5_ = bf16[4,256,512]{2,1,0:T(8,128)(2,1)} collective-permute-done((bf16[4,256,512]{2,1,0:T(8,128)(2,1)S(1)}, bf16[4,256,512]{2,1,0:T(8,128)(2,1)}, u32[]{:S(2)}, u32[]{:S(2)}) %collective-permute-start.8) | collective-permute-done | bytes 1048608 | tf_op jit(solution)/shard_map/ppermute | solution.py:49
  43.5 0.7 collective-permute-start.9
  44.3 0.0 collective-permute-done.3.refs_2_
  44.3 5.1 %collective-permute-start.4 = (bf16[4,256,512]{2,1,0:T(8,128)(2,1)}, bf16[4,256,512]{2,1,0:T(8,128)(2,1)S(1)}, u32[]{:S(2)}, u32[]{:S(2)}) collective-permute-start(bf16[4,256,512]{2,1,0:T(8,128)(2,1)} %collective-permute-done.3.refs_2_), channel_id=1, source_target_pairs={{0,64},{1,193},{2,66},{3,195},{4,68},{5,197},{6,70},{7,199},{8,72}... | collective-permute-start | bytes 3145736 | tf_op jit(solution)/shard_map/ppermute | solution.py:49
  49.4 0.6 convert_reduce_fusion
  50.0 0.6 compare_select_fusion.8.target_slot
  50.7 0.6 compare_select_fusion.10.target_slot
  51.3 0.0 collective-permute-done.11.refs_1_
  51.3 0.3 collective-permute-done.12.refs_4_
  51.7 10.1 %shard_map.98 = (f32[17,256,512]{2,1,0:T(8,128)S(1)}, bf16[8,256,512]{2,1,0:T(8,128)(2,1)S(1)}) custom-call(s32[1]{0:T(128)} %bitcast.9.count, s32[80]{0:T(128)S(1)} %get-tuple-element.32.chosen, s32[80]{0:T(128)S(1)} %get-tuple-element.31.source_slot, s32[80]{0:T(128)S(1)} %compare_select_fusion.8.target_slot, bf16[80,256,256]{2,1,0:T(8,128)(2,1)S(1)} %shard_map.96.blocks, ...), custom_call_target="tpu_custom_call" | custom-call | flops 5368709120 | bytes 10485760 | tf_op jit(solution)/shard_map/pallas_call | solution.py:136
  61.8 3.3 %collective-permute-start.13 = (bf16[8,256,512]{2,1,0:T(8,128)(2,1)S(1)}, bf16[8,256,512]{2,1,0:T(8,128)(2,1)S(1)}, u32[]{:S(2)}, u32[]{:S(2)}) collective-permute-start(bf16[8,256,512]{2,1,0:T(8,128)(2,1)S(1)} %get-tuple-element.22), channel_id=1, source_target_pairs={{0,1},{1,0},{2,3},{3,2},{4,5},{5,4},{6,7},{7,6},{8,9},{9,8},{10,11... | collective-permute-start | bytes 6291464 | tf_op jit(solution)/shard_map/ppermute | solution.py:53
  65.1 0.0 collective-permute-done.4.refs_0_
  65.1 0.0 collective-permute-done.9.refs_1_
  65.1 3.5 %shard_map.97 = (f32[17,256,512]{2,1,0:T(8,128)S(1)}, bf16[8,256,512]{2,1,0:T(8,128)(2,1)S(1)}) custom-call(s32[1]{0:T(128)} %bitcast.4.count, s32[80]{0:T(128)S(1)} %get-tuple-element.36.chosen, s32[80]{0:T(128)S(1)} %get-tuple-element.37.source_slot, s32[80]{0:T(128)S(1)} %compare_select_fusion.10.target_slot, bf16[80,256,256]{2,1,0:T(8,128)(2,1)S(1)} %shard_map.96.blocks, ...), custom_call_target="tpu_custom_call" | custom-call | flops 5368709120 | bytes 10485760 | tf_op jit(solution)/shard_map/pallas_call | solution.py:136
  68.7 4.9 %collective-permute-start.10 = (bf16[8,256,512]{2,1,0:T(8,128)(2,1)S(1)}, bf16[8,256,512]{2,1,0:T(8,128)(2,1)S(1)}, u32[]{:S(2)}, u32[]{:S(2)}) collective-permute-start(bf16[8,256,512]{2,1,0:T(8,128)(2,1)S(1)} %get-tuple-element.20), channel_id=1, source_target_pairs={{0,1},{1,0},{2,3},{3,2},{4,5},{5,4},{6,7},{7,6},{8,9},{9,8},{10,11... | collective-permute-start | bytes 6291464 | tf_op jit(solution)/shard_map/ppermute | solution.py:53
  73.6 0.0 collective-permute-done.13.other
  73.6 0.3 shard_map.99.refs_0_
  74.0 3.4 %collective-permute-done.10.other = bf16[8,256,512]{2,1,0:T(8,128)(2,1)S(1)} collective-permute-done((bf16[8,256,512]{2,1,0:T(8,128)(2,1)S(1)}, bf16[8,256,512]{2,1,0:T(8,128)(2,1)S(1)}, u32[]{:S(2)}, u32[]{:S(2)}) %collective-permute-start.10) | collective-permute-done | bytes 2097184 | tf_op jit(solution)/shard_map/ppermute | solution.py:53
  77.4 0.5 shard_map.100
  77.9 5.6 %collective-permute-start.14 = (bf16[2,256,512]{2,1,0:T(8,128)(2,1)S(1)}, bf16[2,256,512]{2,1,0:T(8,128)(2,1)S(1)}, u32[]{:S(2)}, u32[]{:S(2)}) collective-permute-start(bf16[2,256,512]{2,1,0:T(8,128)(2,1)S(1)} %get-tuple-element.24), channel_id=1, source_target_pairs={{0,2},{1,15},{2,4},{3,1},{4,6},{5,3},{6,8},{7,5},{8,10},{9,7},{10,... | collective-permute-start | bytes 1572872 | tf_op jit(solution)/shard_map/ppermute | solution.py:49
  83.5 0.0 collective-permute-start.15
  83.5 1.9 %collective-permute-start.16 = (bf16[256,512]{1,0:T(8,128)(2,1)S(1)}, bf16[256,512]{1,0:T(8,128)(2,1)S(1)}, u32[]{:S(2)}, u32[]{:S(2)}) collective-permute-start(bf16[256,512]{1,0:T(8,128)(2,1)S(1)} %get-tuple-element.26), channel_id=1, source_target_pairs={{0,4},{1,13},{2,6},{3,15},{4,8},{5,1},{6,10},{7,3},{8,12},{9,5},{1... | collective-permute-start | bytes 786440 | tf_op jit(solution)/shard_map/ppermute | solution.py:49
  85.4 15.4 %collective-permute-done.16.far = bf16[256,512]{1,0:T(8,128)(2,1)S(1)} collective-permute-done((bf16[256,512]{1,0:T(8,128)(2,1)S(1)}, bf16[256,512]{1,0:T(8,128)(2,1)S(1)}, u32[]{:S(2)}, u32[]{:S(2)}) %collective-permute-start.16) | collective-permute-done | bytes 262176 | tf_op jit(solution)/shard_map/ppermute | solution.py:49
  100.9 0.0 collective-permute-done.14.fwd
  100.9 0.4 collective-permute-done.15.bwd
  101.2 0.2 shard_map.101
  101.4 3.8 %collective-permute-start.17 = (bf16[256,512]{1,0:T(8,128)(2,1)S(1)}, bf16[256,512]{1,0:T(8,128)(2,1)S(1)}, u32[]{:S(2)}, u32[]{:S(2)}) collective-permute-start(bf16[256,512]{1,0:T(8,128)(2,1)S(1)} %get-tuple-element.28), channel_id=1, source_target_pairs={{0,4},{1,13},{2,6},{3,15},{4,8},{5,1},{6,10},{7,3},{8,12},{9,5},{1... | collective-permute-start | bytes 786440 | tf_op jit(solution)/shard_map/ppermute | solution.py:49
  105.2 0.0 collective-permute-start.18
  105.2 7.2 %collective-permute-done.17.fwd = bf16[256,512]{1,0:T(8,128)(2,1)S(1)} collective-permute-done((bf16[256,512]{1,0:T(8,128)(2,1)S(1)}, bf16[256,512]{1,0:T(8,128)(2,1)S(1)}, u32[]{:S(2)}, u32[]{:S(2)}) %collective-permute-start.17) | collective-permute-done | bytes 262176 | tf_op jit(solution)/shard_map/ppermute | solution.py:49
  112.5 5.6 %collective-permute-done.18.bwd = bf16[256,512]{1,0:T(8,128)(2,1)S(1)} collective-permute-done((bf16[256,512]{1,0:T(8,128)(2,1)S(1)}, bf16[256,512]{1,0:T(8,128)(2,1)S(1)}, u32[]{:S(2)}, u32[]{:S(2)}) %collective-permute-start.18) | collective-permute-done | bytes 262176 | tf_op jit(solution)/shard_map/ppermute | solution.py:49
  118.1 0.0 copy-done
  118.1 1.0 shard_map.102
  (12 shorter events, 0.1 us)
Async XLA Ops:
  0.6 24.6 %copy-start.2 = (s32[1,1,80]{2,1,0:T(1,128)S(1)}, s32[1,1,80]{2,1,0:T(1,128)}, u32[]{:S(2)}) copy-start(s32[1,1,80]{2,1,0:T(1,128)} %param.13) | copy-start | bytes 964
  2.9 11.3 %collective-permute-start = (bf16[1,256,512]{2,1,0:T(8,128)(2,1)S(1)}, bf16[1,256,512]{2,1,0:T(8,128)(2,1)}, u32[]{:S(2)}, u32[]{:S(2)}) collective-permute-start(bf16[1,256,512]{2,1,0:T(8,128)(2,1)S(1)} %get-tuple-element.17), channel_id=1, source_target_pairs={{0,48},{1,17},{2,50},{3,19},{4,52},{5,21},{6,54},{7,23},{8,56},{9,... | collective-permute-start | bytes 786440 | tf_op jit(solution)/shard_map/ppermute | solution.py:49
  5.0 11.8 %collective-permute-start.1 = (bf16[1,256,512]{2,1,0:T(8,128)(2,1)S(1)}, bf16[1,256,512]{2,1,0:T(8,128)(2,1)}, u32[]{:S(2)}, u32[]{:S(2)}) collective-permute-start(bf16[1,256,512]{2,1,0:T(8,128)(2,1)S(1)} %get-tuple-element.17), channel_id=1, source_target_pairs={{0,32},{1,33},{2,34},{3,35},{4,36},{5,37},{6,38},{7,39},{8,40},{9,... | collective-permute-start | bytes 786440 | tf_op jit(solution)/shard_map/ppermute | solution.py:49
  7.5 10.8 %collective-permute-start.2 = (bf16[1,256,512]{2,1,0:T(8,128)(2,1)S(1)}, bf16[1,256,512]{2,1,0:T(8,128)(2,1)S(1)}, u32[]{:S(2)}, u32[]{:S(2)}) collective-permute-start(bf16[1,256,512]{2,1,0:T(8,128)(2,1)S(1)} %get-tuple-element.17), channel_id=1, source_target_pairs={{0,16},{1,49},{2,18},{3,51},{4,20},{5,53},{6,22},{7,55},{8,24},{9,... | collective-permute-start | bytes 786440 | tf_op jit(solution)/shard_map/ppermute | solution.py:49
  8.6 13.2 %collective-permute-start.5 = (bf16[1,256,512]{2,1,0:T(8,128)(2,1)S(1)}, bf16[1,256,512]{2,1,0:T(8,128)(2,1)S(1)}, u32[]{:S(2)}, u32[]{:S(2)}) collective-permute-start(bf16[1,256,512]{2,1,0:T(8,128)(2,1)S(1)} %get-tuple-element.18), channel_id=1, source_target_pairs={{0,192},{1,65},{2,194},{3,67},{4,196},{5,69},{6,198},{7,71},{8,200... | collective-permute-start | bytes 786440 | tf_op jit(solution)/shard_map/ppermute | solution.py:49
  9.9 12.2 %collective-permute-start.6 = (bf16[1,256,512]{2,1,0:T(8,128)(2,1)S(1)}, bf16[1,256,512]{2,1,0:T(8,128)(2,1)S(1)}, u32[]{:S(2)}, u32[]{:S(2)}) collective-permute-start(bf16[1,256,512]{2,1,0:T(8,128)(2,1)S(1)} %get-tuple-element.18), channel_id=1, source_target_pairs={{0,128},{1,129},{2,130},{3,131},{4,132},{5,133},{6,134},{7,135},{8... | collective-permute-start | bytes 786440 | tf_op jit(solution)/shard_map/ppermute | solution.py:49
  14.2 9.4 %collective-permute-start.7 = (bf16[1,256,512]{2,1,0:T(8,128)(2,1)S(1)}, bf16[1,256,512]{2,1,0:T(8,128)(2,1)S(1)}, u32[]{:S(2)}, u32[]{:S(2)}) collective-permute-start(bf16[1,256,512]{2,1,0:T(8,128)(2,1)S(1)} %get-tuple-element.18), channel_id=1, source_target_pairs={{0,64},{1,193},{2,66},{3,195},{4,68},{5,197},{6,70},{7,199},{8,72}... | collective-permute-start | bytes 786440 | tf_op jit(solution)/shard_map/ppermute | solution.py:49
  18.3 26.0 %collective-permute-start.3 = (bf16[4,256,512]{2,1,0:T(8,128)(2,1)S(1)}, bf16[4,256,512]{2,1,0:T(8,128)(2,1)}, u32[]{:S(2)}, u32[]{:S(2)}) collective-permute-start(bf16[4,256,512]{2,1,0:T(8,128)(2,1)S(1)} %constant_dynamic-update-slice_fusion.refs_0_), channel_id=1, source_target_pairs={{0,64},{1,193},{2,66},{3,195},{4,68},{5,197},{6,70},{7,199},{8,72}... | collective-permute-start | bytes 3145736 | tf_op jit(solution)/shard_map/ppermute | solution.py:49
  23.7 19.8 %collective-permute-start.8 = (bf16[4,256,512]{2,1,0:T(8,128)(2,1)S(1)}, bf16[4,256,512]{2,1,0:T(8,128)(2,1)}, u32[]{:S(2)}, u32[]{:S(2)}) collective-permute-start(bf16[4,256,512]{2,1,0:T(8,128)(2,1)S(1)} %constant_dynamic-update-slice_fusion.4.refs_3_), channel_id=1, source_target_pairs={{0,16},{1,49},{2,18},{3,51},{4,20},{5,53},{6,22},{7,55},{8,24},{9,... | collective-permute-start | bytes 3145736 | tf_op jit(solution)/shard_map/ppermute | solution.py:49
  25.6 25.7 %collective-permute-start.11 = (bf16[4,256,512]{2,1,0:T(8,128)(2,1)S(1)}, bf16[4,256,512]{2,1,0:T(8,128)(2,1)}, u32[]{:S(2)}, u32[]{:S(2)}) collective-permute-start(bf16[4,256,512]{2,1,0:T(8,128)(2,1)S(1)} %constant_dynamic-update-slice_fusion.refs_0_), channel_id=1, source_target_pairs={{0,192},{1,65},{2,194},{3,67},{4,196},{5,69},{6,198},{7,71},{8,200... | collective-permute-start | bytes 3145736 | tf_op jit(solution)/shard_map/ppermute | solution.py:49
  26.1 25.5 %collective-permute-start.12 = (bf16[4,256,512]{2,1,0:T(8,128)(2,1)S(1)}, bf16[4,256,512]{2,1,0:T(8,128)(2,1)}, u32[]{:S(2)}, u32[]{:S(2)}) collective-permute-start(bf16[4,256,512]{2,1,0:T(8,128)(2,1)S(1)} %constant_dynamic-update-slice_fusion.4.refs_3_), channel_id=1, source_target_pairs={{0,48},{1,17},{2,50},{3,19},{4,52},{5,21},{6,54},{7,23},{8,56},{9,... | collective-permute-start | bytes 3145736 | tf_op jit(solution)/shard_map/ppermute | solution.py:49
  43.5 21.6 %collective-permute-start.9 = (bf16[4,256,512]{2,1,0:T(8,128)(2,1)}, bf16[4,256,512]{2,1,0:T(8,128)(2,1)S(1)}, u32[]{:S(2)}, u32[]{:S(2)}) collective-permute-start(bf16[4,256,512]{2,1,0:T(8,128)(2,1)} %collective-permute-done.8.refs_5_), channel_id=1, source_target_pairs={{0,16},{1,49},{2,18},{3,51},{4,20},{5,53},{6,22},{7,55},{8,24},{9,... | collective-permute-start | bytes 3145736 | tf_op jit(solution)/shard_map/ppermute | solution.py:49
  44.3 20.8 %collective-permute-start.4 = (bf16[4,256,512]{2,1,0:T(8,128)(2,1)}, bf16[4,256,512]{2,1,0:T(8,128)(2,1)S(1)}, u32[]{:S(2)}, u32[]{:S(2)}) collective-permute-start(bf16[4,256,512]{2,1,0:T(8,128)(2,1)} %collective-permute-done.3.refs_2_), channel_id=1, source_target_pairs={{0,64},{1,193},{2,66},{3,195},{4,68},{5,197},{6,70},{7,199},{8,72}... | collective-permute-start | bytes 3145736 | tf_op jit(solution)/shard_map/ppermute | solution.py:49
  61.8 11.8 %collective-permute-start.13 = (bf16[8,256,512]{2,1,0:T(8,128)(2,1)S(1)}, bf16[8,256,512]{2,1,0:T(8,128)(2,1)S(1)}, u32[]{:S(2)}, u32[]{:S(2)}) collective-permute-start(bf16[8,256,512]{2,1,0:T(8,128)(2,1)S(1)} %get-tuple-element.22), channel_id=1, source_target_pairs={{0,1},{1,0},{2,3},{3,2},{4,5},{5,4},{6,7},{7,6},{8,9},{9,8},{10,11... | collective-permute-start | bytes 6291464 | tf_op jit(solution)/shard_map/ppermute | solution.py:53
  68.7 8.7 %collective-permute-start.10 = (bf16[8,256,512]{2,1,0:T(8,128)(2,1)S(1)}, bf16[8,256,512]{2,1,0:T(8,128)(2,1)S(1)}, u32[]{:S(2)}, u32[]{:S(2)}) collective-permute-start(bf16[8,256,512]{2,1,0:T(8,128)(2,1)S(1)} %get-tuple-element.20), channel_id=1, source_target_pairs={{0,1},{1,0},{2,3},{3,2},{4,5},{5,4},{6,7},{7,6},{8,9},{9,8},{10,11... | collective-permute-start | bytes 6291464 | tf_op jit(solution)/shard_map/ppermute | solution.py:53
  77.4 40.7 %copy-start = (bf16[1,1,1,256,512]{4,3,2,1,0:T(8,128)(2,1)S(1)}, bf16[1,1,1,256,512]{4,3,2,1,0:T(8,128)(2,1)}, u32[]{:S(2)}) copy-start(bf16[1,1,1,256,512]{4,3,2,1,0:T(8,128)(2,1)} %param.10) | copy-start | bytes 786436
  77.4 40.7 %copy-start.1 = (bf16[1,1,1,256,256]{4,3,2,1,0:T(8,128)(2,1)S(1)}, bf16[1,1,1,256,256]{4,3,2,1,0:T(8,128)(2,1)}, u32[]{:S(2)}) copy-start(bf16[1,1,1,256,256]{4,3,2,1,0:T(8,128)(2,1)} %param.11) | copy-start | bytes 393220
  77.9 23.0 %collective-permute-start.14 = (bf16[2,256,512]{2,1,0:T(8,128)(2,1)S(1)}, bf16[2,256,512]{2,1,0:T(8,128)(2,1)S(1)}, u32[]{:S(2)}, u32[]{:S(2)}) collective-permute-start(bf16[2,256,512]{2,1,0:T(8,128)(2,1)S(1)} %get-tuple-element.24), channel_id=1, source_target_pairs={{0,2},{1,15},{2,4},{3,1},{4,6},{5,3},{6,8},{7,5},{8,10},{9,7},{10,... | collective-permute-start | bytes 1572872 | tf_op jit(solution)/shard_map/ppermute | solution.py:49
  83.5 17.7 %collective-permute-start.15 = (bf16[2,256,512]{2,1,0:T(8,128)(2,1)S(1)}, bf16[2,256,512]{2,1,0:T(8,128)(2,1)S(1)}, u32[]{:S(2)}, u32[]{:S(2)}) collective-permute-start(bf16[2,256,512]{2,1,0:T(8,128)(2,1)S(1)} %get-tuple-element.25), channel_id=1, source_target_pairs={{0,14},{1,3},{2,0},{3,5},{4,2},{5,7},{6,4},{7,9},{8,6},{9,11},{10,... | collective-permute-start | bytes 1572872 | tf_op jit(solution)/shard_map/ppermute | solution.py:49
  83.5 17.4 %collective-permute-start.16 = (bf16[256,512]{1,0:T(8,128)(2,1)S(1)}, bf16[256,512]{1,0:T(8,128)(2,1)S(1)}, u32[]{:S(2)}, u32[]{:S(2)}) collective-permute-start(bf16[256,512]{1,0:T(8,128)(2,1)S(1)} %get-tuple-element.26), channel_id=1, source_target_pairs={{0,4},{1,13},{2,6},{3,15},{4,8},{5,1},{6,10},{7,3},{8,12},{9,5},{1... | collective-permute-start | bytes 786440 | tf_op jit(solution)/shard_map/ppermute | solution.py:49
  101.4 11.0 %collective-permute-start.17 = (bf16[256,512]{1,0:T(8,128)(2,1)S(1)}, bf16[256,512]{1,0:T(8,128)(2,1)S(1)}, u32[]{:S(2)}, u32[]{:S(2)}) collective-permute-start(bf16[256,512]{1,0:T(8,128)(2,1)S(1)} %get-tuple-element.28), channel_id=1, source_target_pairs={{0,4},{1,13},{2,6},{3,15},{4,8},{5,1},{6,10},{7,3},{8,12},{9,5},{1... | collective-permute-start | bytes 786440 | tf_op jit(solution)/shard_map/ppermute | solution.py:49
  105.2 12.9 %collective-permute-start.18 = (bf16[256,512]{1,0:T(8,128)(2,1)S(1)}, bf16[256,512]{1,0:T(8,128)(2,1)S(1)}, u32[]{:S(2)}, u32[]{:S(2)}) collective-permute-start(bf16[256,512]{1,0:T(8,128)(2,1)S(1)} %get-tuple-element.29), channel_id=1, source_target_pairs={{0,12},{1,5},{2,14},{3,7},{4,0},{5,9},{6,2},{7,11},{8,4},{9,13},{1... | collective-permute-start | bytes 786440 | tf_op jit(solution)/shard_map/ppermute | solution.py:49

commit v3 on v2

--- a/solution.py
+++ b/solution.py
@@ -7,8 +7,8 @@
 from jax.experimental.pallas import tpu as pltpu
 from jax.sharding import PartitionSpec as P
 
-PARTS = 1
-STEP = 8
+PARTS = 2
+STEP = 16
 BOTH = ("row", "col")
 MIB = 1024 * 1024
 F32 = jnp.float32
@@ -65,13 +65,11 @@
         copies[2 * q + 1].wait()
         value = jnp.dot(inverse[q], rhs[q], preferred_element_type=F32).astype(BF16)
         solved[q] = value
-        width = value.shape[1] // PARTS
-        for i in range(PARTS):
-            out[i] = value[:, i * width : (i + 1) * width]
+        out[0] = value
 
 
 def solve_one(rhs, inverse):
-    part = shape((PARTS, rhs.shape[1], rhs.shape[2] // PARTS))
+    part = shape((1, *rhs.shape[1:]))
     return pl.pallas_call(
         solve_one_kernel,
         out_shape=[shape(rhs.shape), part, part],
@@ -86,34 +84,37 @@
     )(*[pltpu.with_memory_space_constraint(value, pltpu.HBM) for value in (rhs, inverse)])
 
 
-def stage_kernel(blocks_hbm, blocks, sems):
+def stage_kernel(blocks_hbm, first_line, second_line, blocks, token, sems):
     size = blocks.shape[0] // STEP
     copies = []
     for i in range(size):
         span = pl.ds(i * STEP, STEP)
         copies.append(pltpu.make_async_copy(blocks_hbm.at[span], blocks.at[span], sems.at[i]))
         copies[-1].start()
+    token[...] = jnp.zeros_like(token)
     for copy in copies:
         copy.wait()
 
 
-def stage(blocks):
+def stage(blocks, lines):
     return pl.pallas_call(
         stage_kernel,
-        out_shape=pltpu.VMEM(blocks.shape, blocks.dtype),
-        in_specs=[whole(pl.ANY)],
-        out_specs=whole(),
+        out_shape=[pltpu.VMEM(blocks.shape, blocks.dtype), shape((8, 128), F32)],
+        in_specs=[whole(pl.ANY)] * 3,
+        out_specs=[whole()] * 2,
         scratch_shapes=[pltpu.SemaphoreType.DMA((blocks.shape[0] // STEP,))],
         compiler_params=params(4),
-    )(pltpu.with_memory_space_constraint(blocks, pltpu.HBM))
-
-
-def couple_kernel(slots, count, chosen, source_slot, target_slot, blocks, *refs):
-    pieces = refs[:slots]
-    total, send, sources, sems = refs[slots:]
+    )(pltpu.with_memory_space_constraint(blocks, pltpu.HBM), *lines)
+
+
+def couple_kernel(size, start, count, chosen, source_slot, target_slot, blocks, *refs):
+    pieces = refs[:size]
+    total, send, sources, sems = refs[size:]
+    width = sources.shape[2]
     copies = []
     for i, piece in enumerate(pieces):
-        copies.append(pltpu.make_async_copy(piece, sources.at[pl.ds(4 * i, 4)], sems.at[i]))
+        spot = sources.at[pl.ds(4 * i, 4)]
+        copies.append(pltpu.make_async_copy(piece.at[:, :, pl.ds(start, width)], spot, sems.at[i]))
         copies[-1].start()
     total[...] = jnp.zeros_like(total)
     for copy in copies:
@@ -130,16 +131,16 @@
     send[...] = total[8:16].astype(BF16)
 
 
-def couple(picked, blocks, pieces):
+def couple(picked, blocks, pieces, start, width):
     count, rows, _ = blocks.shape
-    width = pieces[0].shape[-1]
+    slots = 4 * len(pieces)
     return pl.pallas_call(
-        functools.partial(couple_kernel, len(pieces)),
+        functools.partial(couple_kernel, len(pieces), start),
         out_shape=[pltpu.VMEM((17, rows, width), F32), shape((8, rows, width))],
         in_specs=[whole(pltpu.SMEM)] * 4 + [whole()] + [whole(pl.ANY)] * len(pieces),
         out_specs=[whole()] * 2,
         scratch_shapes=[
-            pltpu.VMEM((4 * len(pieces), rows, width), BF16),
+            pltpu.VMEM((slots, rows, width), BF16),
             pltpu.SemaphoreType.DMA((len(pieces),)),
         ],
         compiler_params=params(16),
@@ -168,13 +169,11 @@
     base[...] = keep[:8] + other[...].astype(F32)
 
 
-def first_kernel(bases, keep, other, *refs):
-    base = refs[:bases]
-    fwd, bwd, far, held = refs[bases:]
-
+def first_kernel(column, base, keep, other, fwd, bwd, far, held):
     def part(place):
-        value = keep[place] + other[place].astype(F32)
-        return value + base[0][place] if bases else value
+        width = keep.shape[2]
+        early = base[place, :, column : column + width]
+        return early + (keep[place] + other[place].astype(F32))
 
     fwd[0] = part(0).astype(BF16)
     fwd[1] = part(1).astype(BF16)
@@ -191,10 +190,15 @@
     own[...] = held[2] + (fwd[0].astype(F32) + bwd[0].astype(F32))
 
 
-def last_kernel(own, fwd, bwd, rhs, inverse, solved):
+def last_kernel(start, own, fwd, bwd, rhs, inverse, *refs):
+    solved = refs[-1]
+    width = own.shape[1]
     coupled = own[...] + (fwd[...].astype(F32) + bwd[...].astype(F32))
-    residual = (rhs[...].astype(F32) - coupled).astype(BF16)
-    solved[...] = jnp.dot(inverse[...], residual, preferred_element_type=F32).astype(BF16)
+    residual = (rhs[:, start : start + width].astype(F32) - coupled).astype(BF16)
+    value = jnp.dot(inverse[...], residual, preferred_element_type=F32).astype(BF16)
+    if start:
+        solved[:, :start] = refs[0][...]
+    solved[:, start : start + width] = value
 
 
 def call(kernel, outs, *args):
@@ -211,27 +215,26 @@
     return lax.optimization_barrier((value, *others))[0]
 
 
-def line_of(part, axis):
+def line_of(part, axis, direct):
     fwd = move(part, axis, 1)
     bwd = move(part, axis, -1)
-    far = move(part, axis, 2)
-    return [jnp.stack([part[i], bwd[i], far[i], fwd[i]]) for i in range(PARTS)]
-
-
-def reduce_along_z(base, keep, other):
+    far = move(part, axis, 2) if direct else move(fwd, axis, 1)
+    return jnp.concatenate([part, bwd, far, fwd])
+
+
+def reduce_along_z(column, base, keep, other):
     _, rows, width = other.shape
     one = shape((rows, width))
     two = shape((2, rows, width))
-    kernel = functools.partial(first_kernel, len(base))
-    fwd, bwd, far, held = call(kernel, [two, two, one, shape((3, rows, width), F32)], keep, other, *base)
+    kernel = functools.partial(first_kernel, column)
+    fwd, bwd, far, held = call(kernel, [two, two, one, shape((3, rows, width), F32)], base, keep, other)
     fwd = move(fwd, "z", 1)
     bwd = move(bwd, "z", -1)
     far = move(far, "z", 2)
-    sent = (fwd, bwd, far)
     out_fwd, out_bwd, own = call(second_kernel, [one, one, shape((rows, width), F32)], held, fwd, bwd, far)
     out_fwd = move(out_fwd, "z", 2)
     out_bwd = move(out_bwd, "z", -2)
-    return (own, out_fwd, out_bwd), sent
+    return own, out_fwd, out_bwd
 
 
 def local(rhs_one, inv_one, rhs_two, inv_two, blocks, block_rows, block_cols):
@@ -253,55 +256,34 @@
     even = source % 2 == 0
     near = jnp.where(even, from_x, from_y)
     distant = jnp.where(even, from_y, from_x)
-    later = distant == 2
-    early_slot = jnp.where(even, 0, 12) + jnp.where(distant == 3, 2, distant) * 4 + near
-    early_picked = pick(jnp.logical_not(later), early_slot, target_slot)
-    later_picked = pick(later, jnp.where(even, 0, 4) + near, target_slot)
-    all_slot = jnp.where(later, jnp.where(even, 24, 28) + near, early_slot)
-    all_picked = (jnp.full((1,), target.shape[0], jnp.int32), jnp.arange(target.shape[0], dtype=jnp.int32), all_slot, target_slot)
+    ranks = jnp.where((distant == 1) | (distant == 2), 1, 0)
+    slot = (jnp.where(even, 0, 2) + jnp.where((distant == 2) | (distant == 3), 1, 0)) * 4 + near
+    early_picked = pick(ranks == 0, slot, target_slot)
+    later_picked = pick(ranks == 1, slot, target_slot)
 
     solved_one, even, odd = solve_one(rhs_one[0, 0], inv_one[0, 0])
-    lines = list(zip(line_of(even, "x"), line_of(odd, "y")))
-    factor = stage(blocks[0, 0])
+    lines = [line_of(even, "x", False), line_of(odd, "y", False)]
     axes = ("y", "x")
     both = range(2)
-    sums = []
-
-    if PARTS == 2:
-        line = lines[0]
-        fwd = [move(line[q], axes[q], 1) for q in both]
-        bwd = [move(line[q], axes[q], -1) for q in both]
-        far = [move(fwd[q], axes[q], 1) for q in both]
-        line = lines[1]
-        next_fwd = [move(after(line[q], *bwd), axes[q], 1) for q in both]
-        next_bwd = [move(after(line[q], *bwd), axes[q], -1) for q in both]
-        pieces = [lines[0][0], bwd[0], fwd[0], lines[0][1], bwd[1], fwd[1], far[0], far[1]]
-        keep, send = couple(all_picked, factor, pieces)
-        far = [move(after(next_fwd[q], send), axes[q], 1) for q in both]
-        fwd, bwd = next_fwd, next_bwd
-        done, sent = reduce_along_z([], keep, swap_cores(send))
-        sums.append(done)
-    else:
-        line = lines[0]
-        fwd = [move(line[q], axes[q], 1) for q in both]
-        bwd = [move(line[q], axes[q], -1) for q in both]
-        far = [move(fwd[q], axes[q], 1) for q in both]
-        sent = ()
-
-    pieces = [line[0], bwd[0], fwd[0], line[1], bwd[1], fwd[1]]
-    keep, send = couple(early_picked, factor, pieces)
+
+    fwd = [move(lines[q], axes[q], 1) for q in both]
+    factor, token = stage(blocks[0, 0], lines)
+    bwd = [move(after(lines[q], token), axes[q], -1) for q in both]
+    far = [move(fwd[q], axes[q], 1) for q in both]
+
+    whole_width = rhs_two.shape[4]
+    pieces = [lines[0], fwd[0], lines[1], fwd[1]]
+    keep, send = couple(early_picked, factor, pieces, 0, whole_width)
     (base,) = call(merge_kernel, [shape(send.shape, F32)], keep, swap_cores(send))
-    keep, send = couple(later_picked, factor, [after(far[0], *sent), far[1]])
-    done, _ = reduce_along_z([base], keep, swap_cores(send))
-    sums.append(done)
-
-    width = rhs_two.shape[4] // PARTS
-    columns = []
-    for i, done in enumerate(sums):
-        rhs = rhs_two[0, 0, 0, :, i * width : (i + 1) * width]
-        columns += call(last_kernel, [shape((rows, width))], *done, rhs, inv_two[0, 0, 0])
-    solved_two = jnp.concatenate(columns, 1)
-    return (solved_one[None, None], solved_two[None, None, None])
+    width = whole_width // PARTS
+    solved_two = []
+    for i in range(PARTS):
+        start = i * width
+        keep, send = couple(later_picked, factor, [bwd[0], far[0], bwd[1], far[1]], start, width)
+        sums = reduce_along_z(start, base, keep, swap_cores(send))
+        kernel = functools.partial(last_kernel, start)
+        solved_two = call(kernel, [shape((rows, start + width))], *sums, rhs_two[0, 0, 0], inv_two[0, 0, 0], *solved_two)
+    return (solved_one[None, None], solved_two[0][None, None, None])
 
 
 def solution(mesh):

time: 121 us -> 112 us (0.926)
  waiting for transfers between devices: 47.4 us -> 21.7 us
  starting transfers between devices: 42.3 us -> 54.3 us
  Pallas kernels: 22.1 us -> 25.5 us
  other arithmetic: 3.56 us -> 5.91 us
    ppermute x17 -> x22, waiting for transfers between devices: 44 us -> 21.7 us  [move(): return lax.ppermute(value, BOTH, ring_pairs(axis, steps))]
    ppermute x17 -> x22, starting transfers between devices: 34.1 us -> 43.1 us  [move(): return lax.ppermute(value, BOTH, ring_pairs(axis, steps))]
    ppermute x2 -> x3, waiting for transfers between devices: 3.44 us -> 0.01 us  [swap_cores(): return lax.ppermute(value, 'col', [(i, i ^ 1) for i in range(16)])]
    pallas_call x3 -> x4, Pallas kernels: 17.8 us -> 20.8 us  [the longest x3 16.1 us: couple(): pl.pallas_call(functools.partial(couple_kernel, len(pieces), start), out_...]
    ppermute x2 -> x3, starting transfers between devices: 8.24 us -> 11.2 us  [swap_cores(): return lax.ppermute(value, 'col', [(i, i ^ 1) for i in range(16)])]
    gather x2, other arithmetic: 0.28 us -> 2.17 us  [local(): jnp.array(PLACES, jnp.int32)[steps]]
  transfers between devices with their start and end apart: 19 -> 25, of which waited for: 11 -> 8; matrix products, arithmetic and copies ran while one was open for 5% -> 8% of each run, Pallas kernels for 15% -> 20%
where the time goes in v3:
time: 112 us; the launch traced here: 111 us
  starting transfers between devices  54.3 us (48%)
  Pallas kernels  25.5 us (23%)
  waiting for transfers between devices  21.7 us (19%)
  other arithmetic  5.91 us (5%)
  local copies, waits for them, and re-layouts  2.61 us (2%)
    ppermute x22, starting transfers between devices, move(): return lax.ppermute(value, BOTH, ring_pairs(axis, steps))  43.1 us
    ppermute x22, waiting for transfers between devices, move(): return lax.ppermute(value, BOTH, ring_pairs(axis, steps))  21.7 us
    pallas_call x3, Pallas kernels, couple(): pl.pallas_call(functools.partial(couple_kernel, len(pieces), start), out_...  16.1 us
    ppermute x3, starting transfers between devices, swap_cores(): return lax.ppermute(value, 'col', [(i, i ^ 1) for i in range(16)])  11.2 us
    pallas_call x1, Pallas kernels, stage(): pl.pallas_call(stage_kernel, out_shape=[pltpu.VMEM(blocks.shape, blocks.d...  4.7 us
    pallas_call x7, Pallas kernels, call(): pl.pallas_call(kernel, out_shape=outs, in_specs=[whole()] * len(args), ou...  2.38 us
    pallas_call x1, Pallas kernels, solve_one(): pl.pallas_call(solve_one_kernel, out_shape=[shape(rhs.shape), part, part]...  2.27 us
  transfers between devices with their start and end apart: 25, of which 8 were waited for; matrix products, arithmetic and copies ran while one was open for 8% of the time, Pallas kernels for 20%

profile of v3, /device:TPU:1, one launch (start us, length us, event | category | flops | bytes accessed | tf_op | source)
XLA Modules:
  0.0 110.9 jit_solution(12746009827354262692)
XLA Ops:
  0.6 0.0 copy-start.2
  0.6 2.3 %shard_map.95 = (bf16[2,256,512]{2,1,0:T(8,128)(2,1)}, bf16[1,256,512]{2,1,0:T(8,128)(2,1)S(1)}, bf16[1,256,512]{2,1,0:T(8,128)(2,1)S(1)}) custom-call(bf16[2,256,512]{2,1,0:T(8,128)(2,1)} %bitcast.34, bf16[2,256,256]{2,1,0:T(8,128)(2,1)} %bitcast.35), custom_call_target="tpu_custom_call" | custom-call | tf_op jit(solution)/shard_map/pallas_call | solution.py:73
  2.9 2.1 %collective-permute-start = (bf16[1,256,512]{2,1,0:T(8,128)(2,1)S(1)}, bf16[1,256,512]{2,1,0:T(8,128)(2,1)S(1)}, u32[]{:S(2)}, u32[]{:S(2)}) collective-permute-start(bf16[1,256,512]{2,1,0:T(8,128)(2,1)S(1)} %get-tuple-element.30), channel_id=1, source_target_pairs={{0,48},{1,17},{2,50},{3,19},{4,52},{5,21},{6,54},{7,23},{8,56},{9,... | collective-permute-start | bytes 786440 | tf_op jit(solution)/shard_map/ppermute | solution.py:49
  5.0 1.4 %collective-permute-start.1 = (bf16[1,256,512]{2,1,0:T(8,128)(2,1)S(1)}, bf16[1,256,512]{2,1,0:T(8,128)(2,1)S(1)}, u32[]{:S(2)}, u32[]{:S(2)}) collective-permute-start(bf16[1,256,512]{2,1,0:T(8,128)(2,1)S(1)} %get-tuple-element.30), channel_id=1, source_target_pairs={{0,16},{1,49},{2,18},{3,51},{4,20},{5,53},{6,22},{7,55},{8,24},{9,... | collective-permute-start | bytes 786440 | tf_op jit(solution)/shard_map/ppermute | solution.py:49
  6.4 1.4 %collective-permute-start.3 = (bf16[1,256,512]{2,1,0:T(8,128)(2,1)S(1)}, bf16[1,256,512]{2,1,0:T(8,128)(2,1)}, u32[]{:S(2)}, u32[]{:S(2)}) collective-permute-start(bf16[1,256,512]{2,1,0:T(8,128)(2,1)S(1)} %get-tuple-element.31), channel_id=1, source_target_pairs={{0,192},{1,65},{2,194},{3,67},{4,196},{5,69},{6,198},{7,71},{8,200... | collective-permute-start | bytes 786440 | tf_op jit(solution)/shard_map/ppermute | solution.py:49
  7.8 1.4 %collective-permute-start.4 = (bf16[1,256,512]{2,1,0:T(8,128)(2,1)S(1)}, bf16[1,256,512]{2,1,0:T(8,128)(2,1)S(1)}, u32[]{:S(2)}, u32[]{:S(2)}) collective-permute-start(bf16[1,256,512]{2,1,0:T(8,128)(2,1)S(1)} %get-tuple-element.31), channel_id=1, source_target_pairs={{0,64},{1,193},{2,66},{3,195},{4,68},{5,197},{6,70},{7,199},{8,72}... | collective-permute-start | bytes 786440 | tf_op jit(solution)/shard_map/ppermute | solution.py:49
  9.2 0.7 copy.30
  10.0 0.7 copy.26
  10.7 0.1 fusion.22
  10.9 1.3 %select_reduce_fusion = (s32[80]{0:T(128)}, s32[80,1]{1,0:T(8,128)}) fusion(s32[]{:T(128)S(6)} %select_n.394, s32[80,1]{1,0:T(8,128)S(1)} %copy.30), kind=kLoop, calls=%fused_computation.40 | loop fusion | flops 3920 | bytes 964 | tf_op jit(solution)/shard_map/gather | solution.py:251
  12.2 0.7 broadcast_compare_fusion
  12.9 0.1 reduce-window.17
  13.0 0.1 reduce-window.16
  13.2 0.0 collective-permute-done.1
  13.2 1.7 %collective-permute-start.2 = (bf16[1,256,512]{2,1,0:T(8,128)(2,1)S(1)}, bf16[1,256,512]{2,1,0:T(8,128)(2,1)S(1)}, u32[]{:S(2)}, u32[]{:S(2)}) collective-permute-start(bf16[1,256,512]{2,1,0:T(8,128)(2,1)S(1)} %collective-permute-done.1), channel_id=1, source_target_pairs={{0,16},{1,49},{2,18},{3,51},{4,20},{5,53},{6,22},{7,55},{8,24},{9,... | collective-permute-start | bytes 786440 | tf_op jit(solution)/shard_map/ppermute | solution.py:49
  14.9 0.1 add_reduce_fusion
  15.0 0.4 collective-permute-done.4
  15.4 2.8 %collective-permute-start.5 = (bf16[1,256,512]{2,1,0:T(8,128)(2,1)S(1)}, bf16[1,256,512]{2,1,0:T(8,128)(2,1)S(1)}, u32[]{:S(2)}, u32[]{:S(2)}) collective-permute-start(bf16[1,256,512]{2,1,0:T(8,128)(2,1)S(1)} %collective-permute-done.4), channel_id=1, source_target_pairs={{0,64},{1,193},{2,66},{3,195},{4,68},{5,197},{6,70},{7,199},{8,72}... | collective-permute-start | bytes 786440 | tf_op jit(solution)/shard_map/ppermute | solution.py:49
  18.2 1.0 constant_dynamic-update-slice_fusion.6
  19.1 0.0 collective-permute-done.2
  19.2 2.6 %collective-permute-start.6 = (bf16[4,256,512]{2,1,0:T(8,128)(2,1)S(1)}, bf16[4,256,512]{2,1,0:T(8,128)(2,1)S(1)}, u32[]{:S(2)}, u32[]{:S(2)}) collective-permute-start(bf16[4,256,512]{2,1,0:T(8,128)(2,1)S(1)} %constant_dynamic-update-slice_fusion.first_line.refs_0_), channel_id=1, source_target_pairs={{0,64},{1,193},{2,66},{3,195},{4,68},{5,197},{6,70},{7,199},{8,72}... | collective-permute-start | bytes 3145736 | tf_op jit(solution)/shard_map/ppermute | solution.py:49
  21.8 2.8 %collective-permute-start.7 = (bf16[4,256,512]{2,1,0:T(8,128)(2,1)S(1)}, bf16[4,256,512]{2,1,0:T(8,128)(2,1)S(1)}, u32[]{:S(2)}, u32[]{:S(2)}) collective-permute-start(bf16[4,256,512]{2,1,0:T(8,128)(2,1)S(1)} %constant_dynamic-update-slice_fusion.4.second_line.refs_2_), channel_id=1, source_target_pairs={{0,16},{1,49},{2,18},{3,51},{4,20},{5,53},{6,22},{7,55},{8,24},{9,... | collective-permute-start | bytes 3145736 | tf_op jit(solution)/shard_map/ppermute | solution.py:49
  24.6 0.9 compare_reduce_fusion
  25.5 0.6 fusion.28
  26.1 0.6 convert_reduce_fusion
  26.8 0.2 select_reduce_fusion.4
  27.0 0.6 compare_select_fusion.9.target_slot
  27.5 4.7 %shard_map.96 = (bf16[80,256,256]{2,1,0:T(8,128)(2,1)S(1)}, f32[8,128]{1,0:T(8,128)}) custom-call(bf16[80,256,256]{2,1,0:T(8,128)(2,1)} %bitcast.33, bf16[4,256,512]{2,1,0:T(8,128)(2,1)S(1)} %constant_dynamic-update-slice_fusion.first_line.refs_0_, bf16[4,256,512]{2,1,0:T(8,128)(2,1)S(1)} %constant_dynamic-update-slice_fusion.4.second_line.refs_2_), custom_call_target="tpu_custom_call" | custom-call | tf_op jit(solution)/shard_map/pallas_call | solution.py:100
  32.2 0.1 collective-permute-start.9
  32.3 0.1 collective-permute-start.11
  32.4 1.1 %collective-permute-done.6.refs_1_ = bf16[4,256,512]{2,1,0:T(8,128)(2,1)S(1)} collective-permute-done((bf16[4,256,512]{2,1,0:T(8,128)(2,1)S(1)}, bf16[4,256,512]{2,1,0:T(8,128)(2,1)S(1)}, u32[]{:S(2)}, u32[]{:S(2)}) %collective-permute-start.6) | collective-permute-done | bytes 1048608 | tf_op jit(solution)/shard_map/ppermute | solution.py:49
  33.5 3.4 %collective-permute-start.10 = (bf16[4,256,512]{2,1,0:T(8,128)(2,1)S(1)}, bf16[4,256,512]{2,1,0:T(8,128)(2,1)S(1)}, u32[]{:S(2)}, u32[]{:S(2)}) collective-permute-start(bf16[4,256,512]{2,1,0:T(8,128)(2,1)S(1)} %collective-permute-done.6.refs_1_), channel_id=1, source_target_pairs={{0,64},{1,193},{2,66},{3,195},{4,68},{5,197},{6,70},{7,199},{8,72}... | collective-permute-start | bytes 3145736 | tf_op jit(solution)/shard_map/ppermute | solution.py:49
  36.9 0.0 collective-permute-done.7.refs_3_
  36.9 2.8 %collective-permute-start.12 = (bf16[4,256,512]{2,1,0:T(8,128)(2,1)S(1)}, bf16[4,256,512]{2,1,0:T(8,128)(2,1)S(1)}, u32[]{:S(2)}, u32[]{:S(2)}) collective-permute-start(bf16[4,256,512]{2,1,0:T(8,128)(2,1)S(1)} %collective-permute-done.7.refs_3_), channel_id=1, source_target_pairs={{0,16},{1,49},{2,18},{3,51},{4,20},{5,53},{6,22},{7,55},{8,24},{9,... | collective-permute-start | bytes 3145736 | tf_op jit(solution)/shard_map/ppermute | solution.py:49
  39.8 7.5 %shard_map.97 = (f32[17,256,512]{2,1,0:T(8,128)S(1)}, bf16[8,256,512]{2,1,0:T(8,128)(2,1)}) custom-call(s32[1]{0:T(128)} %bitcast.4.count, s32[80]{0:T(128)S(1)} %get-tuple-element.64.chosen, s32[80]{0:T(128)S(1)} %get-tuple-element.60.source_slot, s32[80]{0:T(128)S(1)} %compare_select_fusion.9.target_slot, ...), custom_call_target="tpu_custom_call" | custom-call | flops 5368709120 | bytes 10485760 | tf_op jit(solution)/shard_map/pallas_call | solution.py:137
  47.3 7.0 %collective-permute-start.8 = (bf16[8,256,512]{2,1,0:T(8,128)(2,1)}, bf16[8,256,512]{2,1,0:T(8,128)(2,1)S(1)}, u32[]{:S(2)}, u32[]{:S(2)}) collective-permute-start(bf16[8,256,512]{2,1,0:T(8,128)(2,1)} %get-tuple-element.34), channel_id=1, source_target_pairs={{0,1},{1,0},{2,3},{3,2},{4,5},{5,4},{6,7},{7,6},{8,9},{9,8},{10,11... | collective-permute-start | bytes 6291464 | tf_op jit(solution)/shard_map/ppermute | solution.py:53
  54.3 0.6 compare_select_fusion.7.target_slot
  54.9 0.0 collective-permute-done.11.refs_2_
  54.9 2.9 %collective-permute-done.10.refs_1_ = bf16[4,256,512]{2,1,0:T(8,128)(2,1)S(1)} collective-permute-done((bf16[4,256,512]{2,1,0:T(8,128)(2,1)S(1)}, bf16[4,256,512]{2,1,0:T(8,128)(2,1)S(1)}, u32[]{:S(2)}, u32[]{:S(2)}) %collective-permute-start.10) | collective-permute-done | bytes 1048608 | tf_op jit(solution)/shard_map/ppermute | solution.py:49
  57.8 2.4 %collective-permute-done.12.refs_3_ = bf16[4,256,512]{2,1,0:T(8,128)(2,1)S(1)} collective-permute-done((bf16[4,256,512]{2,1,0:T(8,128)(2,1)S(1)}, bf16[4,256,512]{2,1,0:T(8,128)(2,1)S(1)}, u32[]{:S(2)}, u32[]{:S(2)}) %collective-permute-start.12) | collective-permute-done | bytes 1048608 | tf_op jit(solution)/shard_map/ppermute | solution.py:49
  60.2 4.3 %shard_map.102 = (f32[17,256,256]{2,1,0:T(8,128)S(1)}, bf16[8,256,256]{2,1,0:T(8,128)(2,1)S(1)}) custom-call(s32[1]{0:T(128)} %bitcast.9.count, s32[80]{0:T(128)S(1)} %get-tuple-element.61.chosen, s32[80]{0:T(128)S(1)} %get-tuple-element.62.source_slot, s32[80]{0:T(128)S(1)} %compare_select_fusion.7.target_slot, ...), custom_call_target="tpu_custom_call" | custom-call | flops 2684354560 | bytes 10485760 | tf_op jit(solution)/shard_map/pallas_call | solution.py:137
  64.5 4.1 %collective-permute-start.19 = (bf16[8,256,256]{2,1,0:T(8,128)(2,1)S(1)}, bf16[8,256,256]{2,1,0:T(8,128)(2,1)S(1)}, u32[]{:S(2)}, u32[]{:S(2)}) collective-permute-start(bf16[8,256,256]{2,1,0:T(8,128)(2,1)S(1)} %get-tuple-element.48), channel_id=1, source_target_pairs={{0,1},{1,0},{2,3},{3,2},{4,5},{5,4},{6,7},{7,6},{8,9},{9,8},{10,11... | collective-permute-start | bytes 3145736 | tf_op jit(solution)/shard_map/ppermute | solution.py:53
  68.6 4.3 %shard_map.99 = (f32[17,256,256]{2,1,0:T(8,128)S(1)}, bf16[8,256,256]{2,1,0:T(8,128)(2,1)S(1)}) custom-call(s32[1]{0:T(128)} %bitcast.9.count, s32[80]{0:T(128)S(1)} %get-tuple-element.61.chosen, s32[80]{0:T(128)S(1)} %get-tuple-element.62.source_slot, s32[80]{0:T(128)S(1)} %compare_select_fusion.7.target_slot, ...), custom_call_target="tpu_custom_call" | custom-call | flops 2684354560 | bytes 10485760 | tf_op jit(solution)/shard_map/pallas_call | solution.py:137
  72.9 0.1 collective-permute-start.13
  73.0 0.0 collective-permute-done.8.other
  73.0 0.3 shard_map.98.base
  73.3 0.4 shard_map.103
  73.7 5.6 %collective-permute-start.20 = (bf16[2,256,256]{2,1,0:T(8,128)(2,1)S(1)}, bf16[2,256,256]{2,1,0:T(8,128)(2,1)S(1)}, u32[]{:S(2)}, u32[]{:S(2)}) collective-permute-start(bf16[2,256,256]{2,1,0:T(8,128)(2,1)S(1)} %get-tuple-element.50), channel_id=1, source_target_pairs={{0,2},{1,15},{2,4},{3,1},{4,6},{5,3},{6,8},{7,5},{8,10},{9,7},{10,... | collective-permute-start | bytes 786440 | tf_op jit(solution)/shard_map/ppermute | solution.py:49
  79.3 2.7 %collective-permute-start.22 = (bf16[256,256]{1,0:T(8,128)(2,1)S(1)}, bf16[256,256]{1,0:T(8,128)(2,1)S(1)}, u32[]{:S(2)}, u32[]{:S(2)}) collective-permute-start(bf16[256,256]{1,0:T(8,128)(2,1)S(1)} %get-tuple-element.52), channel_id=1, source_target_pairs={{0,4},{1,13},{2,6},{3,15},{4,8},{5,1},{6,10},{7,3},{8,12},{9,5},{1... | collective-permute-start | bytes 393224 | tf_op jit(solution)/shard_map/ppermute | solution.py:49
  82.1 0.3 shard_map.100
  82.4 0.2 collective-permute-start.14
  82.6 1.4 %collective-permute-start.15 = (bf16[2,256,256]{2,1,0:T(8,128)(2,1)S(1)}, bf16[2,256,256]{2,1,0:T(8,128)(2,1)S(1)}, u32[]{:S(2)}, u32[]{:S(2)}) collective-permute-start(bf16[2,256,256]{2,1,0:T(8,128)(2,1)S(1)} %get-tuple-element.42), channel_id=1, source_target_pairs={{0,14},{1,3},{2,0},{3,5},{4,2},{5,7},{6,4},{7,9},{8,6},{9,11},{10,... | collective-permute-start | bytes 786440 | tf_op jit(solution)/shard_map/ppermute | solution.py:49
  84.0 4.7 %collective-permute-done.22.far = bf16[256,256]{1,0:T(8,128)(2,1)S(1)} collective-permute-done((bf16[256,256]{1,0:T(8,128)(2,1)S(1)}, bf16[256,256]{1,0:T(8,128)(2,1)S(1)}, u32[]{:S(2)}, u32[]{:S(2)}) %collective-permute-start.22) | collective-permute-done | bytes 131104 | tf_op jit(solution)/shard_map/ppermute | solution.py:49
  88.6 4.0 %collective-permute-start.16 = (bf16[256,256]{1,0:T(8,128)(2,1)S(1)}, bf16[256,256]{1,0:T(8,128)(2,1)S(1)}, u32[]{:S(2)}, u32[]{:S(2)}) collective-permute-start(bf16[256,256]{1,0:T(8,128)(2,1)S(1)} %get-tuple-element.43), channel_id=1, source_target_pairs={{0,4},{1,13},{2,6},{3,15},{4,8},{5,1},{6,10},{7,3},{8,12},{9,5},{1... | collective-permute-start | bytes 393224 | tf_op jit(solution)/shard_map/ppermute | solution.py:49
  92.7 0.1 shard_map.104
  92.8 0.1 collective-permute-start.23
  92.9 2.4 %collective-permute-start.24 = (bf16[256,256]{1,0:T(8,128)(2,1)S(1)}, bf16[256,256]{1,0:T(8,128)(2,1)S(1)}, u32[]{:S(2)}, u32[]{:S(2)}) collective-permute-start(bf16[256,256]{1,0:T(8,128)(2,1)S(1)} %get-tuple-element.55), channel_id=1, source_target_pairs={{0,12},{1,5},{2,14},{3,7},{4,0},{5,9},{6,2},{7,11},{8,4},{9,13},{1... | collective-permute-start | bytes 393224 | tf_op jit(solution)/shard_map/ppermute | solution.py:49
  95.2 4.3 %collective-permute-done.16.far = bf16[256,256]{1,0:T(8,128)(2,1)S(1)} collective-permute-done((bf16[256,256]{1,0:T(8,128)(2,1)S(1)}, bf16[256,256]{1,0:T(8,128)(2,1)S(1)}, u32[]{:S(2)}, u32[]{:S(2)}) %collective-permute-start.16) | collective-permute-done | bytes 131104 | tf_op jit(solution)/shard_map/ppermute | solution.py:49
  99.6 0.1 shard_map.101
  99.7 4.1 %collective-permute-start.17 = (bf16[256,256]{1,0:T(8,128)(2,1)S(1)}, bf16[256,256]{1,0:T(8,128)(2,1)S(1)}, u32[]{:S(2)}, u32[]{:S(2)}) collective-permute-start(bf16[256,256]{1,0:T(8,128)(2,1)S(1)} %get-tuple-element.45), channel_id=1, source_target_pairs={{0,4},{1,13},{2,6},{3,15},{4,8},{5,1},{6,10},{7,3},{8,12},{9,5},{1... | collective-permute-start | bytes 393224 | tf_op jit(solution)/shard_map/ppermute | solution.py:49
  103.9 0.2 shard_map.105.refs_0_
  104.1 3.5 %collective-permute-done.17.fwd = bf16[256,256]{1,0:T(8,128)(2,1)S(1)} collective-permute-done((bf16[256,256]{1,0:T(8,128)(2,1)S(1)}, bf16[256,256]{1,0:T(8,128)(2,1)S(1)}, u32[]{:S(2)}, u32[]{:S(2)}) %collective-permute-start.17) | collective-permute-done | bytes 131104 | tf_op jit(solution)/shard_map/ppermute | solution.py:49
  107.6 2.4 %collective-permute-done.18.bwd = bf16[256,256]{1,0:T(8,128)(2,1)S(1)} collective-permute-done((bf16[256,256]{1,0:T(8,128)(2,1)S(1)}, bf16[256,256]{1,0:T(8,128)(2,1)S(1)}, u32[]{:S(2)}, u32[]{:S(2)}) %collective-permute-start.18) | collective-permute-done | bytes 131104 | tf_op jit(solution)/shard_map/ppermute | solution.py:49
  110.0 0.9 shard_map.106
  (28 shorter events, 0.2 us)
Async XLA Ops:
  0.6 24.9 %copy-start.2 = (s32[1,1,80]{2,1,0:T(1,128)S(1)}, s32[1,1,80]{2,1,0:T(1,128)}, u32[]{:S(2)}) copy-start(s32[1,1,80]{2,1,0:T(1,128)} %param.13) | copy-start | bytes 964
  2.9 15.2 %collective-permute-start = (bf16[1,256,512]{2,1,0:T(8,128)(2,1)S(1)}, bf16[1,256,512]{2,1,0:T(8,128)(2,1)S(1)}, u32[]{:S(2)}, u32[]{:S(2)}) collective-permute-start(bf16[1,256,512]{2,1,0:T(8,128)(2,1)S(1)} %get-tuple-element.30), channel_id=1, source_target_pairs={{0,48},{1,17},{2,50},{3,19},{4,52},{5,21},{6,54},{7,23},{8,56},{9,... | collective-permute-start | bytes 786440 | tf_op jit(solution)/shard_map/ppermute | solution.py:49
  5.0 8.1 %collective-permute-start.1 = (bf16[1,256,512]{2,1,0:T(8,128)(2,1)S(1)}, bf16[1,256,512]{2,1,0:T(8,128)(2,1)S(1)}, u32[]{:S(2)}, u32[]{:S(2)}) collective-permute-start(bf16[1,256,512]{2,1,0:T(8,128)(2,1)S(1)} %get-tuple-element.30), channel_id=1, source_target_pairs={{0,16},{1,49},{2,18},{3,51},{4,20},{5,53},{6,22},{7,55},{8,24},{9,... | collective-permute-start | bytes 786440 | tf_op jit(solution)/shard_map/ppermute | solution.py:49
  6.4 11.8 %collective-permute-start.3 = (bf16[1,256,512]{2,1,0:T(8,128)(2,1)S(1)}, bf16[1,256,512]{2,1,0:T(8,128)(2,1)}, u32[]{:S(2)}, u32[]{:S(2)}) collective-permute-start(bf16[1,256,512]{2,1,0:T(8,128)(2,1)S(1)} %get-tuple-element.31), channel_id=1, source_target_pairs={{0,192},{1,65},{2,194},{3,67},{4,196},{5,69},{6,198},{7,71},{8,200... | collective-permute-start | bytes 786440 | tf_op jit(solution)/shard_map/ppermute | solution.py:49
  7.8 7.5 %collective-permute-start.4 = (bf16[1,256,512]{2,1,0:T(8,128)(2,1)S(1)}, bf16[1,256,512]{2,1,0:T(8,128)(2,1)S(1)}, u32[]{:S(2)}, u32[]{:S(2)}) collective-permute-start(bf16[1,256,512]{2,1,0:T(8,128)(2,1)S(1)} %get-tuple-element.31), channel_id=1, source_target_pairs={{0,64},{1,193},{2,66},{3,195},{4,68},{5,197},{6,70},{7,199},{8,72}... | collective-permute-start | bytes 786440 | tf_op jit(solution)/shard_map/ppermute | solution.py:49
  13.2 6.0 %collective-permute-start.2 = (bf16[1,256,512]{2,1,0:T(8,128)(2,1)S(1)}, bf16[1,256,512]{2,1,0:T(8,128)(2,1)S(1)}, u32[]{:S(2)}, u32[]{:S(2)}) collective-permute-start(bf16[1,256,512]{2,1,0:T(8,128)(2,1)S(1)} %collective-permute-done.1), channel_id=1, source_target_pairs={{0,16},{1,49},{2,18},{3,51},{4,20},{5,53},{6,22},{7,55},{8,24},{9,... | collective-permute-start | bytes 786440 | tf_op jit(solution)/shard_map/ppermute | solution.py:49
  15.4 6.4 %collective-permute-start.5 = (bf16[1,256,512]{2,1,0:T(8,128)(2,1)S(1)}, bf16[1,256,512]{2,1,0:T(8,128)(2,1)S(1)}, u32[]{:S(2)}, u32[]{:S(2)}) collective-permute-start(bf16[1,256,512]{2,1,0:T(8,128)(2,1)S(1)} %collective-permute-done.4), channel_id=1, source_target_pairs={{0,64},{1,193},{2,66},{3,195},{4,68},{5,197},{6,70},{7,199},{8,72}... | collective-permute-start | bytes 786440 | tf_op jit(solution)/shard_map/ppermute | solution.py:49
  19.2 14.3 %collective-permute-start.6 = (bf16[4,256,512]{2,1,0:T(8,128)(2,1)S(1)}, bf16[4,256,512]{2,1,0:T(8,128)(2,1)S(1)}, u32[]{:S(2)}, u32[]{:S(2)}) collective-permute-start(bf16[4,256,512]{2,1,0:T(8,128)(2,1)S(1)} %constant_dynamic-update-slice_fusion.first_line.refs_0_), channel_id=1, source_target_pairs={{0,64},{1,193},{2,66},{3,195},{4,68},{5,197},{6,70},{7,199},{8,72}... | collective-permute-start | bytes 3145736 | tf_op jit(solution)/shard_map/ppermute | solution.py:49
  21.8 15.1 %collective-permute-start.7 = (bf16[4,256,512]{2,1,0:T(8,128)(2,1)S(1)}, bf16[4,256,512]{2,1,0:T(8,128)(2,1)S(1)}, u32[]{:S(2)}, u32[]{:S(2)}) collective-permute-start(bf16[4,256,512]{2,1,0:T(8,128)(2,1)S(1)} %constant_dynamic-update-slice_fusion.4.second_line.refs_2_), channel_id=1, source_target_pairs={{0,16},{1,49},{2,18},{3,51},{4,20},{5,53},{6,22},{7,55},{8,24},{9,... | collective-permute-start | bytes 3145736 | tf_op jit(solution)/shard_map/ppermute | solution.py:49
  32.2 22.7 %collective-permute-start.9 = (bf16[4,256,512]{2,1,0:T(8,128)(2,1)S(1)}, bf16[4,256,512]{2,1,0:T(8,128)(2,1)S(1)}, u32[]{:S(2)}, u32[]{:S(2)}) collective-permute-start(bf16[4,256,512]{2,1,0:T(8,128)(2,1)S(1)} %constant_dynamic-update-slice_fusion.first_line.refs_0_), channel_id=1, source_target_pairs={{0,192},{1,65},{2,194},{3,67},{4,196},{5,69},{6,198},{7,71},{8,200... | collective-permute-start | bytes 3145736 | tf_op jit(solution)/shard_map/ppermute | solution.py:49
  32.3 22.6 %collective-permute-start.11 = (bf16[4,256,512]{2,1,0:T(8,128)(2,1)S(1)}, bf16[4,256,512]{2,1,0:T(8,128)(2,1)S(1)}, u32[]{:S(2)}, u32[]{:S(2)}) collective-permute-start(bf16[4,256,512]{2,1,0:T(8,128)(2,1)S(1)} %constant_dynamic-update-slice_fusion.4.second_line.refs_2_), channel_id=1, source_target_pairs={{0,48},{1,17},{2,50},{3,19},{4,52},{5,21},{6,54},{7,23},{8,56},{9,... | collective-permute-start | bytes 3145736 | tf_op jit(solution)/shard_map/ppermute | solution.py:49
  33.5 24.3 %collective-permute-start.10 = (bf16[4,256,512]{2,1,0:T(8,128)(2,1)S(1)}, bf16[4,256,512]{2,1,0:T(8,128)(2,1)S(1)}, u32[]{:S(2)}, u32[]{:S(2)}) collective-permute-start(bf16[4,256,512]{2,1,0:T(8,128)(2,1)S(1)} %collective-permute-done.6.refs_1_), channel_id=1, source_target_pairs={{0,64},{1,193},{2,66},{3,195},{4,68},{5,197},{6,70},{7,199},{8,72}... | collective-permute-start | bytes 3145736 | tf_op jit(solution)/shard_map/ppermute | solution.py:49
  36.9 23.2 %collective-permute-start.12 = (bf16[4,256,512]{2,1,0:T(8,128)(2,1)S(1)}, bf16[4,256,512]{2,1,0:T(8,128)(2,1)S(1)}, u32[]{:S(2)}, u32[]{:S(2)}) collective-permute-start(bf16[4,256,512]{2,1,0:T(8,128)(2,1)S(1)} %collective-permute-done.7.refs_3_), channel_id=1, source_target_pairs={{0,16},{1,49},{2,18},{3,51},{4,20},{5,53},{6,22},{7,55},{8,24},{9,... | collective-permute-start | bytes 3145736 | tf_op jit(solution)/shard_map/ppermute | solution.py:49
  47.3 25.7 %collective-permute-start.8 = (bf16[8,256,512]{2,1,0:T(8,128)(2,1)}, bf16[8,256,512]{2,1,0:T(8,128)(2,1)S(1)}, u32[]{:S(2)}, u32[]{:S(2)}) collective-permute-start(bf16[8,256,512]{2,1,0:T(8,128)(2,1)} %get-tuple-element.34), channel_id=1, source_target_pairs={{0,1},{1,0},{2,3},{3,2},{4,5},{5,4},{6,7},{7,6},{8,9},{9,8},{10,11... | collective-permute-start | bytes 6291464 | tf_op jit(solution)/shard_map/ppermute | solution.py:53
  64.5 8.9 %collective-permute-start.19 = (bf16[8,256,256]{2,1,0:T(8,128)(2,1)S(1)}, bf16[8,256,256]{2,1,0:T(8,128)(2,1)S(1)}, u32[]{:S(2)}, u32[]{:S(2)}) collective-permute-start(bf16[8,256,256]{2,1,0:T(8,128)(2,1)S(1)} %get-tuple-element.48), channel_id=1, source_target_pairs={{0,1},{1,0},{2,3},{3,2},{4,5},{5,4},{6,7},{7,6},{8,9},{9,8},{10,11... | collective-permute-start | bytes 3145736 | tf_op jit(solution)/shard_map/ppermute | solution.py:53
  72.9 9.2 %collective-permute-start.13 = (bf16[8,256,256]{2,1,0:T(8,128)(2,1)S(1)}, bf16[8,256,256]{2,1,0:T(8,128)(2,1)S(1)}, u32[]{:S(2)}, u32[]{:S(2)}) collective-permute-start(bf16[8,256,256]{2,1,0:T(8,128)(2,1)S(1)} %get-tuple-element.39), channel_id=1, source_target_pairs={{0,1},{1,0},{2,3},{3,2},{4,5},{5,4},{6,7},{7,6},{8,9},{9,8},{10,11... | collective-permute-start | bytes 3145736 | tf_op jit(solution)/shard_map/ppermute | solution.py:53
  73.7 19.0 %collective-permute-start.20 = (bf16[2,256,256]{2,1,0:T(8,128)(2,1)S(1)}, bf16[2,256,256]{2,1,0:T(8,128)(2,1)S(1)}, u32[]{:S(2)}, u32[]{:S(2)}) collective-permute-start(bf16[2,256,256]{2,1,0:T(8,128)(2,1)S(1)} %get-tuple-element.50), channel_id=1, source_target_pairs={{0,2},{1,15},{2,4},{3,1},{4,6},{5,3},{6,8},{7,5},{8,10},{9,7},{10,... | collective-permute-start | bytes 786440 | tf_op jit(solution)/shard_map/ppermute | solution.py:49
  79.3 13.3 %collective-permute-start.21 = (bf16[2,256,256]{2,1,0:T(8,128)(2,1)S(1)}, bf16[2,256,256]{2,1,0:T(8,128)(2,1)S(1)}, u32[]{:S(2)}, u32[]{:S(2)}) collective-permute-start(bf16[2,256,256]{2,1,0:T(8,128)(2,1)S(1)} %get-tuple-element.51), channel_id=1, source_target_pairs={{0,14},{1,3},{2,0},{3,5},{4,2},{5,7},{6,4},{7,9},{8,6},{9,11},{10,... | collective-permute-start | bytes 786440 | tf_op jit(solution)/shard_map/ppermute | solution.py:49
  79.3 9.3 %collective-permute-start.22 = (bf16[256,256]{1,0:T(8,128)(2,1)S(1)}, bf16[256,256]{1,0:T(8,128)(2,1)S(1)}, u32[]{:S(2)}, u32[]{:S(2)}) collective-permute-start(bf16[256,256]{1,0:T(8,128)(2,1)S(1)} %get-tuple-element.52), channel_id=1, source_target_pairs={{0,4},{1,13},{2,6},{3,15},{4,8},{5,1},{6,10},{7,3},{8,12},{9,5},{1... | collective-permute-start | bytes 393224 | tf_op jit(solution)/shard_map/ppermute | solution.py:49
  82.1 21.7 %copy-start = (bf16[1,1,1,256,512]{4,3,2,1,0:T(8,128)(2,1)S(1)}, bf16[1,1,1,256,512]{4,3,2,1,0:T(8,128)(2,1)}, u32[]{:S(2)}) copy-start(bf16[1,1,1,256,512]{4,3,2,1,0:T(8,128)(2,1)} %param.10) | copy-start | bytes 786436
  82.1 21.8 %copy-start.1 = (bf16[1,1,1,256,256]{4,3,2,1,0:T(8,128)(2,1)S(1)}, bf16[1,1,1,256,256]{4,3,2,1,0:T(8,128)(2,1)}, u32[]{:S(2)}) copy-start(bf16[1,1,1,256,256]{4,3,2,1,0:T(8,128)(2,1)} %param.11) | copy-start | bytes 393220
  82.4 17.1 %collective-permute-start.14 = (bf16[2,256,256]{2,1,0:T(8,128)(2,1)S(1)}, bf16[2,256,256]{2,1,0:T(8,128)(2,1)S(1)}, u32[]{:S(2)}, u32[]{:S(2)}) collective-permute-start(bf16[2,256,256]{2,1,0:T(8,128)(2,1)S(1)} %get-tuple-element.41), channel_id=1, source_target_pairs={{0,2},{1,15},{2,4},{3,1},{4,6},{5,3},{6,8},{7,5},{8,10},{9,7},{10,... | collective-permute-start | bytes 786440 | tf_op jit(solution)/shard_map/ppermute | solution.py:49
  82.6 17.0 %collective-permute-start.15 = (bf16[2,256,256]{2,1,0:T(8,128)(2,1)S(1)}, bf16[2,256,256]{2,1,0:T(8,128)(2,1)S(1)}, u32[]{:S(2)}, u32[]{:S(2)}) collective-permute-start(bf16[2,256,256]{2,1,0:T(8,128)(2,1)S(1)} %get-tuple-element.42), channel_id=1, source_target_pairs={{0,14},{1,3},{2,0},{3,5},{4,2},{5,7},{6,4},{7,9},{8,6},{9,11},{10,... | collective-permute-start | bytes 786440 | tf_op jit(solution)/shard_map/ppermute | solution.py:49
  88.6 10.9 %collective-permute-start.16 = (bf16[256,256]{1,0:T(8,128)(2,1)S(1)}, bf16[256,256]{1,0:T(8,128)(2,1)S(1)}, u32[]{:S(2)}, u32[]{:S(2)}) collective-permute-start(bf16[256,256]{1,0:T(8,128)(2,1)S(1)} %get-tuple-element.43), channel_id=1, source_target_pairs={{0,4},{1,13},{2,6},{3,15},{4,8},{5,1},{6,10},{7,3},{8,12},{9,5},{1... | collective-permute-start | bytes 393224 | tf_op jit(solution)/shard_map/ppermute | solution.py:49
  92.8 11.0 %collective-permute-start.23 = (bf16[256,256]{1,0:T(8,128)(2,1)S(1)}, bf16[256,256]{1,0:T(8,128)(2,1)S(1)}, u32[]{:S(2)}, u32[]{:S(2)}) collective-permute-start(bf16[256,256]{1,0:T(8,128)(2,1)S(1)} %get-tuple-element.54), channel_id=1, source_target_pairs={{0,4},{1,13},{2,6},{3,15},{4,8},{5,1},{6,10},{7,3},{8,12},{9,5},{1... | collective-permute-start | bytes 393224 | tf_op jit(solution)/shard_map/ppermute | solution.py:49
  92.9 11.0 %collective-permute-start.24 = (bf16[256,256]{1,0:T(8,128)(2,1)S(1)}, bf16[256,256]{1,0:T(8,128)(2,1)S(1)}, u32[]{:S(2)}, u32[]{:S(2)}) collective-permute-start(bf16[256,256]{1,0:T(8,128)(2,1)S(1)} %get-tuple-element.55), channel_id=1, source_target_pairs={{0,12},{1,5},{2,14},{3,7},{4,0},{5,9},{6,2},{7,11},{8,4},{9,13},{1... | collective-permute-start | bytes 393224 | tf_op jit(solution)/shard_map/ppermute | solution.py:49
  99.7 7.9 %collective-permute-start.17 = (bf16[256,256]{1,0:T(8,128)(2,1)S(1)}, bf16[256,256]{1,0:T(8,128)(2,1)S(1)}, u32[]{:S(2)}, u32[]{:S(2)}) collective-permute-start(bf16[256,256]{1,0:T(8,128)(2,1)S(1)} %get-tuple-element.45), channel_id=1, source_target_pairs={{0,4},{1,13},{2,6},{3,15},{4,8},{5,1},{6,10},{7,3},{8,12},{9,5},{1... | collective-permute-start | bytes 393224 | tf_op jit(solution)/shard_map/ppermute | solution.py:49
  103.8 6.2 %collective-permute-start.18 = (bf16[256,256]{1,0:T(8,128)(2,1)S(1)}, bf16[256,256]{1,0:T(8,128)(2,1)S(1)}, u32[]{:S(2)}, u32[]{:S(2)}) collective-permute-start(bf16[256,256]{1,0:T(8,128)(2,1)S(1)} %get-tuple-element.46), channel_id=1, source_target_pairs={{0,12},{1,5},{2,14},{3,7},{4,0},{5,9},{6,2},{7,11},{8,4},{9,13},{1... | collective-permute-start | bytes 393224 | tf_op jit(solution)/shard_map/ppermute | solution.py:49

commit v4 on v3

v4 whole, which is shorter than its diff:
```python
import functools

import jax
import jax.numpy as jnp
from jax import lax
from jax.experimental import pallas as pl
from jax.experimental.pallas import tpu as pltpu
from jax.sharding import PartitionSpec as P

PARTS = 2
STEP = 16
BOTH = ("row", "col")
MIB = 1024 * 1024
F32 = jnp.float32
BF16 = jnp.bfloat16


def whole(memory=pltpu.VMEM):
    return pl.BlockSpec(memory_space=memory)


def shape(dims, dtype=BF16):
    return jax.ShapeDtypeStruct(dims, dtype)


def params(mib=16):
    return pltpu.CompilerParams(vmem_limit_bytes=mib * MIB)


def ring_pairs(axis, steps):
    pairs = []
    for y in range(4):
        for x in range(4):
            for z in range(8):
                for core in range(2):
                    way = steps if core == 0 else -steps
                    to_y, to_x, to_z = y, x, z
                    if axis == "x":
                        to_x = (x + way) % 4
                    elif axis == "y":
                        to_y = (y + way) % 4
                    else:
                        to_z = (z + way) % 8
                    pairs.append(((y * 4 + x) * 16 + z * 2 + core, (to_y * 4 + to_x) * 16 + to_z * 2 + core))
    return pairs


def move(value, axis, steps):
    return lax.ppermute(value, BOTH, ring_pairs(axis, steps))


def swap_cores(value):
    return lax.ppermute(value, "col", [(i, i ^ 1) for i in range(16)])


def solve_one_kernel(rhs_hbm, inverse_hbm, solved, rhs, inverse, sems):
    copies = []
    for q in range(2):
        copies.append(pltpu.make_async_copy(rhs_hbm.at[q], rhs.at[q], sems.at[2 * q]))
        copies.append(pltpu.make_async_copy(inverse_hbm.at[q], inverse.at[q], sems.at[2 * q + 1]))
    for copy in copies:
        copy.start()
    for q in range(2):
        copies[2 * q].wait()
        copies[2 * q + 1].wait()
        solved[q] = jnp.dot(inverse[q], rhs[q], preferred_element_type=F32).astype(BF16)


def solve_one(rhs, inverse):
    return pl.pallas_call(
        solve_one_kernel,
        out_shape=shape(rhs.shape),
        in_specs=[whole(pltpu.HBM)] * 2,
        out_specs=whole(),
        scratch_shapes=[
            pltpu.VMEM(rhs.shape, BF16),
            pltpu.VMEM(inverse.shape, BF16),
            pltpu.SemaphoreType.DMA((4,)),
        ],
        compiler_params=params(),
    )(*[pltpu.with_memory_space_constraint(value, pltpu.HBM) for value in (rhs, inverse)])


def stage_kernel(blocks_hbm, first_line, second_line, blocks, first_same, second_same, sems):
    size = blocks.shape[0] // STEP
    copies = [
        pltpu.make_async_copy(first_line, first_same, sems.at[size]),
        pltpu.make_async_copy(second_line, second_same, sems.at[size + 1]),
    ]
    for i in range(size):
        span = pl.ds(i * STEP, STEP)
        copies.append(pltpu.make_async_copy(blocks_hbm.at[span], blocks.at[span], sems.at[i]))
    for copy in copies:
        copy.start()
    for copy in copies:
        copy.wait()


def stage(blocks, lines):
    return pl.pallas_call(
        stage_kernel,
        out_shape=[pltpu.VMEM(blocks.shape, blocks.dtype)] + [shape(line.shape) for line in lines],
        in_specs=[whole(pl.ANY)] * 3,
        out_specs=[whole()] + [whole(pl.ANY)] * 2,
        scratch_shapes=[pltpu.SemaphoreType.DMA((blocks.shape[0] // STEP + 2,))],
        compiler_params=params(4),
    )(pltpu.with_memory_space_constraint(blocks, pltpu.HBM), *lines)


def couple_kernel(size, start, goes_on, sends, count, chosen, source_slot, target_slot, blocks, *refs):
    pieces = refs[:size]
    refs = refs[size + goes_on :]
    total, sources, sems = refs[0], refs[-2], refs[-1]
    width = sources.shape[2]
    copies = []
    slot = 0
    for i, piece in enumerate(pieces):
        spot = sources.at[pl.ds(slot, piece.shape[0])]
        copies.append(pltpu.make_async_copy(piece.at[:, :, pl.ds(start, width)], spot, sems.at[i]))
        copies[-1].start()
        slot += piece.shape[0]
    if not goes_on:
        total[...] = jnp.zeros_like(total)
    for copy in copies:
        copy.wait()

    def products(group, carry):
        for j in range(STEP):
            index = group * STEP + j
            product = jnp.dot(blocks[chosen[index]], sources[source_slot[index]], preferred_element_type=F32)
            total[target_slot[index]] += product
        return carry

    lax.fori_loop(0, (count[0] + STEP - 1) // STEP, products, 0)
    if sends:
        refs[1][...] = total[8:16].astype(BF16)


def couple(picked, blocks, pieces, start, width, before=None, sends=True):
    count, rows, _ = blocks.shape
    goes_on = before is not None
    in_vmem = [pltpu.with_memory_space_constraint(value, pltpu.VMEM) for value in ([blocks, before] if goes_on else [blocks])]
    return pl.pallas_call(
        functools.partial(couple_kernel, len(pieces), start, int(goes_on), sends),
        out_shape=[pltpu.VMEM((17, rows, width), F32)] + [shape((8, rows, width))] * sends,
        in_specs=[whole(pltpu.SMEM)] * 4 + [whole()] + [whole(pl.ANY)] * len(pieces) + [whole()] * goes_on,
        out_specs=[whole()] * (1 + sends),
        scratch_shapes=[
            pltpu.VMEM((sum(piece.shape[0] for piece in pieces), rows, width), BF16),
            pltpu.SemaphoreType.DMA((len(pieces),)),
        ],
        input_output_aliases={5 + len(pieces): 0} if goes_on else {},
        compiler_params=params(16),
        cost_estimate=pl.CostEstimate(
            flops=2 * count * rows * rows * width, bytes_accessed=2 * count * rows * rows, transcendentals=0
        ),
    )(*picked, in_vmem[0], *pieces, *in_vmem[1:])


def pick(wanted, source_slot, target_slot):
    size = wanted.shape[0]
    index = jnp.arange(size, dtype=jnp.int32)
    place = jnp.cumsum(wanted.astype(jnp.int32)) - 1
    hits = wanted[None, :] & (place[None, :] == index[:, None])
    gathered = lambda values: jnp.sum(jnp.where(hits, values[None, :], 0), axis=1, dtype=jnp.int32)
    found = jnp.sum(wanted, dtype=jnp.int32)
    target = jnp.where(index < found, gathered(target_slot), 16)
    return found.reshape(1), gathered(index), gathered(source_slot), target


ORDER = (4, 2, 5, 3, 6, 1, 7, 0)
PLACES = tuple(ORDER.index(u) for u in range(8))


def first_kernel(column, early, early_other, keep, other, fwd, bwd, held):
    def part(place):
        columns = slice(column, column + keep.shape[2])
        known = early[place, :, columns] + early_other[place, :, columns].astype(F32)
        return known + (keep[place] + other[place].astype(F32))

    fwd[0] = part(0).astype(BF16)
    fwd[1] = part(1).astype(BF16)
    bwd[...] = part(2).astype(BF16)
    for i in range(5):
        held[i] = part(3 + i)


def second_kernel(held, fwd, bwd, out_fwd, out_bwd):
    out_fwd[...] = (held[0] + fwd[0].astype(F32)).astype(BF16)
    out_bwd[...] = (held[1] + bwd[...].astype(F32)).astype(BF16)


def third_kernel(held, near, fwd, bwd, out_fwd, out_bwd):
    out_fwd[...] = (held[2] + (near[1].astype(F32) + fwd[...].astype(F32))).astype(BF16)
    out_bwd[...] = (held[3] + bwd[...].astype(F32)).astype(BF16)


def last_kernel(start, held, fwd, bwd, rhs, inverse, *refs):
    solved = refs[-1]
    width = held.shape[2]
    coupled = held[4] + (fwd[...].astype(F32) + bwd[...].astype(F32))
    residual = (rhs[:, start : start + width].astype(F32) - coupled).astype(BF16)
    value = jnp.dot(inverse[...], residual, preferred_element_type=F32).astype(BF16)
    if start:
        solved[:, :start] = refs[0][...]
    solved[:, start : start + width] = value


def call(kernel, outs, *args):
    return pl.pallas_call(
        kernel,
        out_shape=outs,
        in_specs=[whole()] * len(args),
        out_specs=[whole()] * len(outs),
        compiler_params=params(),
    )(*args)


def reduce_along_z(column, early, early_other, keep, other):
    _, rows, width = other.shape
    one = shape((rows, width))
    kernel = functools.partial(first_kernel, column)
    outs = [shape((2, rows, width)), one, shape((5, rows, width), F32)]
    fwd, bwd, held = call(kernel, outs, early, early_other, keep, other)
    near = move(fwd, "z", 1)
    bwd = move(bwd, "z", -1)
    fwd, bwd = call(second_kernel, [one, one], held, near, bwd)
    fwd = move(fwd, "z", 2)
    bwd = move(bwd, "z", -1)
    fwd, bwd = call(third_kernel, [one, one], held, near, fwd, bwd)
    return held, move(fwd, "z", 1), move(bwd, "z", -1)


def again_kernel(value, same, sem):
    copy = pltpu.make_async_copy(value, same, sem)
    copy.start()
    copy.wait()


def again(value):
    return pl.pallas_call(
        again_kernel,
        out_shape=shape(value.shape),
        in_specs=[whole(pl.ANY)],
        out_specs=whole(pl.ANY),
        scratch_shapes=[pltpu.SemaphoreType.DMA],
        compiler_params=params(1),
    )(value)


def local(rhs_one, inv_one, rhs_two, inv_two, blocks, block_rows, block_cols):
    rows = rhs_one.shape[3]
    row = lax.axis_index("row")
    col = lax.axis_index("col")
    core = col % 2
    sign = 1 - 2 * core
    here_y, here_x, here_z = row // 4, row % 4, col // 2

    target = block_rows[0, 0]
    parity = target % 2
    steps = ((1 - 2 * parity) * (target // 2 - here_z)) % 8
    target_slot = jnp.where(parity == core, 0, 8) + jnp.array(PLACES, jnp.int32)[steps]
    source = block_cols[0, 0]
    place = source // 2
    from_y = (sign * (place // 4 - here_y)) % 4
    from_x = (sign * (place % 4 - here_x)) % 4
    q = source % 2
    near = jnp.where(q == 0, from_x, from_y)
    distant = jnp.where(q == 0, from_y, from_x)
    first_phase = (near == 0) | (distant == 0)
    across = 3 * q + near - 1
    first_slot = jnp.where(from_y == 0, 2 * from_x, jnp.where(from_x == 0, 6 + 2 * from_y, 0)) + q
    turn = jnp.where(first_phase | (distant == 3), 0, distant)
    picked = [
        pick(turn == 0, jnp.where(first_phase, first_slot, 14 + across), target_slot),
        pick(turn == 1, across, target_slot),
        pick(turn == 2, across, target_slot),
    ]

    solved_one = solve_one(rhs_one[0, 0], inv_one[0, 0])
    axes = ("x", "y")
    both = range(2)
    fwd = [move(solved_one, axis, 1) for axis in axes]
    solved_later = again(solved_one)
    bwd = [move(solved_later, axis, -1) for axis in axes]
    far = [move(fwd[i], axes[i], 1) for i in both]
    pieces = [solved_one] + [piece for i in both for piece in (bwd[i], far[i], fwd[i])]

    lines = [jnp.concatenate([bwd[q][q : q + 1], far[q][q : q + 1], fwd[q][q : q + 1]]) for q in both]
    fwd = [move(lines[q], axes[1 - q], 1) for q in both]
    factor, *lines = stage(blocks[0, 0], lines)
    bwd = [move(lines[q], axes[1 - q], -1) for q in both]
    far = [move(fwd[q], axes[1 - q], 1) for q in both]

    whole_width = rhs_two.shape[4]
    (early,) = couple(picked[0], factor, pieces + fwd, 0, whole_width, sends=False)
    early, send = couple(picked[1], factor, bwd, 0, whole_width, before=early)
    early_other = swap_cores(send)
    width = whole_width // PARTS
    solved_two = []
    for i in range(PARTS):
        start = i * width
        keep, send = couple(picked[2], factor, far, start, width)
        held, fwd, bwd = reduce_along_z(start, early, early_other, keep, swap_cores(send))
        kernel = functools.partial(last_kernel, start)
        solved_two = call(
            kernel, [shape((rows, start + width))], held, fwd, bwd, rhs_two[0, 0, 0], inv_two[0, 0, 0], *solved_two
        )
    return (solved_one[None, None], solved_two[0][None, None, None])


def solution(mesh):
    in_specs = (
        P("row", "col", None, None, None),
        P("row", "col", None, None, None),
        P("row", "col", None, None, None),
        P("row", "col", None, None, None),
        P("row", "col", None, None, None),
        P("row", "col", None),
        P("row", "col", None),
    )
    out_specs = (P("row", "col", None, None, None), P("row", "col", None, None, None))
    return jax.shard_map(local, mesh=mesh, in_specs=in_specs, out_specs=out_specs, check_vma=False)
```

time: 112 us -> 103 us (0.920)
  the two profiles are of different devices: /device:TPU:1 before, /device:TPU:7 now
where the time goes in v4:
time: 103 us
  starting transfers between devices  38.3 us (37%)
  waiting for transfers between devices  30.1 us (29%)
  Pallas kernels  26 us (25%)
  other arithmetic  4.85 us (5%)
  local copies, waits for them, and re-layouts  2.71 us (3%)
    ppermute x24, waiting for transfers between devices, move(): return lax.ppermute(value, BOTH, ring_pairs(axis, steps))  30.1 us
    ppermute x24, starting transfers between devices, move(): return lax.ppermute(value, BOTH, ring_pairs(axis, steps))  29.7 us
    pallas_call x4, Pallas kernels, couple(): pl.pallas_call(functools.partial(couple_kernel, len(pieces), start, int(g...  16.6 us
    ppermute x3, starting transfers between devices, swap_cores(): return lax.ppermute(value, 'col', [(i, i ^ 1) for i in range(16)])  8.61 us
    pallas_call x1, Pallas kernels, stage(): pl.pallas_call(stage_kernel, out_shape=[pltpu.VMEM(blocks.shape, blocks.d...  4.27 us
    pallas_call x1, Pallas kernels, solve_one(): pl.pallas_call(solve_one_kernel, out_shape=shape(rhs.shape), in_specs=[wh...  2.28 us
  transfers between devices with their start and end apart: 27, of which 12 were waited for; matrix products, arithmetic and copies ran while one was open for 6% of the time, Pallas kernels for 22%

profile of v4, /device:TPU:7, one launch (start us, length us, event | category | flops | bytes accessed | tf_op | source)
XLA Modules:
  0.0 103.0 jit_solution(8547255641613701826)
XLA Ops:
  0.6 2.3 %shard_map.95.value.refs_0_ = bf16[2,256,512]{2,1,0:T(8,128)(2,1)} custom-call(bf16[2,256,512]{2,1,0:T(8,128)(2,1)} %bitcast.36, bf16[2,256,256]{2,1,0:T(8,128)(2,1)} %bitcast.37), custom_call_target="tpu_custom_call" | custom-call | tf_op jit(solution)/shard_map/pallas_call | solution.py:70
  2.9 2.8 %collective-permute-start.4 = (bf16[2,256,512]{2,1,0:T(8,128)(2,1)}, bf16[2,256,512]{2,1,0:T(8,128)(2,1)S(1)}, u32[]{:S(2)}, u32[]{:S(2)}) collective-permute-start(bf16[2,256,512]{2,1,0:T(8,128)(2,1)} %shard_map.95.value.refs_0_), channel_id=1, source_target_pairs={{0,64},{1,193},{2,66},{3,195},{4,68},{5,197},{6,70},{7,199},{8,72}... | collective-permute-start | bytes 1572872 | tf_op jit(solution)/shard_map/ppermute | solution.py:49
  5.7 0.5 collective-permute-start.1
  6.3 1.1 %copy-done = bf16[2,256,512]{2,1,0:T(8,128)(2,1)S(1)} copy-done((bf16[2,256,512]{2,1,0:T(8,128)(2,1)S(1)}, bf16[2,256,512]{2,1,0:T(8,128)(2,1)}, u32[]{:S(2)}) %copy-start) | copy-done | bytes 524312
  7.4 0.8 shard_map.96
  8.2 2.2 %collective-permute-start = (bf16[2,256,512]{2,1,0:T(8,128)(2,1)}, bf16[2,256,512]{2,1,0:T(8,128)(2,1)S(1)}, u32[]{:S(2)}, u32[]{:S(2)}) collective-permute-start(bf16[2,256,512]{2,1,0:T(8,128)(2,1)} %shard_map.96), channel_id=1, source_target_pairs={{0,48},{1,17},{2,50},{3,19},{4,52},{5,21},{6,54},{7,23},{8,56},{9,... | collective-permute-start | bytes 1572872 | tf_op jit(solution)/shard_map/ppermute | solution.py:49
  10.5 0.7 copy.27
  11.2 0.7 broadcast_add_fusion
  11.9 0.1 compare_convert_fusion
  12.1 0.1 reduce-window.25
  12.2 0.1 reduce-window.24
  12.3 3.2 %collective-permute-start.5 = (bf16[2,256,512]{2,1,0:T(8,128)(2,1)S(1)}, bf16[2,256,512]{2,1,0:T(8,128)(2,1)S(1)}, u32[]{:S(2)}, u32[]{:S(2)}) collective-permute-start(bf16[2,256,512]{2,1,0:T(8,128)(2,1)S(1)} %collective-permute-done.4.refs_6_), channel_id=1, source_target_pairs={{0,64},{1,193},{2,66},{3,195},{4,68},{5,197},{6,70},{7,199},{8,72}... | collective-permute-start | bytes 1572872 | tf_op jit(solution)/shard_map/ppermute | solution.py:49
  15.5 0.1 add_reduce_fusion.1
  15.6 1.6 %collective-permute-start.2 = (bf16[2,256,512]{2,1,0:T(8,128)(2,1)S(1)}, bf16[2,256,512]{2,1,0:T(8,128)(2,1)S(1)}, u32[]{:S(2)}, u32[]{:S(2)}) collective-permute-start(bf16[2,256,512]{2,1,0:T(8,128)(2,1)S(1)} %collective-permute-done.1.refs_3_), channel_id=1, source_target_pairs={{0,16},{1,49},{2,18},{3,51},{4,20},{5,53},{6,22},{7,55},{8,24},{9,... | collective-permute-start | bytes 1572872 | tf_op jit(solution)/shard_map/ppermute | solution.py:49
  17.2 0.1 add_reduce_fusion.2
  17.4 0.1 reduce-window.26
  17.5 0.8 copy.31
  18.2 0.1 add_reduce_fusion
  18.3 0.2 select_reduce_fusion
  18.6 0.9 collective-permute-done.3.refs_4_
  19.5 0.3 collective-permute-done.refs_1_
  19.9 3.4 %collective-permute-done.5.refs_5_ = bf16[2,256,512]{2,1,0:T(8,128)(2,1)S(1)} collective-permute-done((bf16[2,256,512]{2,1,0:T(8,128)(2,1)S(1)}, bf16[2,256,512]{2,1,0:T(8,128)(2,1)S(1)}, u32[]{:S(2)}, u32[]{:S(2)}) %collective-permute-start.5) | collective-permute-done | bytes 524320 | tf_op jit(solution)/shard_map/ppermute | solution.py:49
  23.3 0.1 pad_maximum_fusion.1.second_line
  23.4 0.6 collective-permute-start.9
  24.0 2.6 %collective-permute-done.2.refs_2_ = bf16[2,256,512]{2,1,0:T(8,128)(2,1)S(1)} collective-permute-done((bf16[2,256,512]{2,1,0:T(8,128)(2,1)S(1)}, bf16[2,256,512]{2,1,0:T(8,128)(2,1)S(1)}, u32[]{:S(2)}, u32[]{:S(2)}) %collective-permute-start.2) | collective-permute-done | bytes 524320 | tf_op jit(solution)/shard_map/ppermute | solution.py:49
  26.7 0.6 collective-permute-start.8
  27.4 0.1 compare_reduce_fusion
  27.5 0.3 select_reduce_fusion.4
  27.8 4.3 %shard_map.97 = (bf16[80,256,256]{2,1,0:T(8,128)(2,1)S(1)}, bf16[3,256,512]{2,1,0:T(8,128)(2,1)S(1)}, bf16[3,256,512]{2,1,0:T(8,128)(2,1)S(1)}) custom-call(bf16[80,256,256]{2,1,0:T(8,128)(2,1)} %bitcast.35, bf16[3,256,512]{2,1,0:T(8,128)(2,1)S(1)} %pad_maximum_fusion.first_line, bf16[3,256,512]{2,1,0:T(8,128)(2,1)S(1)} %pad_maximum_fusion.1.second_line), custom_call_target="tpu_custom_call" | custom-call | tf_op jit(solution)/shard_map/pallas_call | solution.py:100
  32.0 1.0 collective-permute-start.6
  33.0 1.3 %collective-permute-start.7 = (bf16[3,256,512]{2,1,0:T(8,128)(2,1)S(1)}, bf16[3,256,512]{2,1,0:T(8,128)(2,1)S(1)}, u32[]{:S(2)}, u32[]{:S(2)}) collective-permute-start(bf16[3,256,512]{2,1,0:T(8,128)(2,1)S(1)} %get-tuple-element.27), channel_id=1, source_target_pairs={{0,48},{1,17},{2,50},{3,19},{4,52},{5,21},{6,54},{7,23},{8,56},{9,... | collective-permute-start | bytes 2359304 | tf_op jit(solution)/shard_map/ppermute | solution.py:49
  34.4 0.7 convert_reduce_fusion
  35.1 1.2 %compare_select_fusion.8 = (s32[80]{0:T(128)S(1)}, s32[80]{0:T(128)S(1)}) fusion(s32[80]{0:T(128)S(1)} %get-tuple-element.51, s32[]{:T(128)} %get-tuple-element.62, s32[80]{0:T(128)S(1)} %get-tuple-element.68, s32[]{:T(128)} %get-tuple-element.61), kind=kLoop, calls=%fused_computation.85 | loop fusion | flops 320 | bytes 1288 | tf_op jit(solution)/shard_map/jit(_where)/select_n | solution.py:167
  36.3 0.2 collective-permute-start.12
  36.6 1.4 %collective-permute-done.8.refs_7_ = bf16[3,256,512]{2,1,0:T(8,128)(2,1)S(1)} collective-permute-done((bf16[3,256,512]{2,1,0:T(8,128)(2,1)S(1)}, bf16[3,256,512]{2,1,0:T(8,128)(2,1)S(1)}, u32[]{:S(2)}, u32[]{:S(2)}) %collective-permute-start.8) | collective-permute-done | bytes 786464 | tf_op jit(solution)/shard_map/ppermute | solution.py:49
  37.9 1.5 %collective-permute-start.11 = (bf16[3,256,512]{2,1,0:T(8,128)(2,1)S(1)}, bf16[3,256,512]{2,1,0:T(8,128)(2,1)S(1)}, u32[]{:S(2)}, u32[]{:S(2)}) collective-permute-start(bf16[3,256,512]{2,1,0:T(8,128)(2,1)S(1)} %collective-permute-done.8.refs_7_), channel_id=1, source_target_pairs={{0,64},{1,193},{2,66},{3,195},{4,68},{5,197},{6,70},{7,199},{8,72}... | collective-permute-start | bytes 2359304 | tf_op jit(solution)/shard_map/ppermute | solution.py:49
  39.4 6.1 %shard_map.98.refs_2_ = f32[17,256,512]{2,1,0:T(8,128)S(1)} custom-call(s32[1]{0:T(128)} %bitcast.9.count, s32[80]{0:T(128)S(1)} %get-tuple-element.53.chosen, s32[80]{0:T(128)S(1)} %get-tuple-element.52.source_slot, s32[80]{0:T(128)S(1)} %get-tuple-element.83.target_slot, bf16[80,256,256]{2,1,0:T(8,128)(2,1)S(1)} %get-tuple-element.25.blocks, ...), custom_call_target="tpu_custom_call" | custom-call | flops 5368709120 | bytes 10485760 | tf_op jit(solution)/shard_map/pallas_call | solution.py:143
  45.5 4.2 %collective-permute-done.6.refs_0_ = bf16[3,256,512]{2,1,0:T(8,128)(2,1)S(1)} collective-permute-done((bf16[3,256,512]{2,1,0:T(8,128)(2,1)S(1)}, bf16[3,256,512]{2,1,0:T(8,128)(2,1)S(1)}, u32[]{:S(2)}, u32[]{:S(2)}) %collective-permute-start.6) | collective-permute-done | bytes 786464 | tf_op jit(solution)/shard_map/ppermute | solution.py:49
  49.7 4.1 %shard_map.99 = (f32[17,256,512]{2,1,0:T(8,128)S(1)}, bf16[8,256,512]{2,1,0:T(8,128)(2,1)S(1)}) custom-call(s32[1]{0:T(128)} %bitcast.4.count, s32[80]{0:T(128)S(1)} %get-tuple-element.63.chosen, s32[80]{0:T(128)S(1)} %get-tuple-element.67.source_slot, s32[80]{0:T(128)S(1)} %get-tuple-element.84.target_slot, ...), custom_call_target="tpu_custom_call", output_to_operand_aliasing={{0}: (7, {})} | custom-call | flops 5368709120 | bytes 10485760 | tf_op jit(solution)/shard_map/pallas_call | solution.py:143
  53.9 7.9 %collective-permute-start.10 = (bf16[8,256,512]{2,1,0:T(8,128)(2,1)S(1)}, bf16[8,256,512]{2,1,0:T(8,128)(2,1)S(1)}, u32[]{:S(2)}, u32[]{:S(2)}) collective-permute-start(bf16[8,256,512]{2,1,0:T(8,128)(2,1)S(1)} %get-tuple-element.29), channel_id=1, source_target_pairs={{0,1},{1,0},{2,3},{3,2},{4,5},{5,4},{6,7},{7,6},{8,9},{9,8},{10,11... | collective-permute-start | bytes 6291464 | tf_op jit(solution)/shard_map/ppermute | solution.py:53
  61.8 0.6 compare_select_fusion.7.target_slot
  62.5 3.2 %shard_map.104 = (f32[17,256,256]{2,1,0:T(8,128)S(1)}, bf16[8,256,256]{2,1,0:T(8,128)(2,1)S(1)}) custom-call(s32[1]{0:T(128)} %bitcast.10.count, s32[80]{0:T(128)S(1)} %get-tuple-element.66.chosen, s32[80]{0:T(128)S(1)} %get-tuple-element.65.source_slot, s32[80]{0:T(128)S(1)} %compare_select_fusion.7.target_slot, ...), custom_call_target="tpu_custom_call" | custom-call | flops 2684354560 | bytes 10485760 | tf_op jit(solution)/shard_map/pallas_call | solution.py:143
  65.7 0.1 collective-permute-start.20
  65.8 3.2 %shard_map.100 = (f32[17,256,256]{2,1,0:T(8,128)S(1)}, bf16[8,256,256]{2,1,0:T(8,128)(2,1)S(1)}) custom-call(s32[1]{0:T(128)} %bitcast.10.count, s32[80]{0:T(128)S(1)} %get-tuple-element.66.chosen, s32[80]{0:T(128)S(1)} %get-tuple-element.65.source_slot, s32[80]{0:T(128)S(1)} %compare_select_fusion.7.target_slot, ...), custom_call_target="tpu_custom_call" | custom-call | flops 2684354560 | bytes 10485760 | tf_op jit(solution)/shard_map/pallas_call | solution.py:143
  69.0 0.6 collective-permute-start.13
  69.6 0.4 shard_map.105
  70.0 4.1 %collective-permute-start.21 = (bf16[2,256,256]{2,1,0:T(8,128)(2,1)S(1)}, bf16[2,256,256]{2,1,0:T(8,128)(2,1)S(1)}, u32[]{:S(2)}, u32[]{:S(2)}) collective-permute-start(bf16[2,256,256]{2,1,0:T(8,128)(2,1)S(1)} %get-tuple-element.42), channel_id=1, source_target_pairs={{0,2},{1,15},{2,4},{3,1},{4,6},{5,3},{6,8},{7,5},{8,10},{9,7},{10,... | collective-permute-start | bytes 786440 | tf_op jit(solution)/shard_map/ppermute | solution.py:49
  74.1 0.4 shard_map.101
  74.5 1.9 %collective-permute-start.14 = (bf16[2,256,256]{2,1,0:T(8,128)(2,1)S(1)}, bf16[2,256,256]{2,1,0:T(8,128)(2,1)S(1)}, u32[]{:S(2)}, u32[]{:S(2)}) collective-permute-start(bf16[2,256,256]{2,1,0:T(8,128)(2,1)S(1)} %get-tuple-element.33), channel_id=1, source_target_pairs={{0,2},{1,15},{2,4},{3,1},{4,6},{5,3},{6,8},{7,5},{8,10},{9,7},{10,... | collective-permute-start | bytes 786440 | tf_op jit(solution)/shard_map/ppermute | solution.py:49
  76.4 5.9 %collective-permute-done.22.bwd = bf16[256,256]{1,0:T(8,128)(2,1)S(1)} collective-permute-done((bf16[256,256]{1,0:T(8,128)(2,1)S(1)}, bf16[256,256]{1,0:T(8,128)(2,1)S(1)}, u32[]{:S(2)}, u32[]{:S(2)}) %collective-permute-start.22) | collective-permute-done | bytes 131104 | tf_op jit(solution)/shard_map/ppermute | solution.py:49
  82.3 0.6 collective-permute-start.23
  83.0 1.4 %collective-permute-start.24 = (bf16[256,256]{1,0:T(8,128)(2,1)S(1)}, bf16[256,256]{1,0:T(8,128)(2,1)S(1)}, u32[]{:S(2)}, u32[]{:S(2)}) collective-permute-start(bf16[256,256]{1,0:T(8,128)(2,1)S(1)} %get-tuple-element.45), channel_id=1, source_target_pairs={{0,14},{1,3},{2,0},{3,5},{4,2},{5,7},{6,4},{7,9},{8,6},{9,11},{10,... | collective-permute-start | bytes 393224 | tf_op jit(solution)/shard_map/ppermute | solution.py:49
  84.4 1.4 %collective-permute-start.16 = (bf16[256,256]{1,0:T(8,128)(2,1)S(1)}, bf16[256,256]{1,0:T(8,128)(2,1)S(1)}, u32[]{:S(2)}, u32[]{:S(2)}) collective-permute-start(bf16[256,256]{1,0:T(8,128)(2,1)S(1)} %get-tuple-element.35), channel_id=1, source_target_pairs={{0,4},{1,13},{2,6},{3,15},{4,8},{5,1},{6,10},{7,3},{8,12},{9,5},{1... | collective-permute-start | bytes 393224 | tf_op jit(solution)/shard_map/ppermute | solution.py:49
  85.8 1.5 %collective-permute-start.17 = (bf16[256,256]{1,0:T(8,128)(2,1)S(1)}, bf16[256,256]{1,0:T(8,128)(2,1)S(1)}, u32[]{:S(2)}, u32[]{:S(2)}) collective-permute-start(bf16[256,256]{1,0:T(8,128)(2,1)S(1)} %get-tuple-element.36), channel_id=1, source_target_pairs={{0,14},{1,3},{2,0},{3,5},{4,2},{5,7},{6,4},{7,9},{8,6},{9,11},{10,... | collective-permute-start | bytes 393224 | tf_op jit(solution)/shard_map/ppermute | solution.py:49
  87.2 0.2 collective-permute-done.23.fwd
  87.5 3.5 %collective-permute-done.24.bwd = bf16[256,256]{1,0:T(8,128)(2,1)S(1)} collective-permute-done((bf16[256,256]{1,0:T(8,128)(2,1)S(1)}, bf16[256,256]{1,0:T(8,128)(2,1)S(1)}, u32[]{:S(2)}, u32[]{:S(2)}) %collective-permute-start.24) | collective-permute-done | bytes 131104 | tf_op jit(solution)/shard_map/ppermute | solution.py:49
  91.0 1.5 %collective-permute-start.25 = (bf16[256,256]{1,0:T(8,128)(2,1)S(1)}, bf16[256,256]{1,0:T(8,128)(2,1)S(1)}, u32[]{:S(2)}, u32[]{:S(2)}) collective-permute-start(bf16[256,256]{1,0:T(8,128)(2,1)S(1)} %get-tuple-element.46), channel_id=1, source_target_pairs={{0,2},{1,15},{2,4},{3,1},{4,6},{5,3},{6,8},{7,5},{8,10},{9,7},{10,... | collective-permute-start | bytes 393224 | tf_op jit(solution)/shard_map/ppermute | solution.py:49
  92.5 1.7 %collective-permute-done.17.bwd = bf16[256,256]{1,0:T(8,128)(2,1)S(1)} collective-permute-done((bf16[256,256]{1,0:T(8,128)(2,1)S(1)}, bf16[256,256]{1,0:T(8,128)(2,1)S(1)}, u32[]{:S(2)}, u32[]{:S(2)}) %collective-permute-start.17) | collective-permute-done | bytes 131104 | tf_op jit(solution)/shard_map/ppermute | solution.py:49
  94.2 1.4 %collective-permute-start.18 = (bf16[256,256]{1,0:T(8,128)(2,1)S(1)}, bf16[256,256]{1,0:T(8,128)(2,1)S(1)}, u32[]{:S(2)}, u32[]{:S(2)}) collective-permute-start(bf16[256,256]{1,0:T(8,128)(2,1)S(1)} %get-tuple-element.37), channel_id=1, source_target_pairs={{0,2},{1,15},{2,4},{3,1},{4,6},{5,3},{6,8},{7,5},{8,10},{9,7},{10,... | collective-permute-start | bytes 393224 | tf_op jit(solution)/shard_map/ppermute | solution.py:49
  95.7 0.1 collective-permute-start.19
  95.8 3.2 %collective-permute-done.26.bwd = bf16[256,256]{1,0:T(8,128)(2,1)S(1)} collective-permute-done((bf16[256,256]{1,0:T(8,128)(2,1)S(1)}, bf16[256,256]{1,0:T(8,128)(2,1)S(1)}, u32[]{:S(2)}, u32[]{:S(2)}) %collective-permute-start.26) | collective-permute-done | bytes 131104 | tf_op jit(solution)/shard_map/ppermute | solution.py:49
  99.0 0.2 shard_map.108.refs_0_
  99.2 2.8 %collective-permute-done.19.bwd = bf16[256,256]{1,0:T(8,128)(2,1)S(1)} collective-permute-done((bf16[256,256]{1,0:T(8,128)(2,1)S(1)}, bf16[256,256]{1,0:T(8,128)(2,1)S(1)}, u32[]{:S(2)}, u32[]{:S(2)}) %collective-permute-start.19) | collective-permute-done | bytes 131104 | tf_op jit(solution)/shard_map/ppermute | solution.py:49
  102.1 0.9 shard_map.109
  (44 shorter events, 0.6 us)
Async XLA Ops:
  0.6 26.8 %copy-start.4 = (s32[1,1,80]{2,1,0:T(1,128)S(1)}, s32[1,1,80]{2,1,0:T(1,128)}, u32[]{:S(2)}) copy-start(s32[1,1,80]{2,1,0:T(1,128)} %param.13) | copy-start | bytes 964
  2.9 9.4 %collective-permute-start.4 = (bf16[2,256,512]{2,1,0:T(8,128)(2,1)}, bf16[2,256,512]{2,1,0:T(8,128)(2,1)S(1)}, u32[]{:S(2)}, u32[]{:S(2)}) collective-permute-start(bf16[2,256,512]{2,1,0:T(8,128)(2,1)} %shard_map.95.value.refs_0_), channel_id=1, source_target_pairs={{0,64},{1,193},{2,66},{3,195},{4,68},{5,197},{6,70},{7,199},{8,72}... | collective-permute-start | bytes 1572872 | tf_op jit(solution)/shard_map/ppermute | solution.py:49
  5.7 9.9 %collective-permute-start.1 = (bf16[2,256,512]{2,1,0:T(8,128)(2,1)}, bf16[2,256,512]{2,1,0:T(8,128)(2,1)S(1)}, u32[]{:S(2)}, u32[]{:S(2)}) collective-permute-start(bf16[2,256,512]{2,1,0:T(8,128)(2,1)} %shard_map.95.value.refs_0_), channel_id=1, source_target_pairs={{0,16},{1,49},{2,18},{3,51},{4,20},{5,53},{6,22},{7,55},{8,24},{9,... | collective-permute-start | bytes 1572872 | tf_op jit(solution)/shard_map/ppermute | solution.py:49
  6.3 1.1 %copy-start = (bf16[2,256,512]{2,1,0:T(8,128)(2,1)S(1)}, bf16[2,256,512]{2,1,0:T(8,128)(2,1)}, u32[]{:S(2)}) copy-start(bf16[2,256,512]{2,1,0:T(8,128)(2,1)} %shard_map.95.value.refs_0_) | copy-start | bytes 1572868
  8.2 11.4 %collective-permute-start.3 = (bf16[2,256,512]{2,1,0:T(8,128)(2,1)}, bf16[2,256,512]{2,1,0:T(8,128)(2,1)S(1)}, u32[]{:S(2)}, u32[]{:S(2)}) collective-permute-start(bf16[2,256,512]{2,1,0:T(8,128)(2,1)} %shard_map.96), channel_id=1, source_target_pairs={{0,192},{1,65},{2,194},{3,67},{4,196},{5,69},{6,198},{7,71},{8,200... | collective-permute-start | bytes 1572872 | tf_op jit(solution)/shard_map/ppermute | solution.py:49
  8.2 11.6 %collective-permute-start = (bf16[2,256,512]{2,1,0:T(8,128)(2,1)}, bf16[2,256,512]{2,1,0:T(8,128)(2,1)S(1)}, u32[]{:S(2)}, u32[]{:S(2)}) collective-permute-start(bf16[2,256,512]{2,1,0:T(8,128)(2,1)} %shard_map.96), channel_id=1, source_target_pairs={{0,48},{1,17},{2,50},{3,19},{4,52},{5,21},{6,54},{7,23},{8,56},{9,... | collective-permute-start | bytes 1572872 | tf_op jit(solution)/shard_map/ppermute | solution.py:49
  12.3 11.0 %collective-permute-start.5 = (bf16[2,256,512]{2,1,0:T(8,128)(2,1)S(1)}, bf16[2,256,512]{2,1,0:T(8,128)(2,1)S(1)}, u32[]{:S(2)}, u32[]{:S(2)}) collective-permute-start(bf16[2,256,512]{2,1,0:T(8,128)(2,1)S(1)} %collective-permute-done.4.refs_6_), channel_id=1, source_target_pairs={{0,64},{1,193},{2,66},{3,195},{4,68},{5,197},{6,70},{7,199},{8,72}... | collective-permute-start | bytes 1572872 | tf_op jit(solution)/shard_map/ppermute | solution.py:49
  15.6 11.0 %collective-permute-start.2 = (bf16[2,256,512]{2,1,0:T(8,128)(2,1)S(1)}, bf16[2,256,512]{2,1,0:T(8,128)(2,1)S(1)}, u32[]{:S(2)}, u32[]{:S(2)}) collective-permute-start(bf16[2,256,512]{2,1,0:T(8,128)(2,1)S(1)} %collective-permute-done.1.refs_3_), channel_id=1, source_target_pairs={{0,16},{1,49},{2,18},{3,51},{4,20},{5,53},{6,22},{7,55},{8,24},{9,... | collective-permute-start | bytes 1572872 | tf_op jit(solution)/shard_map/ppermute | solution.py:49
  23.4 12.9 %collective-permute-start.9 = (bf16[3,256,512]{2,1,0:T(8,128)(2,1)S(1)}, bf16[3,256,512]{2,1,0:T(8,128)(2,1)S(1)}, u32[]{:S(2)}, u32[]{:S(2)}) collective-permute-start(bf16[3,256,512]{2,1,0:T(8,128)(2,1)S(1)} %pad_maximum_fusion.1.second_line), channel_id=1, source_target_pairs={{0,16},{1,49},{2,18},{3,51},{4,20},{5,53},{6,22},{7,55},{8,24},{9,... | collective-permute-start | bytes 2359304 | tf_op jit(solution)/shard_map/ppermute | solution.py:49
  26.7 11.2 %collective-permute-start.8 = (bf16[3,256,512]{2,1,0:T(8,128)(2,1)S(1)}, bf16[3,256,512]{2,1,0:T(8,128)(2,1)S(1)}, u32[]{:S(2)}, u32[]{:S(2)}) collective-permute-start(bf16[3,256,512]{2,1,0:T(8,128)(2,1)S(1)} %pad_maximum_fusion.first_line), channel_id=1, source_target_pairs={{0,64},{1,193},{2,66},{3,195},{4,68},{5,197},{6,70},{7,199},{8,72}... | collective-permute-start | bytes 2359304 | tf_op jit(solution)/shard_map/ppermute | solution.py:49
  27.8 11.7 %copy-start.1 = (bf16[2,256,512]{2,1,0:T(8,128)(2,1)S(1)}, bf16[2,256,512]{2,1,0:T(8,128)(2,1)}, u32[]{:S(2)}) copy-start(bf16[2,256,512]{2,1,0:T(8,128)(2,1)} %shard_map.95.value.refs_0_) | copy-start | bytes 1572868
  32.0 17.7 %collective-permute-start.6 = (bf16[3,256,512]{2,1,0:T(8,128)(2,1)S(1)}, bf16[3,256,512]{2,1,0:T(8,128)(2,1)S(1)}, u32[]{:S(2)}, u32[]{:S(2)}) collective-permute-start(bf16[3,256,512]{2,1,0:T(8,128)(2,1)S(1)} %get-tuple-element.26), channel_id=1, source_target_pairs={{0,192},{1,65},{2,194},{3,67},{4,196},{5,69},{6,198},{7,71},{8,200... | collective-permute-start | bytes 2359304 | tf_op jit(solution)/shard_map/ppermute | solution.py:49
  33.0 16.7 %collective-permute-start.7 = (bf16[3,256,512]{2,1,0:T(8,128)(2,1)S(1)}, bf16[3,256,512]{2,1,0:T(8,128)(2,1)S(1)}, u32[]{:S(2)}, u32[]{:S(2)}) collective-permute-start(bf16[3,256,512]{2,1,0:T(8,128)(2,1)S(1)} %get-tuple-element.27), channel_id=1, source_target_pairs={{0,48},{1,17},{2,50},{3,19},{4,52},{5,21},{6,54},{7,23},{8,56},{9,... | collective-permute-start | bytes 2359304 | tf_op jit(solution)/shard_map/ppermute | solution.py:49
  36.3 26.1 %collective-permute-start.12 = (bf16[3,256,512]{2,1,0:T(8,128)(2,1)S(1)}, bf16[3,256,512]{2,1,0:T(8,128)(2,1)S(1)}, u32[]{:S(2)}, u32[]{:S(2)}) collective-permute-start(bf16[3,256,512]{2,1,0:T(8,128)(2,1)S(1)} %collective-permute-done.9.refs_8_), channel_id=1, source_target_pairs={{0,16},{1,49},{2,18},{3,51},{4,20},{5,53},{6,22},{7,55},{8,24},{9,... | collective-permute-start | bytes 2359304 | tf_op jit(solution)/shard_map/ppermute | solution.py:49
  37.9 24.5 %collective-permute-start.11 = (bf16[3,256,512]{2,1,0:T(8,128)(2,1)S(1)}, bf16[3,256,512]{2,1,0:T(8,128)(2,1)S(1)}, u32[]{:S(2)}, u32[]{:S(2)}) collective-permute-start(bf16[3,256,512]{2,1,0:T(8,128)(2,1)S(1)} %collective-permute-done.8.refs_7_), channel_id=1, source_target_pairs={{0,64},{1,193},{2,66},{3,195},{4,68},{5,197},{6,70},{7,199},{8,72}... | collective-permute-start | bytes 2359304 | tf_op jit(solution)/shard_map/ppermute | solution.py:49
  53.9 15.7 %collective-permute-start.10 = (bf16[8,256,512]{2,1,0:T(8,128)(2,1)S(1)}, bf16[8,256,512]{2,1,0:T(8,128)(2,1)S(1)}, u32[]{:S(2)}, u32[]{:S(2)}) collective-permute-start(bf16[8,256,512]{2,1,0:T(8,128)(2,1)S(1)} %get-tuple-element.29), channel_id=1, source_target_pairs={{0,1},{1,0},{2,3},{3,2},{4,5},{5,4},{6,7},{7,6},{8,9},{9,8},{10,11... | collective-permute-start | bytes 6291464 | tf_op jit(solution)/shard_map/ppermute | solution.py:53
  65.7 3.9 %collective-permute-start.20 = (bf16[8,256,256]{2,1,0:T(8,128)(2,1)S(1)}, bf16[8,256,256]{2,1,0:T(8,128)(2,1)S(1)}, u32[]{:S(2)}, u32[]{:S(2)}) collective-permute-start(bf16[8,256,256]{2,1,0:T(8,128)(2,1)S(1)} %get-tuple-element.40), channel_id=1, source_target_pairs={{0,1},{1,0},{2,3},{3,2},{4,5},{5,4},{6,7},{7,6},{8,9},{9,8},{10,11... | collective-permute-start | bytes 3145736 | tf_op jit(solution)/shard_map/ppermute | solution.py:53
  69.0 5.1 %collective-permute-start.13 = (bf16[8,256,256]{2,1,0:T(8,128)(2,1)S(1)}, bf16[8,256,256]{2,1,0:T(8,128)(2,1)S(1)}, u32[]{:S(2)}, u32[]{:S(2)}) collective-permute-start(bf16[8,256,256]{2,1,0:T(8,128)(2,1)S(1)} %get-tuple-element.31), channel_id=1, source_target_pairs={{0,1},{1,0},{2,3},{3,2},{4,5},{5,4},{6,7},{7,6},{8,9},{9,8},{10,11... | collective-permute-start | bytes 3145736 | tf_op jit(solution)/shard_map/ppermute | solution.py:53
  70.0 12.3 %collective-permute-start.21 = (bf16[2,256,256]{2,1,0:T(8,128)(2,1)S(1)}, bf16[2,256,256]{2,1,0:T(8,128)(2,1)S(1)}, u32[]{:S(2)}, u32[]{:S(2)}) collective-permute-start(bf16[2,256,256]{2,1,0:T(8,128)(2,1)S(1)} %get-tuple-element.42), channel_id=1, source_target_pairs={{0,2},{1,15},{2,4},{3,1},{4,6},{5,3},{6,8},{7,5},{8,10},{9,7},{10,... | collective-permute-start | bytes 786440 | tf_op jit(solution)/shard_map/ppermute | solution.py:49
  74.4 24.6 %copy-start.2 = (bf16[1,1,1,256,512]{4,3,2,1,0:T(8,128)(2,1)S(1)}, bf16[1,1,1,256,512]{4,3,2,1,0:T(8,128)(2,1)}, u32[]{:S(2)}) copy-start(bf16[1,1,1,256,512]{4,3,2,1,0:T(8,128)(2,1)} %param.10) | copy-start | bytes 786436
  74.5 24.5 %copy-start.3 = (bf16[1,1,1,256,256]{4,3,2,1,0:T(8,128)(2,1)S(1)}, bf16[1,1,1,256,256]{4,3,2,1,0:T(8,128)(2,1)}, u32[]{:S(2)}) copy-start(bf16[1,1,1,256,256]{4,3,2,1,0:T(8,128)(2,1)} %param.11) | copy-start | bytes 393220
  74.5 9.9 %collective-permute-start.14 = (bf16[2,256,256]{2,1,0:T(8,128)(2,1)S(1)}, bf16[2,256,256]{2,1,0:T(8,128)(2,1)S(1)}, u32[]{:S(2)}, u32[]{:S(2)}) collective-permute-start(bf16[2,256,256]{2,1,0:T(8,128)(2,1)S(1)} %get-tuple-element.33), channel_id=1, source_target_pairs={{0,2},{1,15},{2,4},{3,1},{4,6},{5,3},{6,8},{7,5},{8,10},{9,7},{10,... | collective-permute-start | bytes 786440 | tf_op jit(solution)/shard_map/ppermute | solution.py:49
  76.4 5.9 %collective-permute-start.22 = (bf16[256,256]{1,0:T(8,128)(2,1)S(1)}, bf16[256,256]{1,0:T(8,128)(2,1)S(1)}, u32[]{:S(2)}, u32[]{:S(2)}) collective-permute-start(bf16[256,256]{1,0:T(8,128)(2,1)S(1)} %get-tuple-element.43), channel_id=1, source_target_pairs={{0,14},{1,3},{2,0},{3,5},{4,2},{5,7},{6,4},{7,9},{8,6},{9,11},{10,... | collective-permute-start | bytes 393224 | tf_op jit(solution)/shard_map/ppermute | solution.py:49
  76.4 8.0 %collective-permute-start.15 = (bf16[256,256]{1,0:T(8,128)(2,1)S(1)}, bf16[256,256]{1,0:T(8,128)(2,1)S(1)}, u32[]{:S(2)}, u32[]{:S(2)}) collective-permute-start(bf16[256,256]{1,0:T(8,128)(2,1)S(1)} %get-tuple-element.34), channel_id=1, source_target_pairs={{0,14},{1,3},{2,0},{3,5},{4,2},{5,7},{6,4},{7,9},{8,6},{9,11},{10,... | collective-permute-start | bytes 393224 | tf_op jit(solution)/shard_map/ppermute | solution.py:49
  82.3 5.1 %collective-permute-start.23 = (bf16[256,256]{1,0:T(8,128)(2,1)S(1)}, bf16[256,256]{1,0:T(8,128)(2,1)S(1)}, u32[]{:S(2)}, u32[]{:S(2)}) collective-permute-start(bf16[256,256]{1,0:T(8,128)(2,1)S(1)} %get-tuple-element.44), channel_id=1, source_target_pairs={{0,4},{1,13},{2,6},{3,15},{4,8},{5,1},{6,10},{7,3},{8,12},{9,5},{1... | collective-permute-start | bytes 393224 | tf_op jit(solution)/shard_map/ppermute | solution.py:49
  83.0 7.9 %collective-permute-start.24 = (bf16[256,256]{1,0:T(8,128)(2,1)S(1)}, bf16[256,256]{1,0:T(8,128)(2,1)S(1)}, u32[]{:S(2)}, u32[]{:S(2)}) collective-permute-start(bf16[256,256]{1,0:T(8,128)(2,1)S(1)} %get-tuple-element.45), channel_id=1, source_target_pairs={{0,14},{1,3},{2,0},{3,5},{4,2},{5,7},{6,4},{7,9},{8,6},{9,11},{10,... | collective-permute-start | bytes 393224 | tf_op jit(solution)/shard_map/ppermute | solution.py:49
  84.4 8.1 %collective-permute-start.16 = (bf16[256,256]{1,0:T(8,128)(2,1)S(1)}, bf16[256,256]{1,0:T(8,128)(2,1)S(1)}, u32[]{:S(2)}, u32[]{:S(2)}) collective-permute-start(bf16[256,256]{1,0:T(8,128)(2,1)S(1)} %get-tuple-element.35), channel_id=1, source_target_pairs={{0,4},{1,13},{2,6},{3,15},{4,8},{5,1},{6,10},{7,3},{8,12},{9,5},{1... | collective-permute-start | bytes 393224 | tf_op jit(solution)/shard_map/ppermute | solution.py:49
  85.8 8.4 %collective-permute-start.17 = (bf16[256,256]{1,0:T(8,128)(2,1)S(1)}, bf16[256,256]{1,0:T(8,128)(2,1)S(1)}, u32[]{:S(2)}, u32[]{:S(2)}) collective-permute-start(bf16[256,256]{1,0:T(8,128)(2,1)S(1)} %get-tuple-element.36), channel_id=1, source_target_pairs={{0,14},{1,3},{2,0},{3,5},{4,2},{5,7},{6,4},{7,9},{8,6},{9,11},{10,... | collective-permute-start | bytes 393224 | tf_op jit(solution)/shard_map/ppermute | solution.py:49
  91.0 4.8 %collective-permute-start.25 = (bf16[256,256]{1,0:T(8,128)(2,1)S(1)}, bf16[256,256]{1,0:T(8,128)(2,1)S(1)}, u32[]{:S(2)}, u32[]{:S(2)}) collective-permute-start(bf16[256,256]{1,0:T(8,128)(2,1)S(1)} %get-tuple-element.46), channel_id=1, source_target_pairs={{0,2},{1,15},{2,4},{3,1},{4,6},{5,3},{6,8},{7,5},{8,10},{9,7},{10,... | collective-permute-start | bytes 393224 | tf_op jit(solution)/shard_map/ppermute | solution.py:49
  92.5 6.5 %collective-permute-start.26 = (bf16[256,256]{1,0:T(8,128)(2,1)S(1)}, bf16[256,256]{1,0:T(8,128)(2,1)S(1)}, u32[]{:S(2)}, u32[]{:S(2)}) collective-permute-start(bf16[256,256]{1,0:T(8,128)(2,1)S(1)} %get-tuple-element.47), channel_id=1, source_target_pairs={{0,14},{1,3},{2,0},{3,5},{4,2},{5,7},{6,4},{7,9},{8,6},{9,11},{10,... | collective-permute-start | bytes 393224 | tf_op jit(solution)/shard_map/ppermute | solution.py:49
  94.2 5.0 %collective-permute-start.18 = (bf16[256,256]{1,0:T(8,128)(2,1)S(1)}, bf16[256,256]{1,0:T(8,128)(2,1)S(1)}, u32[]{:S(2)}, u32[]{:S(2)}) collective-permute-start(bf16[256,256]{1,0:T(8,128)(2,1)S(1)} %get-tuple-element.37), channel_id=1, source_target_pairs={{0,2},{1,15},{2,4},{3,1},{4,6},{5,3},{6,8},{7,5},{8,10},{9,7},{10,... | collective-permute-start | bytes 393224 | tf_op jit(solution)/shard_map/ppermute | solution.py:49
  95.7 6.4 %collective-permute-start.19 = (bf16[256,256]{1,0:T(8,128)(2,1)S(1)}, bf16[256,256]{1,0:T(8,128)(2,1)S(1)}, u32[]{:S(2)}, u32[]{:S(2)}) collective-permute-start(bf16[256,256]{1,0:T(8,128)(2,1)S(1)} %get-tuple-element.38), channel_id=1, source_target_pairs={{0,14},{1,3},{2,0},{3,5},{4,2},{5,7},{6,4},{7,9},{8,6},{9,11},{10,... | collective-permute-start | bytes 393224 | tf_op jit(solution)/shard_map/ppermute | solution.py:49

commit v5 on v4

--- a/solution.py
+++ b/solution.py
@@ -107,7 +107,7 @@
     )(pltpu.with_memory_space_constraint(blocks, pltpu.HBM), *lines)
 
 
-def couple_kernel(size, start, goes_on, sends, count, chosen, source_slot, target_slot, blocks, *refs):
+def couple_kernel(turn, size, start, goes_on, sends, picked, blocks, *refs):
     pieces = refs[:size]
     refs = refs[size + goes_on :]
     total, sources, sems = refs[0], refs[-2], refs[-1]
@@ -126,46 +126,49 @@
 
     def products(group, carry):
         for j in range(STEP):
-            index = group * STEP + j
-            product = jnp.dot(blocks[chosen[index]], sources[source_slot[index]], preferred_element_type=F32)
-            total[target_slot[index]] += product
+            entry = picked[turn, group * STEP + j]
+            block, source, target = entry >> 11, (entry >> 5) & 63, 16 - (entry & 31)
+            total[target] += jnp.dot(blocks[block], sources[source], preferred_element_type=F32)
         return carry
 
-    lax.fori_loop(0, (count[0] + STEP - 1) // STEP, products, 0)
+    def more(group):
+        return (group < blocks.shape[0] // STEP) & (picked[turn, jnp.minimum(group * STEP, blocks.shape[0] - 1)] != 0)
+
+    lax.while_loop(more, lambda group: products(group, group + 1), 0)
     if sends:
         refs[1][...] = total[8:16].astype(BF16)
 
 
-def couple(picked, blocks, pieces, start, width, before=None, sends=True):
+def couple(turn, picked, blocks, pieces, start, width, before=None, sends=True):
     count, rows, _ = blocks.shape
     goes_on = before is not None
     in_vmem = [pltpu.with_memory_space_constraint(value, pltpu.VMEM) for value in ([blocks, before] if goes_on else [blocks])]
     return pl.pallas_call(
-        functools.partial(couple_kernel, len(pieces), start, int(goes_on), sends),
+        functools.partial(couple_kernel, turn, len(pieces), start, int(goes_on), sends),
         out_shape=[pltpu.VMEM((17, rows, width), F32)] + [shape((8, rows, width))] * sends,
-        in_specs=[whole(pltpu.SMEM)] * 4 + [whole()] + [whole(pl.ANY)] * len(pieces) + [whole()] * goes_on,
+        in_specs=[whole(pltpu.SMEM)] + [whole()] + [whole(pl.ANY)] * len(pieces) + [whole()] * goes_on,
         out_specs=[whole()] * (1 + sends),
         scratch_shapes=[
             pltpu.VMEM((sum(piece.shape[0] for piece in pieces), rows, width), BF16),
             pltpu.SemaphoreType.DMA((len(pieces),)),
         ],
-        input_output_aliases={5 + len(pieces): 0} if goes_on else {},
+        input_output_aliases={2 + len(pieces): 0} if goes_on else {},
         compiler_params=params(16),
         cost_estimate=pl.CostEstimate(
             flops=2 * count * rows * rows * width, bytes_accessed=2 * count * rows * rows, transcendentals=0
         ),
-    )(*picked, in_vmem[0], *pieces, *in_vmem[1:])
-
-
-def pick(wanted, source_slot, target_slot):
-    size = wanted.shape[0]
+    )(picked, in_vmem[0], *pieces, *in_vmem[1:])
+
+
+def pick(turn, turns, source_slot, target_slot):
+    size = turn.shape[0]
     index = jnp.arange(size, dtype=jnp.int32)
-    place = jnp.cumsum(wanted.astype(jnp.int32)) - 1
-    hits = wanted[None, :] & (place[None, :] == index[:, None])
-    gathered = lambda values: jnp.sum(jnp.where(hits, values[None, :], 0), axis=1, dtype=jnp.int32)
-    found = jnp.sum(wanted, dtype=jnp.int32)
-    target = jnp.where(index < found, gathered(target_slot), 16)
-    return found.reshape(1), gathered(index), gathered(source_slot), target
+    wanted = turn[None, :] == jnp.arange(turns, dtype=jnp.int32)[:, None]
+    before = index[None, :] < index[:, None]
+    place = jnp.sum(wanted[:, None, :] & before[None], axis=2, dtype=jnp.int32)
+    hits = wanted[:, None, :] & (place[:, None, :] == index[None, :, None])
+    packed = (index * 64 + source_slot) * 32 + (16 - target_slot)
+    return jnp.sum(jnp.where(hits, packed[None, None, :], 0), axis=2, dtype=jnp.int32)
 
 
 ORDER = (4, 2, 5, 3, 6, 1, 7, 0)
@@ -271,11 +274,7 @@
     across = 3 * q + near - 1
     first_slot = jnp.where(from_y == 0, 2 * from_x, jnp.where(from_x == 0, 6 + 2 * from_y, 0)) + q
     turn = jnp.where(first_phase | (distant == 3), 0, distant)
-    picked = [
-        pick(turn == 0, jnp.where(first_phase, first_slot, 14 + across), target_slot),
-        pick(turn == 1, across, target_slot),
-        pick(turn == 2, across, target_slot),
-    ]
+    picked = pick(turn, 3, jnp.where(first_phase, first_slot, jnp.where(turn == 0, 14, 0) + across), target_slot)
 
     solved_one = solve_one(rhs_one[0, 0], inv_one[0, 0])
     axes = ("x", "y")
@@ -293,14 +292,14 @@
     far = [move(fwd[q], axes[1 - q], 1) for q in both]
 
     whole_width = rhs_two.shape[4]
-    (early,) = couple(picked[0], factor, pieces + fwd, 0, whole_width, sends=False)
-    early, send = couple(picked[1], factor, bwd, 0, whole_width, before=early)
+    (early,) = couple(0, picked, factor, pieces + fwd, 0, whole_width, sends=False)
+    early, send = couple(1, picked, factor, bwd, 0, whole_width, before=early)
     early_other = swap_cores(send)
     width = whole_width // PARTS
     solved_two = []
     for i in range(PARTS):
         start = i * width
-        keep, send = couple(picked[2], factor, far, start, width)
+        keep, send = couple(2, picked, factor, far, start, width)
         held, fwd, bwd = reduce_along_z(start, early, early_other, keep, swap_cores(send))
         kernel = functools.partial(last_kernel, start)
         solved_two = call(

time: 103 us -> 101 us (0.981)
  the two profiles are of different devices: /device:TPU:7 before, /device:TPU:1 now
where the time goes in v5:
time: 101 us; the launch traced here: 99 us
  starting transfers between devices  48.4 us (48%)
  waiting for transfers between devices  25.1 us (25%)
  Pallas kernels  22.2 us (22%)
  other arithmetic  1.22 us (1%)
  local copies, waits for them, and re-layouts  1.21 us (1%)
    ppermute x24, starting transfers between devices, move(): return lax.ppermute(value, BOTH, ring_pairs(axis, steps))  41 us
    ppermute x24, waiting for transfers between devices, move(): return lax.ppermute(value, BOTH, ring_pairs(axis, steps))  24.7 us
    pallas_call x4, Pallas kernels, couple(): pl.pallas_call(functools.partial(couple_kernel, turn, len(pieces), start,...  12.7 us
    ppermute x3, starting transfers between devices, swap_cores(): return lax.ppermute(value, 'col', [(i, i ^ 1) for i in range(16)])  7.39 us
    pallas_call x1, Pallas kernels, stage(): pl.pallas_call(stage_kernel, out_shape=[pltpu.VMEM(blocks.shape, blocks.d...  4.26 us
    pallas_call x1, Pallas kernels, solve_one(): pl.pallas_call(solve_one_kernel, out_shape=shape(rhs.shape), in_specs=[wh...  2.27 us
    pallas_call x8, Pallas kernels, call(): pl.pallas_call(kernel, out_shape=outs, in_specs=[whole()] * len(args), ou...  2.21 us
  transfers between devices with their start and end apart: 27, of which 15 were waited for; matrix products, arithmetic and copies ran while one was open for 1% of the time, Pallas kernels for 19%

profile of v5, /device:TPU:1, one launch (start us, length us, event | category | flops | bytes accessed | tf_op | source)
XLA Modules:
  0.0 99.0 jit_solution(17048879628155805927)
XLA Ops:
  0.6 0.0 copy-start.4
  0.7 2.3 %shard_map.95.value.refs_0_ = bf16[2,256,512]{2,1,0:T(8,128)(2,1)} custom-call(bf16[2,256,512]{2,1,0:T(8,128)(2,1)} %bitcast.67, bf16[2,256,256]{2,1,0:T(8,128)(2,1)} %bitcast.68), custom_call_target="tpu_custom_call" | custom-call | tf_op jit(solution)/shard_map/pallas_call | solution.py:70
  2.9 3.6 %collective-permute-start.4 = (bf16[2,256,512]{2,1,0:T(8,128)(2,1)}, bf16[2,256,512]{2,1,0:T(8,128)(2,1)S(1)}, u32[]{:S(2)}, u32[]{:S(2)}) collective-permute-start(bf16[2,256,512]{2,1,0:T(8,128)(2,1)} %shard_map.95.value.refs_0_), channel_id=1, source_target_pairs={{0,64},{1,193},{2,66},{3,195},{4,68},{5,197},{6,70},{7,199},{8,72}... | collective-permute-start | bytes 1572872 | tf_op jit(solution)/shard_map/ppermute | solution.py:49
  6.6 2.5 %collective-permute-start.1 = (bf16[2,256,512]{2,1,0:T(8,128)(2,1)}, bf16[2,256,512]{2,1,0:T(8,128)(2,1)S(1)}, u32[]{:S(2)}, u32[]{:S(2)}) collective-permute-start(bf16[2,256,512]{2,1,0:T(8,128)(2,1)} %shard_map.95.value.refs_0_), channel_id=1, source_target_pairs={{0,16},{1,49},{2,18},{3,51},{4,20},{5,53},{6,22},{7,55},{8,24},{9,... | collective-permute-start | bytes 1572872 | tf_op jit(solution)/shard_map/ppermute | solution.py:49
  9.1 1.1 %copy-done = bf16[2,256,512]{2,1,0:T(8,128)(2,1)S(1)} copy-done((bf16[2,256,512]{2,1,0:T(8,128)(2,1)S(1)}, bf16[2,256,512]{2,1,0:T(8,128)(2,1)}, u32[]{:S(2)}) %copy-start) | copy-done | bytes 524312
  10.1 0.8 shard_map.96
  10.9 0.1 collective-permute-start.3
  11.0 0.1 collective-permute-start
  11.1 2.4 %collective-permute-done.4.refs_6_ = bf16[2,256,512]{2,1,0:T(8,128)(2,1)S(1)} collective-permute-done((bf16[2,256,512]{2,1,0:T(8,128)(2,1)}, bf16[2,256,512]{2,1,0:T(8,128)(2,1)S(1)}, u32[]{:S(2)}, u32[]{:S(2)}) %collective-permute-start.4) | collective-permute-done | bytes 524320 | tf_op jit(solution)/shard_map/ppermute | solution.py:49
  13.5 3.3 %collective-permute-start.5 = (bf16[2,256,512]{2,1,0:T(8,128)(2,1)S(1)}, bf16[2,256,512]{2,1,0:T(8,128)(2,1)S(1)}, u32[]{:S(2)}, u32[]{:S(2)}) collective-permute-start(bf16[2,256,512]{2,1,0:T(8,128)(2,1)S(1)} %collective-permute-done.4.refs_6_), channel_id=1, source_target_pairs={{0,64},{1,193},{2,66},{3,195},{4,68},{5,197},{6,70},{7,199},{8,72}... | collective-permute-start | bytes 1572872 | tf_op jit(solution)/shard_map/ppermute | solution.py:49
  16.8 2.1 %collective-permute-start.2 = (bf16[2,256,512]{2,1,0:T(8,128)(2,1)S(1)}, bf16[2,256,512]{2,1,0:T(8,128)(2,1)S(1)}, u32[]{:S(2)}, u32[]{:S(2)}) collective-permute-start(bf16[2,256,512]{2,1,0:T(8,128)(2,1)S(1)} %collective-permute-done.1.refs_3_), channel_id=1, source_target_pairs={{0,16},{1,49},{2,18},{3,51},{4,20},{5,53},{6,22},{7,55},{8,24},{9,... | collective-permute-start | bytes 1572872 | tf_op jit(solution)/shard_map/ppermute | solution.py:49
  18.9 0.7 or_select_fusion.1
  19.6 2.2 %collective-permute-done.3.refs_4_ = bf16[2,256,512]{2,1,0:T(8,128)(2,1)S(1)} collective-permute-done((bf16[2,256,512]{2,1,0:T(8,128)(2,1)}, bf16[2,256,512]{2,1,0:T(8,128)(2,1)S(1)}, u32[]{:S(2)}, u32[]{:S(2)}) %collective-permute-start.3) | collective-permute-done | bytes 524320 | tf_op jit(solution)/shard_map/ppermute | solution.py:49
  21.8 0.1 collective-permute-done.refs_1_
  21.9 2.3 %collective-permute-done.5.refs_5_ = bf16[2,256,512]{2,1,0:T(8,128)(2,1)S(1)} collective-permute-done((bf16[2,256,512]{2,1,0:T(8,128)(2,1)S(1)}, bf16[2,256,512]{2,1,0:T(8,128)(2,1)S(1)}, u32[]{:S(2)}, u32[]{:S(2)}) %collective-permute-start.5) | collective-permute-done | bytes 524320 | tf_op jit(solution)/shard_map/ppermute | solution.py:49
  24.2 0.1 pad_maximum_fusion.1.second_line
  24.3 2.6 %collective-permute-start.9 = (bf16[3,256,512]{2,1,0:T(8,128)(2,1)S(1)}, bf16[3,256,512]{2,1,0:T(8,128)(2,1)S(1)}, u32[]{:S(2)}, u32[]{:S(2)}) collective-permute-start(bf16[3,256,512]{2,1,0:T(8,128)(2,1)S(1)} %pad_maximum_fusion.1.second_line), channel_id=1, source_target_pairs={{0,16},{1,49},{2,18},{3,51},{4,20},{5,53},{6,22},{7,55},{8,24},{9,... | collective-permute-start | bytes 2359304 | tf_op jit(solution)/shard_map/ppermute | solution.py:49
  26.9 0.1 pad_maximum_fusion.first_line
  27.0 3.2 %collective-permute-start.8 = (bf16[3,256,512]{2,1,0:T(8,128)(2,1)S(1)}, bf16[3,256,512]{2,1,0:T(8,128)(2,1)S(1)}, u32[]{:S(2)}, u32[]{:S(2)}) collective-permute-start(bf16[3,256,512]{2,1,0:T(8,128)(2,1)S(1)} %pad_maximum_fusion.first_line), channel_id=1, source_target_pairs={{0,64},{1,193},{2,66},{3,195},{4,68},{5,197},{6,70},{7,199},{8,72}... | collective-permute-start | bytes 2359304 | tf_op jit(solution)/shard_map/ppermute | solution.py:49
  30.2 0.0 copy-start.1
  30.2 4.3 %shard_map.97 = (bf16[80,256,256]{2,1,0:T(8,128)(2,1)S(1)}, bf16[3,256,512]{2,1,0:T(8,128)(2,1)S(1)}, bf16[3,256,512]{2,1,0:T(8,128)(2,1)S(1)}) custom-call(bf16[80,256,256]{2,1,0:T(8,128)(2,1)} %bitcast.66, bf16[3,256,512]{2,1,0:T(8,128)(2,1)S(1)} %pad_maximum_fusion.first_line, bf16[3,256,512]{2,1,0:T(8,128)(2,1)S(1)} %pad_maximum_fusion.1.second_line), custom_call_target="tpu_custom_call" | custom-call | tf_op jit(solution)/shard_map/pallas_call | solution.py:100
  34.5 0.1 collective-permute-start.6
  34.6 0.1 collective-permute-start.7
  34.7 0.1 convert_reduce_fusion
  34.8 0.2 select_reduce_fusion.picked
  35.0 0.8 collective-permute-done.9.refs_8_
  35.8 3.4 %collective-permute-start.12 = (bf16[3,256,512]{2,1,0:T(8,128)(2,1)S(1)}, bf16[3,256,512]{2,1,0:T(8,128)(2,1)S(1)}, u32[]{:S(2)}, u32[]{:S(2)}) collective-permute-start(bf16[3,256,512]{2,1,0:T(8,128)(2,1)S(1)} %collective-permute-done.9.refs_8_), channel_id=1, source_target_pairs={{0,16},{1,49},{2,18},{3,51},{4,20},{5,53},{6,22},{7,55},{8,24},{9,... | collective-permute-start | bytes 2359304 | tf_op jit(solution)/shard_map/ppermute | solution.py:49
  39.2 0.6 collective-permute-done.8.refs_7_
  39.8 3.4 %collective-permute-start.11 = (bf16[3,256,512]{2,1,0:T(8,128)(2,1)S(1)}, bf16[3,256,512]{2,1,0:T(8,128)(2,1)S(1)}, u32[]{:S(2)}, u32[]{:S(2)}) collective-permute-start(bf16[3,256,512]{2,1,0:T(8,128)(2,1)S(1)} %collective-permute-done.8.refs_7_), channel_id=1, source_target_pairs={{0,64},{1,193},{2,66},{3,195},{4,68},{5,197},{6,70},{7,199},{8,72}... | collective-permute-start | bytes 2359304 | tf_op jit(solution)/shard_map/ppermute | solution.py:49
  43.2 6.8 %shard_map.98.refs_2_ = f32[17,256,512]{2,1,0:T(8,128)S(1)} custom-call(s32[3,80]{1,0:T(4,128)S(1)} %select_reduce_fusion.picked, bf16[80,256,256]{2,1,0:T(8,128)(2,1)S(1)} %get-tuple-element.25.blocks, bf16[2,256,512]{2,1,0:T(8,128)(2,1)S(1)} %copy-done.1, bf16[2,256,512]{2,1,0:T(8,128)(2,1)S(1)} %collective-permute-done.refs_1_, ...), custom_call_target="tpu_custom_call" | custom-call | flops 5368709120 | bytes 10485760 | tf_op jit(solution)/shard_map/pallas_call | solution.py:146
  50.0 1.2 %collective-permute-done.6.refs_0_ = bf16[3,256,512]{2,1,0:T(8,128)(2,1)S(1)} collective-permute-done((bf16[3,256,512]{2,1,0:T(8,128)(2,1)S(1)}, bf16[3,256,512]{2,1,0:T(8,128)(2,1)S(1)}, u32[]{:S(2)}, u32[]{:S(2)}) %collective-permute-start.6) | collective-permute-done | bytes 786464 | tf_op jit(solution)/shard_map/ppermute | solution.py:49
  51.2 2.2 %shard_map.99 = (f32[17,256,512]{2,1,0:T(8,128)S(1)}, bf16[8,256,512]{2,1,0:T(8,128)(2,1)S(1)}) custom-call(s32[3,80]{1,0:T(4,128)S(1)} %select_reduce_fusion.picked, bf16[80,256,256]{2,1,0:T(8,128)(2,1)S(1)} %get-tuple-element.25.blocks, bf16[3,256,512]{2,1,0:T(8,128)(2,1)S(1)} %collective-permute-done.6.refs_0_, ...), custom_call_target="tpu_custom_call", output_to_operand_aliasing={{0}: (4, {})} | custom-call | flops 5368709120 | bytes 10485760 | tf_op jit(solution)/shard_map/pallas_call | solution.py:146
  53.4 5.8 %collective-permute-start.10 = (bf16[8,256,512]{2,1,0:T(8,128)(2,1)S(1)}, bf16[8,256,512]{2,1,0:T(8,128)(2,1)S(1)}, u32[]{:S(2)}, u32[]{:S(2)}) collective-permute-start(bf16[8,256,512]{2,1,0:T(8,128)(2,1)S(1)} %get-tuple-element.29), channel_id=1, source_target_pairs={{0,1},{1,0},{2,3},{3,2},{4,5},{5,4},{6,7},{7,6},{8,9},{9,8},{10,11... | collective-permute-start | bytes 6291464 | tf_op jit(solution)/shard_map/ppermute | solution.py:53
  59.2 1.9 %shard_map.104 = (f32[17,256,256]{2,1,0:T(8,128)S(1)}, bf16[8,256,256]{2,1,0:T(8,128)(2,1)S(1)}) custom-call(s32[3,80]{1,0:T(4,128)S(1)} %select_reduce_fusion.picked, bf16[80,256,256]{2,1,0:T(8,128)(2,1)S(1)} %get-tuple-element.25.blocks, bf16[3,256,512]{2,1,0:T(8,128)(2,1)S(1)} %collective-permute-done.11.refs_0_, ...), custom_call_target="tpu_custom_call" | custom-call | flops 2684354560 | bytes 10485760 | tf_op jit(solution)/shard_map/pallas_call | solution.py:146
  61.1 1.5 %collective-permute-start.20 = (bf16[8,256,256]{2,1,0:T(8,128)(2,1)S(1)}, bf16[8,256,256]{2,1,0:T(8,128)(2,1)S(1)}, u32[]{:S(2)}, u32[]{:S(2)}) collective-permute-start(bf16[8,256,256]{2,1,0:T(8,128)(2,1)S(1)} %get-tuple-element.40), channel_id=1, source_target_pairs={{0,1},{1,0},{2,3},{3,2},{4,5},{5,4},{6,7},{7,6},{8,9},{9,8},{10,11... | collective-permute-start | bytes 3145736 | tf_op jit(solution)/shard_map/ppermute | solution.py:53
  62.6 1.8 %shard_map.100 = (f32[17,256,256]{2,1,0:T(8,128)S(1)}, bf16[8,256,256]{2,1,0:T(8,128)(2,1)S(1)}) custom-call(s32[3,80]{1,0:T(4,128)S(1)} %select_reduce_fusion.picked, bf16[80,256,256]{2,1,0:T(8,128)(2,1)S(1)} %get-tuple-element.25.blocks, bf16[3,256,512]{2,1,0:T(8,128)(2,1)S(1)} %collective-permute-done.11.refs_0_, ...), custom_call_target="tpu_custom_call" | custom-call | flops 2684354560 | bytes 10485760 | tf_op jit(solution)/shard_map/pallas_call | solution.py:146
  64.4 0.1 collective-permute-start.13
  64.5 0.4 collective-permute-done.20.other
  64.9 0.5 shard_map.105
  65.4 5.9 %collective-permute-start.21 = (bf16[2,256,256]{2,1,0:T(8,128)(2,1)S(1)}, bf16[2,256,256]{2,1,0:T(8,128)(2,1)S(1)}, u32[]{:S(2)}, u32[]{:S(2)}) collective-permute-start(bf16[2,256,256]{2,1,0:T(8,128)(2,1)S(1)} %get-tuple-element.42), channel_id=1, source_target_pairs={{0,2},{1,15},{2,4},{3,1},{4,6},{5,3},{6,8},{7,5},{8,10},{9,7},{10,... | collective-permute-start | bytes 786440 | tf_op jit(solution)/shard_map/ppermute | solution.py:49
  71.2 0.4 shard_map.101
  71.6 0.0 copy-start.2
  71.6 0.0 copy-start.3
  71.6 1.4 %collective-permute-start.14 = (bf16[2,256,256]{2,1,0:T(8,128)(2,1)S(1)}, bf16[2,256,256]{2,1,0:T(8,128)(2,1)S(1)}, u32[]{:S(2)}, u32[]{:S(2)}) collective-permute-start(bf16[2,256,256]{2,1,0:T(8,128)(2,1)S(1)} %get-tuple-element.33), channel_id=1, source_target_pairs={{0,2},{1,15},{2,4},{3,1},{4,6},{5,3},{6,8},{7,5},{8,10},{9,7},{10,... | collective-permute-start | bytes 786440 | tf_op jit(solution)/shard_map/ppermute | solution.py:49
  73.0 0.1 collective-permute-start.22
  73.2 0.0 collective-permute-start.15
  73.2 6.6 %collective-permute-done.22.bwd = bf16[256,256]{1,0:T(8,128)(2,1)S(1)} collective-permute-done((bf16[256,256]{1,0:T(8,128)(2,1)S(1)}, bf16[256,256]{1,0:T(8,128)(2,1)S(1)}, u32[]{:S(2)}, u32[]{:S(2)}) %collective-permute-start.22) | collective-permute-done | bytes 131104 | tf_op jit(solution)/shard_map/ppermute | solution.py:49
  79.9 1.3 %collective-permute-start.23 = (bf16[256,256]{1,0:T(8,128)(2,1)S(1)}, bf16[256,256]{1,0:T(8,128)(2,1)S(1)}, u32[]{:S(2)}, u32[]{:S(2)}) collective-permute-start(bf16[256,256]{1,0:T(8,128)(2,1)S(1)} %get-tuple-element.44), channel_id=1, source_target_pairs={{0,4},{1,13},{2,6},{3,15},{4,8},{5,1},{6,10},{7,3},{8,12},{9,5},{1... | collective-permute-start | bytes 393224 | tf_op jit(solution)/shard_map/ppermute | solution.py:49
  81.2 0.4 collective-permute-start.24
  81.7 2.4 %collective-permute-start.16 = (bf16[256,256]{1,0:T(8,128)(2,1)S(1)}, bf16[256,256]{1,0:T(8,128)(2,1)S(1)}, u32[]{:S(2)}, u32[]{:S(2)}) collective-permute-start(bf16[256,256]{1,0:T(8,128)(2,1)S(1)} %get-tuple-element.35), channel_id=1, source_target_pairs={{0,4},{1,13},{2,6},{3,15},{4,8},{5,1},{6,10},{7,3},{8,12},{9,5},{1... | collective-permute-start | bytes 393224 | tf_op jit(solution)/shard_map/ppermute | solution.py:49
  84.0 1.2 %collective-permute-start.17 = (bf16[256,256]{1,0:T(8,128)(2,1)S(1)}, bf16[256,256]{1,0:T(8,128)(2,1)S(1)}, u32[]{:S(2)}, u32[]{:S(2)}) collective-permute-start(bf16[256,256]{1,0:T(8,128)(2,1)S(1)} %get-tuple-element.36), channel_id=1, source_target_pairs={{0,14},{1,3},{2,0},{3,5},{4,2},{5,7},{6,4},{7,9},{8,6},{9,11},{10,... | collective-permute-start | bytes 393224 | tf_op jit(solution)/shard_map/ppermute | solution.py:49
  85.2 0.1 collective-permute-done.23.fwd
  85.3 1.5 %collective-permute-done.24.bwd = bf16[256,256]{1,0:T(8,128)(2,1)S(1)} collective-permute-done((bf16[256,256]{1,0:T(8,128)(2,1)S(1)}, bf16[256,256]{1,0:T(8,128)(2,1)S(1)}, u32[]{:S(2)}, u32[]{:S(2)}) %collective-permute-start.24) | collective-permute-done | bytes 131104 | tf_op jit(solution)/shard_map/ppermute | solution.py:49
  86.8 0.1 shard_map.107
  86.9 2.4 %collective-permute-start.25 = (bf16[256,256]{1,0:T(8,128)(2,1)S(1)}, bf16[256,256]{1,0:T(8,128)(2,1)S(1)}, u32[]{:S(2)}, u32[]{:S(2)}) collective-permute-start(bf16[256,256]{1,0:T(8,128)(2,1)S(1)} %get-tuple-element.46), channel_id=1, source_target_pairs={{0,2},{1,15},{2,4},{3,1},{4,6},{5,3},{6,8},{7,5},{8,10},{9,7},{10,... | collective-permute-start | bytes 393224 | tf_op jit(solution)/shard_map/ppermute | solution.py:49
  89.3 1.8 %collective-permute-done.17.bwd = bf16[256,256]{1,0:T(8,128)(2,1)S(1)} collective-permute-done((bf16[256,256]{1,0:T(8,128)(2,1)S(1)}, bf16[256,256]{1,0:T(8,128)(2,1)S(1)}, u32[]{:S(2)}, u32[]{:S(2)}) %collective-permute-start.17) | collective-permute-done | bytes 131104 | tf_op jit(solution)/shard_map/ppermute | solution.py:49
  91.1 0.1 shard_map.103
  91.2 1.4 %collective-permute-start.18 = (bf16[256,256]{1,0:T(8,128)(2,1)S(1)}, bf16[256,256]{1,0:T(8,128)(2,1)S(1)}, u32[]{:S(2)}, u32[]{:S(2)}) collective-permute-start(bf16[256,256]{1,0:T(8,128)(2,1)S(1)} %get-tuple-element.37), channel_id=1, source_target_pairs={{0,2},{1,15},{2,4},{3,1},{4,6},{5,3},{6,8},{7,5},{8,10},{9,7},{10,... | collective-permute-start | bytes 393224 | tf_op jit(solution)/shard_map/ppermute | solution.py:49
  92.6 0.1 collective-permute-start.19
  92.7 2.1 %collective-permute-done.26.bwd = bf16[256,256]{1,0:T(8,128)(2,1)S(1)} collective-permute-done((bf16[256,256]{1,0:T(8,128)(2,1)S(1)}, bf16[256,256]{1,0:T(8,128)(2,1)S(1)}, u32[]{:S(2)}, u32[]{:S(2)}) %collective-permute-start.26) | collective-permute-done | bytes 131104 | tf_op jit(solution)/shard_map/ppermute | solution.py:49
  94.9 0.2 shard_map.108.refs_0_
  95.1 1.0 collective-permute-done.18.fwd
  96.0 2.0 %collective-permute-done.19.bwd = bf16[256,256]{1,0:T(8,128)(2,1)S(1)} collective-permute-done((bf16[256,256]{1,0:T(8,128)(2,1)S(1)}, bf16[256,256]{1,0:T(8,128)(2,1)S(1)}, u32[]{:S(2)}, u32[]{:S(2)}) %collective-permute-start.19) | collective-permute-done | bytes 131104 | tf_op jit(solution)/shard_map/ppermute | solution.py:49
  98.1 0.9 shard_map.109
  (31 shorter events, 0.3 us)
Async XLA Ops:
  0.6 29.5 %copy-start.4 = (s32[1,1,80]{2,1,0:T(1,128)S(1)}, s32[1,1,80]{2,1,0:T(1,128)}, u32[]{:S(2)}) copy-start(s32[1,1,80]{2,1,0:T(1,128)} %param.14) | copy-start | bytes 964
  0.6 29.5 %copy-start.5 = (s32[1,1,80]{2,1,0:T(1,128)S(1)}, s32[1,1,80]{2,1,0:T(1,128)}, u32[]{:S(2)}) copy-start(s32[1,1,80]{2,1,0:T(1,128)} %param.13) | copy-start | bytes 964
  2.9 10.6 %collective-permute-start.4 = (bf16[2,256,512]{2,1,0:T(8,128)(2,1)}, bf16[2,256,512]{2,1,0:T(8,128)(2,1)S(1)}, u32[]{:S(2)}, u32[]{:S(2)}) collective-permute-start(bf16[2,256,512]{2,1,0:T(8,128)(2,1)} %shard_map.95.value.refs_0_), channel_id=1, source_target_pairs={{0,64},{1,193},{2,66},{3,195},{4,68},{5,197},{6,70},{7,199},{8,72}... | collective-permute-start | bytes 1572872 | tf_op jit(solution)/shard_map/ppermute | solution.py:49
  6.6 10.2 %collective-permute-start.1 = (bf16[2,256,512]{2,1,0:T(8,128)(2,1)}, bf16[2,256,512]{2,1,0:T(8,128)(2,1)S(1)}, u32[]{:S(2)}, u32[]{:S(2)}) collective-permute-start(bf16[2,256,512]{2,1,0:T(8,128)(2,1)} %shard_map.95.value.refs_0_), channel_id=1, source_target_pairs={{0,16},{1,49},{2,18},{3,51},{4,20},{5,53},{6,22},{7,55},{8,24},{9,... | collective-permute-start | bytes 1572872 | tf_op jit(solution)/shard_map/ppermute | solution.py:49
  9.1 1.1 %copy-start = (bf16[2,256,512]{2,1,0:T(8,128)(2,1)S(1)}, bf16[2,256,512]{2,1,0:T(8,128)(2,1)}, u32[]{:S(2)}) copy-start(bf16[2,256,512]{2,1,0:T(8,128)(2,1)} %shard_map.95.value.refs_0_) | copy-start | bytes 1572868
  10.9 10.8 %collective-permute-start.3 = (bf16[2,256,512]{2,1,0:T(8,128)(2,1)}, bf16[2,256,512]{2,1,0:T(8,128)(2,1)S(1)}, u32[]{:S(2)}, u32[]{:S(2)}) collective-permute-start(bf16[2,256,512]{2,1,0:T(8,128)(2,1)} %shard_map.96), channel_id=1, source_target_pairs={{0,192},{1,65},{2,194},{3,67},{4,196},{5,69},{6,198},{7,71},{8,200... | collective-permute-start | bytes 1572872 | tf_op jit(solution)/shard_map/ppermute | solution.py:49
  11.0 10.8 %collective-permute-start = (bf16[2,256,512]{2,1,0:T(8,128)(2,1)}, bf16[2,256,512]{2,1,0:T(8,128)(2,1)S(1)}, u32[]{:S(2)}, u32[]{:S(2)}) collective-permute-start(bf16[2,256,512]{2,1,0:T(8,128)(2,1)} %shard_map.96), channel_id=1, source_target_pairs={{0,48},{1,17},{2,50},{3,19},{4,52},{5,21},{6,54},{7,23},{8,56},{9,... | collective-permute-start | bytes 1572872 | tf_op jit(solution)/shard_map/ppermute | solution.py:49
  13.5 10.7 %collective-permute-start.5 = (bf16[2,256,512]{2,1,0:T(8,128)(2,1)S(1)}, bf16[2,256,512]{2,1,0:T(8,128)(2,1)S(1)}, u32[]{:S(2)}, u32[]{:S(2)}) collective-permute-start(bf16[2,256,512]{2,1,0:T(8,128)(2,1)S(1)} %collective-permute-done.4.refs_6_), channel_id=1, source_target_pairs={{0,64},{1,193},{2,66},{3,195},{4,68},{5,197},{6,70},{7,199},{8,72}... | collective-permute-start | bytes 1572872 | tf_op jit(solution)/shard_map/ppermute | solution.py:49
  16.8 10.0 %collective-permute-start.2 = (bf16[2,256,512]{2,1,0:T(8,128)(2,1)S(1)}, bf16[2,256,512]{2,1,0:T(8,128)(2,1)S(1)}, u32[]{:S(2)}, u32[]{:S(2)}) collective-permute-start(bf16[2,256,512]{2,1,0:T(8,128)(2,1)S(1)} %collective-permute-done.1.refs_3_), channel_id=1, source_target_pairs={{0,16},{1,49},{2,18},{3,51},{4,20},{5,53},{6,22},{7,55},{8,24},{9,... | collective-permute-start | bytes 1572872 | tf_op jit(solution)/shard_map/ppermute | solution.py:49
  24.3 11.5 %collective-permute-start.9 = (bf16[3,256,512]{2,1,0:T(8,128)(2,1)S(1)}, bf16[3,256,512]{2,1,0:T(8,128)(2,1)S(1)}, u32[]{:S(2)}, u32[]{:S(2)}) collective-permute-start(bf16[3,256,512]{2,1,0:T(8,128)(2,1)S(1)} %pad_maximum_fusion.1.second_line), channel_id=1, source_target_pairs={{0,16},{1,49},{2,18},{3,51},{4,20},{5,53},{6,22},{7,55},{8,24},{9,... | collective-permute-start | bytes 2359304 | tf_op jit(solution)/shard_map/ppermute | solution.py:49
  27.0 12.8 %collective-permute-start.8 = (bf16[3,256,512]{2,1,0:T(8,128)(2,1)S(1)}, bf16[3,256,512]{2,1,0:T(8,128)(2,1)S(1)}, u32[]{:S(2)}, u32[]{:S(2)}) collective-permute-start(bf16[3,256,512]{2,1,0:T(8,128)(2,1)S(1)} %pad_maximum_fusion.first_line), channel_id=1, source_target_pairs={{0,64},{1,193},{2,66},{3,195},{4,68},{5,197},{6,70},{7,199},{8,72}... | collective-permute-start | bytes 2359304 | tf_op jit(solution)/shard_map/ppermute | solution.py:49
  30.2 13.0 %copy-start.1 = (bf16[2,256,512]{2,1,0:T(8,128)(2,1)S(1)}, bf16[2,256,512]{2,1,0:T(8,128)(2,1)}, u32[]{:S(2)}) copy-start(bf16[2,256,512]{2,1,0:T(8,128)(2,1)} %shard_map.95.value.refs_0_) | copy-start | bytes 1572868
  34.5 16.7 %collective-permute-start.6 = (bf16[3,256,512]{2,1,0:T(8,128)(2,1)S(1)}, bf16[3,256,512]{2,1,0:T(8,128)(2,1)S(1)}, u32[]{:S(2)}, u32[]{:S(2)}) collective-permute-start(bf16[3,256,512]{2,1,0:T(8,128)(2,1)S(1)} %get-tuple-element.26), channel_id=1, source_target_pairs={{0,192},{1,65},{2,194},{3,67},{4,196},{5,69},{6,198},{7,71},{8,200... | collective-permute-start | bytes 2359304 | tf_op jit(solution)/shard_map/ppermute | solution.py:49
  34.6 16.6 %collective-permute-start.7 = (bf16[3,256,512]{2,1,0:T(8,128)(2,1)S(1)}, bf16[3,256,512]{2,1,0:T(8,128)(2,1)S(1)}, u32[]{:S(2)}, u32[]{:S(2)}) collective-permute-start(bf16[3,256,512]{2,1,0:T(8,128)(2,1)S(1)} %get-tuple-element.27), channel_id=1, source_target_pairs={{0,48},{1,17},{2,50},{3,19},{4,52},{5,21},{6,54},{7,23},{8,56},{9,... | collective-permute-start | bytes 2359304 | tf_op jit(solution)/shard_map/ppermute | solution.py:49
  35.8 23.4 %collective-permute-start.12 = (bf16[3,256,512]{2,1,0:T(8,128)(2,1)S(1)}, bf16[3,256,512]{2,1,0:T(8,128)(2,1)S(1)}, u32[]{:S(2)}, u32[]{:S(2)}) collective-permute-start(bf16[3,256,512]{2,1,0:T(8,128)(2,1)S(1)} %collective-permute-done.9.refs_8_), channel_id=1, source_target_pairs={{0,16},{1,49},{2,18},{3,51},{4,20},{5,53},{6,22},{7,55},{8,24},{9,... | collective-permute-start | bytes 2359304 | tf_op jit(solution)/shard_map/ppermute | solution.py:49
  39.8 19.4 %collective-permute-start.11 = (bf16[3,256,512]{2,1,0:T(8,128)(2,1)S(1)}, bf16[3,256,512]{2,1,0:T(8,128)(2,1)S(1)}, u32[]{:S(2)}, u32[]{:S(2)}) collective-permute-start(bf16[3,256,512]{2,1,0:T(8,128)(2,1)S(1)} %collective-permute-done.8.refs_7_), channel_id=1, source_target_pairs={{0,64},{1,193},{2,66},{3,195},{4,68},{5,197},{6,70},{7,199},{8,72}... | collective-permute-start | bytes 2359304 | tf_op jit(solution)/shard_map/ppermute | solution.py:49
  53.4 11.5 %collective-permute-start.10 = (bf16[8,256,512]{2,1,0:T(8,128)(2,1)S(1)}, bf16[8,256,512]{2,1,0:T(8,128)(2,1)S(1)}, u32[]{:S(2)}, u32[]{:S(2)}) collective-permute-start(bf16[8,256,512]{2,1,0:T(8,128)(2,1)S(1)} %get-tuple-element.29), channel_id=1, source_target_pairs={{0,1},{1,0},{2,3},{3,2},{4,5},{5,4},{6,7},{7,6},{8,9},{9,8},{10,11... | collective-permute-start | bytes 6291464 | tf_op jit(solution)/shard_map/ppermute | solution.py:53
  61.1 3.8 %collective-permute-start.20 = (bf16[8,256,256]{2,1,0:T(8,128)(2,1)S(1)}, bf16[8,256,256]{2,1,0:T(8,128)(2,1)S(1)}, u32[]{:S(2)}, u32[]{:S(2)}) collective-permute-start(bf16[8,256,256]{2,1,0:T(8,128)(2,1)S(1)} %get-tuple-element.40), channel_id=1, source_target_pairs={{0,1},{1,0},{2,3},{3,2},{4,5},{5,4},{6,7},{7,6},{8,9},{9,8},{10,11... | collective-permute-start | bytes 3145736 | tf_op jit(solution)/shard_map/ppermute | solution.py:53
  64.4 6.8 %collective-permute-start.13 = (bf16[8,256,256]{2,1,0:T(8,128)(2,1)S(1)}, bf16[8,256,256]{2,1,0:T(8,128)(2,1)S(1)}, u32[]{:S(2)}, u32[]{:S(2)}) collective-permute-start(bf16[8,256,256]{2,1,0:T(8,128)(2,1)S(1)} %get-tuple-element.31), channel_id=1, source_target_pairs={{0,1},{1,0},{2,3},{3,2},{4,5},{5,4},{6,7},{7,6},{8,9},{9,8},{10,11... | collective-permute-start | bytes 3145736 | tf_op jit(solution)/shard_map/ppermute | solution.py:53
  65.4 14.5 %collective-permute-start.21 = (bf16[2,256,256]{2,1,0:T(8,128)(2,1)S(1)}, bf16[2,256,256]{2,1,0:T(8,128)(2,1)S(1)}, u32[]{:S(2)}, u32[]{:S(2)}) collective-permute-start(bf16[2,256,256]{2,1,0:T(8,128)(2,1)S(1)} %get-tuple-element.42), channel_id=1, source_target_pairs={{0,2},{1,15},{2,4},{3,1},{4,6},{5,3},{6,8},{7,5},{8,10},{9,7},{10,... | collective-permute-start | bytes 786440 | tf_op jit(solution)/shard_map/ppermute | solution.py:49
  71.6 23.3 %copy-start.2 = (bf16[1,1,1,256,512]{4,3,2,1,0:T(8,128)(2,1)S(1)}, bf16[1,1,1,256,512]{4,3,2,1,0:T(8,128)(2,1)}, u32[]{:S(2)}) copy-start(bf16[1,1,1,256,512]{4,3,2,1,0:T(8,128)(2,1)} %param.10) | copy-start | bytes 786436
  71.6 23.3 %copy-start.3 = (bf16[1,1,1,256,256]{4,3,2,1,0:T(8,128)(2,1)S(1)}, bf16[1,1,1,256,256]{4,3,2,1,0:T(8,128)(2,1)}, u32[]{:S(2)}) copy-start(bf16[1,1,1,256,256]{4,3,2,1,0:T(8,128)(2,1)} %param.11) | copy-start | bytes 393220
  71.6 10.0 %collective-permute-start.14 = (bf16[2,256,256]{2,1,0:T(8,128)(2,1)S(1)}, bf16[2,256,256]{2,1,0:T(8,128)(2,1)S(1)}, u32[]{:S(2)}, u32[]{:S(2)}) collective-permute-start(bf16[2,256,256]{2,1,0:T(8,128)(2,1)S(1)} %get-tuple-element.33), channel_id=1, source_target_pairs={{0,2},{1,15},{2,4},{3,1},{4,6},{5,3},{6,8},{7,5},{8,10},{9,7},{10,... | collective-permute-start | bytes 786440 | tf_op jit(solution)/shard_map/ppermute | solution.py:49
  73.0 6.8 %collective-permute-start.22 = (bf16[256,256]{1,0:T(8,128)(2,1)S(1)}, bf16[256,256]{1,0:T(8,128)(2,1)S(1)}, u32[]{:S(2)}, u32[]{:S(2)}) collective-permute-start(bf16[256,256]{1,0:T(8,128)(2,1)S(1)} %get-tuple-element.43), channel_id=1, source_target_pairs={{0,14},{1,3},{2,0},{3,5},{4,2},{5,7},{6,4},{7,9},{8,6},{9,11},{10,... | collective-permute-start | bytes 393224 | tf_op jit(solution)/shard_map/ppermute | solution.py:49
  73.2 8.4 %collective-permute-start.15 = (bf16[256,256]{1,0:T(8,128)(2,1)S(1)}, bf16[256,256]{1,0:T(8,128)(2,1)S(1)}, u32[]{:S(2)}, u32[]{:S(2)}) collective-permute-start(bf16[256,256]{1,0:T(8,128)(2,1)S(1)} %get-tuple-element.34), channel_id=1, source_target_pairs={{0,14},{1,3},{2,0},{3,5},{4,2},{5,7},{6,4},{7,9},{8,6},{9,11},{10,... | collective-permute-start | bytes 393224 | tf_op jit(solution)/shard_map/ppermute | solution.py:49
  79.9 5.4 %collective-permute-start.23 = (bf16[256,256]{1,0:T(8,128)(2,1)S(1)}, bf16[256,256]{1,0:T(8,128)(2,1)S(1)}, u32[]{:S(2)}, u32[]{:S(2)}) collective-permute-start(bf16[256,256]{1,0:T(8,128)(2,1)S(1)} %get-tuple-element.44), channel_id=1, source_target_pairs={{0,4},{1,13},{2,6},{3,15},{4,8},{5,1},{6,10},{7,3},{8,12},{9,5},{1... | collective-permute-start | bytes 393224 | tf_op jit(solution)/shard_map/ppermute | solution.py:49
  81.2 5.6 %collective-permute-start.24 = (bf16[256,256]{1,0:T(8,128)(2,1)S(1)}, bf16[256,256]{1,0:T(8,128)(2,1)S(1)}, u32[]{:S(2)}, u32[]{:S(2)}) collective-permute-start(bf16[256,256]{1,0:T(8,128)(2,1)S(1)} %get-tuple-element.45), channel_id=1, source_target_pairs={{0,14},{1,3},{2,0},{3,5},{4,2},{5,7},{6,4},{7,9},{8,6},{9,11},{10,... | collective-permute-start | bytes 393224 | tf_op jit(solution)/shard_map/ppermute | solution.py:49
  81.7 7.6 %collective-permute-start.16 = (bf16[256,256]{1,0:T(8,128)(2,1)S(1)}, bf16[256,256]{1,0:T(8,128)(2,1)S(1)}, u32[]{:S(2)}, u32[]{:S(2)}) collective-permute-start(bf16[256,256]{1,0:T(8,128)(2,1)S(1)} %get-tuple-element.35), channel_id=1, source_target_pairs={{0,4},{1,13},{2,6},{3,15},{4,8},{5,1},{6,10},{7,3},{8,12},{9,5},{1... | collective-permute-start | bytes 393224 | tf_op jit(solution)/shard_map/ppermute | solution.py:49
  84.0 7.1 %collective-permute-start.17 = (bf16[256,256]{1,0:T(8,128)(2,1)S(1)}, bf16[256,256]{1,0:T(8,128)(2,1)S(1)}, u32[]{:S(2)}, u32[]{:S(2)}) collective-permute-start(bf16[256,256]{1,0:T(8,128)(2,1)S(1)} %get-tuple-element.36), channel_id=1, source_target_pairs={{0,14},{1,3},{2,0},{3,5},{4,2},{5,7},{6,4},{7,9},{8,6},{9,11},{10,... | collective-permute-start | bytes 393224 | tf_op jit(solution)/shard_map/ppermute | solution.py:49
  86.9 5.8 %collective-permute-start.25 = (bf16[256,256]{1,0:T(8,128)(2,1)S(1)}, bf16[256,256]{1,0:T(8,128)(2,1)S(1)}, u32[]{:S(2)}, u32[]{:S(2)}) collective-permute-start(bf16[256,256]{1,0:T(8,128)(2,1)S(1)} %get-tuple-element.46), channel_id=1, source_target_pairs={{0,2},{1,15},{2,4},{3,1},{4,6},{5,3},{6,8},{7,5},{8,10},{9,7},{10,... | collective-permute-start | bytes 393224 | tf_op jit(solution)/shard_map/ppermute | solution.py:49
  89.3 5.6 %collective-permute-start.26 = (bf16[256,256]{1,0:T(8,128)(2,1)S(1)}, bf16[256,256]{1,0:T(8,128)(2,1)S(1)}, u32[]{:S(2)}, u32[]{:S(2)}) collective-permute-start(bf16[256,256]{1,0:T(8,128)(2,1)S(1)} %get-tuple-element.47), channel_id=1, source_target_pairs={{0,14},{1,3},{2,0},{3,5},{4,2},{5,7},{6,4},{7,9},{8,6},{9,11},{10,... | collective-permute-start | bytes 393224 | tf_op jit(solution)/shard_map/ppermute | solution.py:49
  91.2 4.9 %collective-permute-start.18 = (bf16[256,256]{1,0:T(8,128)(2,1)S(1)}, bf16[256,256]{1,0:T(8,128)(2,1)S(1)}, u32[]{:S(2)}, u32[]{:S(2)}) collective-permute-start(bf16[256,256]{1,0:T(8,128)(2,1)S(1)} %get-tuple-element.37), channel_id=1, source_target_pairs={{0,2},{1,15},{2,4},{3,1},{4,6},{5,3},{6,8},{7,5},{8,10},{9,7},{10,... | collective-permute-start | bytes 393224 | tf_op jit(solution)/shard_map/ppermute | solution.py:49
  92.6 5.5 %collective-permute-start.19 = (bf16[256,256]{1,0:T(8,128)(2,1)S(1)}, bf16[256,256]{1,0:T(8,128)(2,1)S(1)}, u32[]{:S(2)}, u32[]{:S(2)}) collective-permute-start(bf16[256,256]{1,0:T(8,128)(2,1)S(1)} %get-tuple-element.38), channel_id=1, source_target_pairs={{0,14},{1,3},{2,0},{3,5},{4,2},{5,7},{6,4},{7,9},{8,6},{9,11},{10,... | collective-permute-start | bytes 393224 | tf_op jit(solution)/shard_map/ppermute | solution.py:49

commit v6 on v5

--- a/solution.py
+++ b/solution.py
@@ -8,7 +8,7 @@
 from jax.sharding import PartitionSpec as P
 
 PARTS = 2
-STEP = 16
+STEP = 20
 BOTH = ("row", "col")
 MIB = 1024 * 1024
 F32 = jnp.float32

time: 101 us -> 102 us (level)
  the two profiles are of different devices: /device:TPU:1 before, /device:TPU:2 now
where the time goes in v6:
time: 102 us; the launch traced here: 101 us
  starting transfers between devices  44.9 us (44%)
  waiting for transfers between devices  30.4 us (30%)
  Pallas kernels  22.3 us (22%)
  other arithmetic  1.22 us (1%)
  local copies, waits for them, and re-layouts  1.21 us (1%)
    ppermute x24, starting transfers between devices, move(): return lax.ppermute(value, BOTH, ring_pairs(axis, steps))  44.2 us
    ppermute x24, waiting for transfers between devices, move(): return lax.ppermute(value, BOTH, ring_pairs(axis, steps))  30.3 us
    pallas_call x4, Pallas kernels, couple(): pl.pallas_call(functools.partial(couple_kernel, turn, len(pieces), start,...  12.8 us
    pallas_call x1, Pallas kernels, stage(): pl.pallas_call(stage_kernel, out_shape=[pltpu.VMEM(blocks.shape, blocks.d...  4.25 us
    pallas_call x1, Pallas kernels, solve_one(): pl.pallas_call(solve_one_kernel, out_shape=shape(rhs.shape), in_specs=[wh...  2.27 us
    pallas_call x8, Pallas kernels, call(): pl.pallas_call(kernel, out_shape=outs, in_specs=[whole()] * len(args), ou...  2.21 us
  transfers between devices with their start and end apart: 27, of which 12 were waited for; matrix products, arithmetic and copies ran while one was open for 1% of the time, Pallas kernels for 19%

profile of v6, /device:TPU:2, one launch (start us, length us, event | category | flops | bytes accessed | tf_op | source)
XLA Modules:
  0.0 101.0 jit_solution(2203532540928993059)
XLA Ops:
  0.6 0.0 copy-start.4
  0.7 2.3 %shard_map.95.value.refs_0_ = bf16[2,256,512]{2,1,0:T(8,128)(2,1)} custom-call(bf16[2,256,512]{2,1,0:T(8,128)(2,1)} %bitcast.67, bf16[2,256,256]{2,1,0:T(8,128)(2,1)} %bitcast.68), custom_call_target="tpu_custom_call" | custom-call | tf_op jit(solution)/shard_map/pallas_call | solution.py:70
  2.9 1.7 %collective-permute-start.4 = (bf16[2,256,512]{2,1,0:T(8,128)(2,1)}, bf16[2,256,512]{2,1,0:T(8,128)(2,1)S(1)}, u32[]{:S(2)}, u32[]{:S(2)}) collective-permute-start(bf16[2,256,512]{2,1,0:T(8,128)(2,1)} %shard_map.95.value.refs_0_), channel_id=1, source_target_pairs={{0,64},{1,193},{2,66},{3,195},{4,68},{5,197},{6,70},{7,199},{8,72}... | collective-permute-start | bytes 1572872 | tf_op jit(solution)/shard_map/ppermute | solution.py:49
  4.6 1.5 %collective-permute-start.1 = (bf16[2,256,512]{2,1,0:T(8,128)(2,1)}, bf16[2,256,512]{2,1,0:T(8,128)(2,1)S(1)}, u32[]{:S(2)}, u32[]{:S(2)}) collective-permute-start(bf16[2,256,512]{2,1,0:T(8,128)(2,1)} %shard_map.95.value.refs_0_), channel_id=1, source_target_pairs={{0,16},{1,49},{2,18},{3,51},{4,20},{5,53},{6,22},{7,55},{8,24},{9,... | collective-permute-start | bytes 1572872 | tf_op jit(solution)/shard_map/ppermute | solution.py:49
  6.1 1.1 %copy-done = bf16[2,256,512]{2,1,0:T(8,128)(2,1)S(1)} copy-done((bf16[2,256,512]{2,1,0:T(8,128)(2,1)S(1)}, bf16[2,256,512]{2,1,0:T(8,128)(2,1)}, u32[]{:S(2)}) %copy-start) | copy-done | bytes 524312
  7.2 0.8 shard_map.96
  8.0 1.7 %collective-permute-start.3 = (bf16[2,256,512]{2,1,0:T(8,128)(2,1)}, bf16[2,256,512]{2,1,0:T(8,128)(2,1)S(1)}, u32[]{:S(2)}, u32[]{:S(2)}) collective-permute-start(bf16[2,256,512]{2,1,0:T(8,128)(2,1)} %shard_map.96), channel_id=1, source_target_pairs={{0,192},{1,65},{2,194},{3,67},{4,196},{5,69},{6,198},{7,71},{8,200... | collective-permute-start | bytes 1572872 | tf_op jit(solution)/shard_map/ppermute | solution.py:49
  9.7 0.8 collective-permute-start
  10.5 4.8 %collective-permute-done.4.refs_6_ = bf16[2,256,512]{2,1,0:T(8,128)(2,1)S(1)} collective-permute-done((bf16[2,256,512]{2,1,0:T(8,128)(2,1)}, bf16[2,256,512]{2,1,0:T(8,128)(2,1)S(1)}, u32[]{:S(2)}, u32[]{:S(2)}) %collective-permute-start.4) | collective-permute-done | bytes 524320 | tf_op jit(solution)/shard_map/ppermute | solution.py:49
  15.3 2.2 %collective-permute-start.5 = (bf16[2,256,512]{2,1,0:T(8,128)(2,1)S(1)}, bf16[2,256,512]{2,1,0:T(8,128)(2,1)S(1)}, u32[]{:S(2)}, u32[]{:S(2)}) collective-permute-start(bf16[2,256,512]{2,1,0:T(8,128)(2,1)S(1)} %collective-permute-done.4.refs_6_), channel_id=1, source_target_pairs={{0,64},{1,193},{2,66},{3,195},{4,68},{5,197},{6,70},{7,199},{8,72}... | collective-permute-start | bytes 1572872 | tf_op jit(solution)/shard_map/ppermute | solution.py:49
  17.5 0.0 collective-permute-done.1.refs_3_
  17.5 1.5 %collective-permute-start.2 = (bf16[2,256,512]{2,1,0:T(8,128)(2,1)S(1)}, bf16[2,256,512]{2,1,0:T(8,128)(2,1)S(1)}, u32[]{:S(2)}, u32[]{:S(2)}) collective-permute-start(bf16[2,256,512]{2,1,0:T(8,128)(2,1)S(1)} %collective-permute-done.1.refs_3_), channel_id=1, source_target_pairs={{0,16},{1,49},{2,18},{3,51},{4,20},{5,53},{6,22},{7,55},{8,24},{9,... | collective-permute-start | bytes 1572872 | tf_op jit(solution)/shard_map/ppermute | solution.py:49
  19.0 0.7 or_select_fusion.1
  19.7 0.0 collective-permute-done.3.refs_4_
  19.8 0.7 collective-permute-done.refs_1_
  20.5 6.1 %collective-permute-done.5.refs_5_ = bf16[2,256,512]{2,1,0:T(8,128)(2,1)S(1)} collective-permute-done((bf16[2,256,512]{2,1,0:T(8,128)(2,1)S(1)}, bf16[2,256,512]{2,1,0:T(8,128)(2,1)S(1)}, u32[]{:S(2)}, u32[]{:S(2)}) %collective-permute-start.5) | collective-permute-done | bytes 524320 | tf_op jit(solution)/shard_map/ppermute | solution.py:49
  26.6 0.1 pad_maximum_fusion.1.second_line
  26.7 1.5 %collective-permute-start.9 = (bf16[3,256,512]{2,1,0:T(8,128)(2,1)S(1)}, bf16[3,256,512]{2,1,0:T(8,128)(2,1)S(1)}, u32[]{:S(2)}, u32[]{:S(2)}) collective-permute-start(bf16[3,256,512]{2,1,0:T(8,128)(2,1)S(1)} %pad_maximum_fusion.1.second_line), channel_id=1, source_target_pairs={{0,16},{1,49},{2,18},{3,51},{4,20},{5,53},{6,22},{7,55},{8,24},{9,... | collective-permute-start | bytes 2359304 | tf_op jit(solution)/shard_map/ppermute | solution.py:49
  28.3 0.1 pad_maximum_fusion.first_line
  28.4 0.9 collective-permute-start.8
  29.3 0.0 copy-start.1
  29.3 4.3 %shard_map.97 = (bf16[80,256,256]{2,1,0:T(8,128)(2,1)S(1)}, bf16[3,256,512]{2,1,0:T(8,128)(2,1)S(1)}, bf16[3,256,512]{2,1,0:T(8,128)(2,1)S(1)}) custom-call(bf16[80,256,256]{2,1,0:T(8,128)(2,1)} %bitcast.66, bf16[3,256,512]{2,1,0:T(8,128)(2,1)S(1)} %pad_maximum_fusion.first_line, bf16[3,256,512]{2,1,0:T(8,128)(2,1)S(1)} %pad_maximum_fusion.1.second_line), custom_call_target="tpu_custom_call" | custom-call | tf_op jit(solution)/shard_map/pallas_call | solution.py:100
  33.6 2.5 %collective-permute-start.6 = (bf16[3,256,512]{2,1,0:T(8,128)(2,1)S(1)}, bf16[3,256,512]{2,1,0:T(8,128)(2,1)S(1)}, u32[]{:S(2)}, u32[]{:S(2)}) collective-permute-start(bf16[3,256,512]{2,1,0:T(8,128)(2,1)S(1)} %get-tuple-element.26), channel_id=1, source_target_pairs={{0,192},{1,65},{2,194},{3,67},{4,196},{5,69},{6,198},{7,71},{8,200... | collective-permute-start | bytes 2359304 | tf_op jit(solution)/shard_map/ppermute | solution.py:49
  36.1 0.6 collective-permute-start.7
  36.7 0.1 convert_reduce_fusion
  36.8 0.2 select_reduce_fusion.picked
  37.0 5.5 %collective-permute-done.9.refs_8_ = bf16[3,256,512]{2,1,0:T(8,128)(2,1)S(1)} collective-permute-done((bf16[3,256,512]{2,1,0:T(8,128)(2,1)S(1)}, bf16[3,256,512]{2,1,0:T(8,128)(2,1)S(1)}, u32[]{:S(2)}, u32[]{:S(2)}) %collective-permute-start.9) | collective-permute-done | bytes 786464 | tf_op jit(solution)/shard_map/ppermute | solution.py:49
  42.4 2.5 %collective-permute-start.12 = (bf16[3,256,512]{2,1,0:T(8,128)(2,1)S(1)}, bf16[3,256,512]{2,1,0:T(8,128)(2,1)S(1)}, u32[]{:S(2)}, u32[]{:S(2)}) collective-permute-start(bf16[3,256,512]{2,1,0:T(8,128)(2,1)S(1)} %collective-permute-done.9.refs_8_), channel_id=1, source_target_pairs={{0,16},{1,49},{2,18},{3,51},{4,20},{5,53},{6,22},{7,55},{8,24},{9,... | collective-permute-start | bytes 2359304 | tf_op jit(solution)/shard_map/ppermute | solution.py:49
  44.9 2.9 %collective-permute-done.8.refs_7_ = bf16[3,256,512]{2,1,0:T(8,128)(2,1)S(1)} collective-permute-done((bf16[3,256,512]{2,1,0:T(8,128)(2,1)S(1)}, bf16[3,256,512]{2,1,0:T(8,128)(2,1)S(1)}, u32[]{:S(2)}, u32[]{:S(2)}) %collective-permute-start.8) | collective-permute-done | bytes 786464 | tf_op jit(solution)/shard_map/ppermute | solution.py:49
  47.8 1.0 collective-permute-start.11
  48.8 6.4 %shard_map.98.refs_2_ = f32[17,256,512]{2,1,0:T(8,128)S(1)} custom-call(s32[3,80]{1,0:T(4,128)S(1)} %select_reduce_fusion.picked, bf16[80,256,256]{2,1,0:T(8,128)(2,1)S(1)} %get-tuple-element.25.blocks, bf16[2,256,512]{2,1,0:T(8,128)(2,1)S(1)} %copy-done.1, bf16[2,256,512]{2,1,0:T(8,128)(2,1)S(1)} %collective-permute-done.refs_1_, ...), custom_call_target="tpu_custom_call" | custom-call | flops 5368709120 | bytes 10485760 | tf_op jit(solution)/shard_map/pallas_call | solution.py:146
  55.2 2.4 %shard_map.99 = (f32[17,256,512]{2,1,0:T(8,128)S(1)}, bf16[8,256,512]{2,1,0:T(8,128)(2,1)S(1)}) custom-call(s32[3,80]{1,0:T(4,128)S(1)} %select_reduce_fusion.picked, bf16[80,256,256]{2,1,0:T(8,128)(2,1)S(1)} %get-tuple-element.25.blocks, bf16[3,256,512]{2,1,0:T(8,128)(2,1)S(1)} %collective-permute-done.6.refs_0_, ...), custom_call_target="tpu_custom_call", output_to_operand_aliasing={{0}: (4, {})} | custom-call | flops 5368709120 | bytes 10485760 | tf_op jit(solution)/shard_map/pallas_call | solution.py:146
  57.6 0.1 collective-permute-start.10
  57.7 3.3 %collective-permute-done.11.refs_0_ = bf16[3,256,512]{2,1,0:T(8,128)(2,1)S(1)} collective-permute-done((bf16[3,256,512]{2,1,0:T(8,128)(2,1)S(1)}, bf16[3,256,512]{2,1,0:T(8,128)(2,1)S(1)}, u32[]{:S(2)}, u32[]{:S(2)}) %collective-permute-start.11) | collective-permute-done | bytes 786464 | tf_op jit(solution)/shard_map/ppermute | solution.py:49
  61.0 2.0 %shard_map.104 = (f32[17,256,256]{2,1,0:T(8,128)S(1)}, bf16[8,256,256]{2,1,0:T(8,128)(2,1)S(1)}) custom-call(s32[3,80]{1,0:T(4,128)S(1)} %select_reduce_fusion.picked, bf16[80,256,256]{2,1,0:T(8,128)(2,1)S(1)} %get-tuple-element.25.blocks, bf16[3,256,512]{2,1,0:T(8,128)(2,1)S(1)} %collective-permute-done.11.refs_0_, ...), custom_call_target="tpu_custom_call" | custom-call | flops 2684354560 | bytes 10485760 | tf_op jit(solution)/shard_map/pallas_call | solution.py:146
  63.1 0.1 collective-permute-start.20
  63.2 2.0 %shard_map.100 = (f32[17,256,256]{2,1,0:T(8,128)S(1)}, bf16[8,256,256]{2,1,0:T(8,128)(2,1)S(1)}) custom-call(s32[3,80]{1,0:T(4,128)S(1)} %select_reduce_fusion.picked, bf16[80,256,256]{2,1,0:T(8,128)(2,1)S(1)} %get-tuple-element.25.blocks, bf16[3,256,512]{2,1,0:T(8,128)(2,1)S(1)} %collective-permute-done.11.refs_0_, ...), custom_call_target="tpu_custom_call" | custom-call | flops 2684354560 | bytes 10485760 | tf_op jit(solution)/shard_map/pallas_call | solution.py:146
  65.1 0.6 collective-permute-start.13
  65.7 0.1 collective-permute-done.20.other
  65.8 0.5 shard_map.105
  66.3 2.1 %collective-permute-start.21 = (bf16[2,256,256]{2,1,0:T(8,128)(2,1)S(1)}, bf16[2,256,256]{2,1,0:T(8,128)(2,1)S(1)}, u32[]{:S(2)}, u32[]{:S(2)}) collective-permute-start(bf16[2,256,256]{2,1,0:T(8,128)(2,1)S(1)} %get-tuple-element.42), channel_id=1, source_target_pairs={{0,2},{1,15},{2,4},{3,1},{4,6},{5,3},{6,8},{7,5},{8,10},{9,7},{10,... | collective-permute-start | bytes 786440 | tf_op jit(solution)/shard_map/ppermute | solution.py:49
  68.4 0.4 shard_map.101
  68.8 0.0 copy-start.2
  68.8 0.0 copy-start.3
  68.8 1.9 %collective-permute-start.14 = (bf16[2,256,256]{2,1,0:T(8,128)(2,1)S(1)}, bf16[2,256,256]{2,1,0:T(8,128)(2,1)S(1)}, u32[]{:S(2)}, u32[]{:S(2)}) collective-permute-start(bf16[2,256,256]{2,1,0:T(8,128)(2,1)S(1)} %get-tuple-element.33), channel_id=1, source_target_pairs={{0,2},{1,15},{2,4},{3,1},{4,6},{5,3},{6,8},{7,5},{8,10},{9,7},{10,... | collective-permute-start | bytes 786440 | tf_op jit(solution)/shard_map/ppermute | solution.py:49
  70.7 3.7 %collective-permute-start.22 = (bf16[256,256]{1,0:T(8,128)(2,1)S(1)}, bf16[256,256]{1,0:T(8,128)(2,1)S(1)}, u32[]{:S(2)}, u32[]{:S(2)}) collective-permute-start(bf16[256,256]{1,0:T(8,128)(2,1)S(1)} %get-tuple-element.43), channel_id=1, source_target_pairs={{0,14},{1,3},{2,0},{3,5},{4,2},{5,7},{6,4},{7,9},{8,6},{9,11},{10,... | collective-permute-start | bytes 393224 | tf_op jit(solution)/shard_map/ppermute | solution.py:49
  74.4 2.8 %collective-permute-start.15 = (bf16[256,256]{1,0:T(8,128)(2,1)S(1)}, bf16[256,256]{1,0:T(8,128)(2,1)S(1)}, u32[]{:S(2)}, u32[]{:S(2)}) collective-permute-start(bf16[256,256]{1,0:T(8,128)(2,1)S(1)} %get-tuple-element.34), channel_id=1, source_target_pairs={{0,14},{1,3},{2,0},{3,5},{4,2},{5,7},{6,4},{7,9},{8,6},{9,11},{10,... | collective-permute-start | bytes 393224 | tf_op jit(solution)/shard_map/ppermute | solution.py:49
  77.3 1.1 %collective-permute-done.22.bwd = bf16[256,256]{1,0:T(8,128)(2,1)S(1)} collective-permute-done((bf16[256,256]{1,0:T(8,128)(2,1)S(1)}, bf16[256,256]{1,0:T(8,128)(2,1)S(1)}, u32[]{:S(2)}, u32[]{:S(2)}) %collective-permute-start.22) | collective-permute-done | bytes 131104 | tf_op jit(solution)/shard_map/ppermute | solution.py:49
  78.4 3.0 %collective-permute-start.23 = (bf16[256,256]{1,0:T(8,128)(2,1)S(1)}, bf16[256,256]{1,0:T(8,128)(2,1)S(1)}, u32[]{:S(2)}, u32[]{:S(2)}) collective-permute-start(bf16[256,256]{1,0:T(8,128)(2,1)S(1)} %get-tuple-element.44), channel_id=1, source_target_pairs={{0,4},{1,13},{2,6},{3,15},{4,8},{5,1},{6,10},{7,3},{8,12},{9,5},{1... | collective-permute-start | bytes 393224 | tf_op jit(solution)/shard_map/ppermute | solution.py:49
  81.4 1.2 %collective-permute-start.24 = (bf16[256,256]{1,0:T(8,128)(2,1)S(1)}, bf16[256,256]{1,0:T(8,128)(2,1)S(1)}, u32[]{:S(2)}, u32[]{:S(2)}) collective-permute-start(bf16[256,256]{1,0:T(8,128)(2,1)S(1)} %get-tuple-element.45), channel_id=1, source_target_pairs={{0,14},{1,3},{2,0},{3,5},{4,2},{5,7},{6,4},{7,9},{8,6},{9,11},{10,... | collective-permute-start | bytes 393224 | tf_op jit(solution)/shard_map/ppermute | solution.py:49
  82.7 3.2 %collective-permute-start.16 = (bf16[256,256]{1,0:T(8,128)(2,1)S(1)}, bf16[256,256]{1,0:T(8,128)(2,1)S(1)}, u32[]{:S(2)}, u32[]{:S(2)}) collective-permute-start(bf16[256,256]{1,0:T(8,128)(2,1)S(1)} %get-tuple-element.35), channel_id=1, source_target_pairs={{0,4},{1,13},{2,6},{3,15},{4,8},{5,1},{6,10},{7,3},{8,12},{9,5},{1... | collective-permute-start | bytes 393224 | tf_op jit(solution)/shard_map/ppermute | solution.py:49
  85.9 1.2 %collective-permute-start.17 = (bf16[256,256]{1,0:T(8,128)(2,1)S(1)}, bf16[256,256]{1,0:T(8,128)(2,1)S(1)}, u32[]{:S(2)}, u32[]{:S(2)}) collective-permute-start(bf16[256,256]{1,0:T(8,128)(2,1)S(1)} %get-tuple-element.36), channel_id=1, source_target_pairs={{0,14},{1,3},{2,0},{3,5},{4,2},{5,7},{6,4},{7,9},{8,6},{9,11},{10,... | collective-permute-start | bytes 393224 | tf_op jit(solution)/shard_map/ppermute | solution.py:49
  87.1 1.1 %collective-permute-done.23.fwd = bf16[256,256]{1,0:T(8,128)(2,1)S(1)} collective-permute-done((bf16[256,256]{1,0:T(8,128)(2,1)S(1)}, bf16[256,256]{1,0:T(8,128)(2,1)S(1)}, u32[]{:S(2)}, u32[]{:S(2)}) %collective-permute-start.23) | collective-permute-done | bytes 131104 | tf_op jit(solution)/shard_map/ppermute | solution.py:49
  88.2 1.6 %collective-permute-done.24.bwd = bf16[256,256]{1,0:T(8,128)(2,1)S(1)} collective-permute-done((bf16[256,256]{1,0:T(8,128)(2,1)S(1)}, bf16[256,256]{1,0:T(8,128)(2,1)S(1)}, u32[]{:S(2)}, u32[]{:S(2)}) %collective-permute-start.24) | collective-permute-done | bytes 131104 | tf_op jit(solution)/shard_map/ppermute | solution.py:49
  89.9 0.1 shard_map.107
  89.9 1.4 %collective-permute-start.25 = (bf16[256,256]{1,0:T(8,128)(2,1)S(1)}, bf16[256,256]{1,0:T(8,128)(2,1)S(1)}, u32[]{:S(2)}, u32[]{:S(2)}) collective-permute-start(bf16[256,256]{1,0:T(8,128)(2,1)S(1)} %get-tuple-element.46), channel_id=1, source_target_pairs={{0,2},{1,15},{2,4},{3,1},{4,6},{5,3},{6,8},{7,5},{8,10},{9,7},{10,... | collective-permute-start | bytes 393224 | tf_op jit(solution)/shard_map/ppermute | solution.py:49
  91.3 2.0 %collective-permute-start.26 = (bf16[256,256]{1,0:T(8,128)(2,1)S(1)}, bf16[256,256]{1,0:T(8,128)(2,1)S(1)}, u32[]{:S(2)}, u32[]{:S(2)}) collective-permute-start(bf16[256,256]{1,0:T(8,128)(2,1)S(1)} %get-tuple-element.47), channel_id=1, source_target_pairs={{0,14},{1,3},{2,0},{3,5},{4,2},{5,7},{6,4},{7,9},{8,6},{9,11},{10,... | collective-permute-start | bytes 393224 | tf_op jit(solution)/shard_map/ppermute | solution.py:49
  93.2 0.1 shard_map.103
  93.3 1.5 %collective-permute-start.18 = (bf16[256,256]{1,0:T(8,128)(2,1)S(1)}, bf16[256,256]{1,0:T(8,128)(2,1)S(1)}, u32[]{:S(2)}, u32[]{:S(2)}) collective-permute-start(bf16[256,256]{1,0:T(8,128)(2,1)S(1)} %get-tuple-element.37), channel_id=1, source_target_pairs={{0,2},{1,15},{2,4},{3,1},{4,6},{5,3},{6,8},{7,5},{8,10},{9,7},{10,... | collective-permute-start | bytes 393224 | tf_op jit(solution)/shard_map/ppermute | solution.py:49
  94.8 1.9 %collective-permute-start.19 = (bf16[256,256]{1,0:T(8,128)(2,1)S(1)}, bf16[256,256]{1,0:T(8,128)(2,1)S(1)}, u32[]{:S(2)}, u32[]{:S(2)}) collective-permute-start(bf16[256,256]{1,0:T(8,128)(2,1)S(1)} %get-tuple-element.38), channel_id=1, source_target_pairs={{0,14},{1,3},{2,0},{3,5},{4,2},{5,7},{6,4},{7,9},{8,6},{9,11},{10,... | collective-permute-start | bytes 393224 | tf_op jit(solution)/shard_map/ppermute | solution.py:49
  96.6 0.7 collective-permute-done.26.bwd
  97.4 0.2 shard_map.108.refs_0_
  97.6 2.5 %collective-permute-done.18.fwd = bf16[256,256]{1,0:T(8,128)(2,1)S(1)} collective-permute-done((bf16[256,256]{1,0:T(8,128)(2,1)S(1)}, bf16[256,256]{1,0:T(8,128)(2,1)S(1)}, u32[]{:S(2)}, u32[]{:S(2)}) %collective-permute-start.18) | collective-permute-done | bytes 131104 | tf_op jit(solution)/shard_map/ppermute | solution.py:49
  100.1 0.9 shard_map.109
  (31 shorter events, 0.3 us)
Async XLA Ops:
  0.6 28.6 %copy-start.4 = (s32[1,1,80]{2,1,0:T(1,128)S(1)}, s32[1,1,80]{2,1,0:T(1,128)}, u32[]{:S(2)}) copy-start(s32[1,1,80]{2,1,0:T(1,128)} %param.14) | copy-start | bytes 964
  0.6 28.6 %copy-start.5 = (s32[1,1,80]{2,1,0:T(1,128)S(1)}, s32[1,1,80]{2,1,0:T(1,128)}, u32[]{:S(2)}) copy-start(s32[1,1,80]{2,1,0:T(1,128)} %param.13) | copy-start | bytes 964
  2.9 12.4 %collective-permute-start.4 = (bf16[2,256,512]{2,1,0:T(8,128)(2,1)}, bf16[2,256,512]{2,1,0:T(8,128)(2,1)S(1)}, u32[]{:S(2)}, u32[]{:S(2)}) collective-permute-start(bf16[2,256,512]{2,1,0:T(8,128)(2,1)} %shard_map.95.value.refs_0_), channel_id=1, source_target_pairs={{0,64},{1,193},{2,66},{3,195},{4,68},{5,197},{6,70},{7,199},{8,72}... | collective-permute-start | bytes 1572872 | tf_op jit(solution)/shard_map/ppermute | solution.py:49
  4.6 12.9 %collective-permute-start.1 = (bf16[2,256,512]{2,1,0:T(8,128)(2,1)}, bf16[2,256,512]{2,1,0:T(8,128)(2,1)S(1)}, u32[]{:S(2)}, u32[]{:S(2)}) collective-permute-start(bf16[2,256,512]{2,1,0:T(8,128)(2,1)} %shard_map.95.value.refs_0_), channel_id=1, source_target_pairs={{0,16},{1,49},{2,18},{3,51},{4,20},{5,53},{6,22},{7,55},{8,24},{9,... | collective-permute-start | bytes 1572872 | tf_op jit(solution)/shard_map/ppermute | solution.py:49
  6.1 1.1 %copy-start = (bf16[2,256,512]{2,1,0:T(8,128)(2,1)S(1)}, bf16[2,256,512]{2,1,0:T(8,128)(2,1)}, u32[]{:S(2)}) copy-start(bf16[2,256,512]{2,1,0:T(8,128)(2,1)} %shard_map.95.value.refs_0_) | copy-start | bytes 1572868
  8.0 11.8 %collective-permute-start.3 = (bf16[2,256,512]{2,1,0:T(8,128)(2,1)}, bf16[2,256,512]{2,1,0:T(8,128)(2,1)S(1)}, u32[]{:S(2)}, u32[]{:S(2)}) collective-permute-start(bf16[2,256,512]{2,1,0:T(8,128)(2,1)} %shard_map.96), channel_id=1, source_target_pairs={{0,192},{1,65},{2,194},{3,67},{4,196},{5,69},{6,198},{7,71},{8,200... | collective-permute-start | bytes 1572872 | tf_op jit(solution)/shard_map/ppermute | solution.py:49
  9.7 10.8 %collective-permute-start = (bf16[2,256,512]{2,1,0:T(8,128)(2,1)}, bf16[2,256,512]{2,1,0:T(8,128)(2,1)S(1)}, u32[]{:S(2)}, u32[]{:S(2)}) collective-permute-start(bf16[2,256,512]{2,1,0:T(8,128)(2,1)} %shard_map.96), channel_id=1, source_target_pairs={{0,48},{1,17},{2,50},{3,19},{4,52},{5,21},{6,54},{7,23},{8,56},{9,... | collective-permute-start | bytes 1572872 | tf_op jit(solution)/shard_map/ppermute | solution.py:49
  15.3 11.2 %collective-permute-start.5 = (bf16[2,256,512]{2,1,0:T(8,128)(2,1)S(1)}, bf16[2,256,512]{2,1,0:T(8,128)(2,1)S(1)}, u32[]{:S(2)}, u32[]{:S(2)}) collective-permute-start(bf16[2,256,512]{2,1,0:T(8,128)(2,1)S(1)} %collective-permute-done.4.refs_6_), channel_id=1, source_target_pairs={{0,64},{1,193},{2,66},{3,195},{4,68},{5,197},{6,70},{7,199},{8,72}... | collective-permute-start | bytes 1572872 | tf_op jit(solution)/shard_map/ppermute | solution.py:49
  17.5 10.7 %collective-permute-start.2 = (bf16[2,256,512]{2,1,0:T(8,128)(2,1)S(1)}, bf16[2,256,512]{2,1,0:T(8,128)(2,1)S(1)}, u32[]{:S(2)}, u32[]{:S(2)}) collective-permute-start(bf16[2,256,512]{2,1,0:T(8,128)(2,1)S(1)} %collective-permute-done.1.refs_3_), channel_id=1, source_target_pairs={{0,16},{1,49},{2,18},{3,51},{4,20},{5,53},{6,22},{7,55},{8,24},{9,... | collective-permute-start | bytes 1572872 | tf_op jit(solution)/shard_map/ppermute | solution.py:49
  26.7 15.7 %collective-permute-start.9 = (bf16[3,256,512]{2,1,0:T(8,128)(2,1)S(1)}, bf16[3,256,512]{2,1,0:T(8,128)(2,1)S(1)}, u32[]{:S(2)}, u32[]{:S(2)}) collective-permute-start(bf16[3,256,512]{2,1,0:T(8,128)(2,1)S(1)} %pad_maximum_fusion.1.second_line), channel_id=1, source_target_pairs={{0,16},{1,49},{2,18},{3,51},{4,20},{5,53},{6,22},{7,55},{8,24},{9,... | collective-permute-start | bytes 2359304 | tf_op jit(solution)/shard_map/ppermute | solution.py:49
  28.4 19.4 %collective-permute-start.8 = (bf16[3,256,512]{2,1,0:T(8,128)(2,1)S(1)}, bf16[3,256,512]{2,1,0:T(8,128)(2,1)S(1)}, u32[]{:S(2)}, u32[]{:S(2)}) collective-permute-start(bf16[3,256,512]{2,1,0:T(8,128)(2,1)S(1)} %pad_maximum_fusion.first_line), channel_id=1, source_target_pairs={{0,64},{1,193},{2,66},{3,195},{4,68},{5,197},{6,70},{7,199},{8,72}... | collective-permute-start | bytes 2359304 | tf_op jit(solution)/shard_map/ppermute | solution.py:49
  29.3 19.5 %copy-start.1 = (bf16[2,256,512]{2,1,0:T(8,128)(2,1)S(1)}, bf16[2,256,512]{2,1,0:T(8,128)(2,1)}, u32[]{:S(2)}) copy-start(bf16[2,256,512]{2,1,0:T(8,128)(2,1)} %shard_map.95.value.refs_0_) | copy-start | bytes 1572868
  33.6 21.6 %collective-permute-start.6 = (bf16[3,256,512]{2,1,0:T(8,128)(2,1)S(1)}, bf16[3,256,512]{2,1,0:T(8,128)(2,1)S(1)}, u32[]{:S(2)}, u32[]{:S(2)}) collective-permute-start(bf16[3,256,512]{2,1,0:T(8,128)(2,1)S(1)} %get-tuple-element.26), channel_id=1, source_target_pairs={{0,192},{1,65},{2,194},{3,67},{4,196},{5,69},{6,198},{7,71},{8,200... | collective-permute-start | bytes 2359304 | tf_op jit(solution)/shard_map/ppermute | solution.py:49
  36.1 19.1 %collective-permute-start.7 = (bf16[3,256,512]{2,1,0:T(8,128)(2,1)S(1)}, bf16[3,256,512]{2,1,0:T(8,128)(2,1)S(1)}, u32[]{:S(2)}, u32[]{:S(2)}) collective-permute-start(bf16[3,256,512]{2,1,0:T(8,128)(2,1)S(1)} %get-tuple-element.27), channel_id=1, source_target_pairs={{0,48},{1,17},{2,50},{3,19},{4,52},{5,21},{6,54},{7,23},{8,56},{9,... | collective-permute-start | bytes 2359304 | tf_op jit(solution)/shard_map/ppermute | solution.py:49
  42.4 15.3 %collective-permute-start.12 = (bf16[3,256,512]{2,1,0:T(8,128)(2,1)S(1)}, bf16[3,256,512]{2,1,0:T(8,128)(2,1)S(1)}, u32[]{:S(2)}, u32[]{:S(2)}) collective-permute-start(bf16[3,256,512]{2,1,0:T(8,128)(2,1)S(1)} %collective-permute-done.9.refs_8_), channel_id=1, source_target_pairs={{0,16},{1,49},{2,18},{3,51},{4,20},{5,53},{6,22},{7,55},{8,24},{9,... | collective-permute-start | bytes 2359304 | tf_op jit(solution)/shard_map/ppermute | solution.py:49
  47.8 13.2 %collective-permute-start.11 = (bf16[3,256,512]{2,1,0:T(8,128)(2,1)S(1)}, bf16[3,256,512]{2,1,0:T(8,128)(2,1)S(1)}, u32[]{:S(2)}, u32[]{:S(2)}) collective-permute-start(bf16[3,256,512]{2,1,0:T(8,128)(2,1)S(1)} %collective-permute-done.8.refs_7_), channel_id=1, source_target_pairs={{0,64},{1,193},{2,66},{3,195},{4,68},{5,197},{6,70},{7,199},{8,72}... | collective-permute-start | bytes 2359304 | tf_op jit(solution)/shard_map/ppermute | solution.py:49
  57.6 8.2 %collective-permute-start.10 = (bf16[8,256,512]{2,1,0:T(8,128)(2,1)S(1)}, bf16[8,256,512]{2,1,0:T(8,128)(2,1)S(1)}, u32[]{:S(2)}, u32[]{:S(2)}) collective-permute-start(bf16[8,256,512]{2,1,0:T(8,128)(2,1)S(1)} %get-tuple-element.29), channel_id=1, source_target_pairs={{0,1},{1,0},{2,3},{3,2},{4,5},{5,4},{6,7},{7,6},{8,9},{9,8},{10,11... | collective-permute-start | bytes 6291464 | tf_op jit(solution)/shard_map/ppermute | solution.py:53
  63.1 2.7 %collective-permute-start.20 = (bf16[8,256,256]{2,1,0:T(8,128)(2,1)S(1)}, bf16[8,256,256]{2,1,0:T(8,128)(2,1)S(1)}, u32[]{:S(2)}, u32[]{:S(2)}) collective-permute-start(bf16[8,256,256]{2,1,0:T(8,128)(2,1)S(1)} %get-tuple-element.40), channel_id=1, source_target_pairs={{0,1},{1,0},{2,3},{3,2},{4,5},{5,4},{6,7},{7,6},{8,9},{9,8},{10,11... | collective-permute-start | bytes 3145736 | tf_op jit(solution)/shard_map/ppermute | solution.py:53
  65.1 3.3 %collective-permute-start.13 = (bf16[8,256,256]{2,1,0:T(8,128)(2,1)S(1)}, bf16[8,256,256]{2,1,0:T(8,128)(2,1)S(1)}, u32[]{:S(2)}, u32[]{:S(2)}) collective-permute-start(bf16[8,256,256]{2,1,0:T(8,128)(2,1)S(1)} %get-tuple-element.31), channel_id=1, source_target_pairs={{0,1},{1,0},{2,3},{3,2},{4,5},{5,4},{6,7},{7,6},{8,9},{9,8},{10,11... | collective-permute-start | bytes 3145736 | tf_op jit(solution)/shard_map/ppermute | solution.py:53
  66.3 12.0 %collective-permute-start.21 = (bf16[2,256,256]{2,1,0:T(8,128)(2,1)S(1)}, bf16[2,256,256]{2,1,0:T(8,128)(2,1)S(1)}, u32[]{:S(2)}, u32[]{:S(2)}) collective-permute-start(bf16[2,256,256]{2,1,0:T(8,128)(2,1)S(1)} %get-tuple-element.42), channel_id=1, source_target_pairs={{0,2},{1,15},{2,4},{3,1},{4,6},{5,3},{6,8},{7,5},{8,10},{9,7},{10,... | collective-permute-start | bytes 786440 | tf_op jit(solution)/shard_map/ppermute | solution.py:49
  68.8 28.6 %copy-start.2 = (bf16[1,1,1,256,512]{4,3,2,1,0:T(8,128)(2,1)S(1)}, bf16[1,1,1,256,512]{4,3,2,1,0:T(8,128)(2,1)}, u32[]{:S(2)}) copy-start(bf16[1,1,1,256,512]{4,3,2,1,0:T(8,128)(2,1)} %param.10) | copy-start | bytes 786436
  68.8 28.6 %copy-start.3 = (bf16[1,1,1,256,256]{4,3,2,1,0:T(8,128)(2,1)S(1)}, bf16[1,1,1,256,256]{4,3,2,1,0:T(8,128)(2,1)}, u32[]{:S(2)}) copy-start(bf16[1,1,1,256,256]{4,3,2,1,0:T(8,128)(2,1)} %param.11) | copy-start | bytes 393220
  68.8 13.8 %collective-permute-start.14 = (bf16[2,256,256]{2,1,0:T(8,128)(2,1)S(1)}, bf16[2,256,256]{2,1,0:T(8,128)(2,1)S(1)}, u32[]{:S(2)}, u32[]{:S(2)}) collective-permute-start(bf16[2,256,256]{2,1,0:T(8,128)(2,1)S(1)} %get-tuple-element.33), channel_id=1, source_target_pairs={{0,2},{1,15},{2,4},{3,1},{4,6},{5,3},{6,8},{7,5},{8,10},{9,7},{10,... | collective-permute-start | bytes 786440 | tf_op jit(solution)/shard_map/ppermute | solution.py:49
  70.7 7.6 %collective-permute-start.22 = (bf16[256,256]{1,0:T(8,128)(2,1)S(1)}, bf16[256,256]{1,0:T(8,128)(2,1)S(1)}, u32[]{:S(2)}, u32[]{:S(2)}) collective-permute-start(bf16[256,256]{1,0:T(8,128)(2,1)S(1)} %get-tuple-element.43), channel_id=1, source_target_pairs={{0,14},{1,3},{2,0},{3,5},{4,2},{5,7},{6,4},{7,9},{8,6},{9,11},{10,... | collective-permute-start | bytes 393224 | tf_op jit(solution)/shard_map/ppermute | solution.py:49
  74.4 8.2 %collective-permute-start.15 = (bf16[256,256]{1,0:T(8,128)(2,1)S(1)}, bf16[256,256]{1,0:T(8,128)(2,1)S(1)}, u32[]{:S(2)}, u32[]{:S(2)}) collective-permute-start(bf16[256,256]{1,0:T(8,128)(2,1)S(1)} %get-tuple-element.34), channel_id=1, source_target_pairs={{0,14},{1,3},{2,0},{3,5},{4,2},{5,7},{6,4},{7,9},{8,6},{9,11},{10,... | collective-permute-start | bytes 393224 | tf_op jit(solution)/shard_map/ppermute | solution.py:49
  78.4 9.9 %collective-permute-start.23 = (bf16[256,256]{1,0:T(8,128)(2,1)S(1)}, bf16[256,256]{1,0:T(8,128)(2,1)S(1)}, u32[]{:S(2)}, u32[]{:S(2)}) collective-permute-start(bf16[256,256]{1,0:T(8,128)(2,1)S(1)} %get-tuple-element.44), channel_id=1, source_target_pairs={{0,4},{1,13},{2,6},{3,15},{4,8},{5,1},{6,10},{7,3},{8,12},{9,5},{1... | collective-permute-start | bytes 393224 | tf_op jit(solution)/shard_map/ppermute | solution.py:49
  81.4 8.4 %collective-permute-start.24 = (bf16[256,256]{1,0:T(8,128)(2,1)S(1)}, bf16[256,256]{1,0:T(8,128)(2,1)S(1)}, u32[]{:S(2)}, u32[]{:S(2)}) collective-permute-start(bf16[256,256]{1,0:T(8,128)(2,1)S(1)} %get-tuple-element.45), channel_id=1, source_target_pairs={{0,14},{1,3},{2,0},{3,5},{4,2},{5,7},{6,4},{7,9},{8,6},{9,11},{10,... | collective-permute-start | bytes 393224 | tf_op jit(solution)/shard_map/ppermute | solution.py:49
  82.7 10.6 %collective-permute-start.16 = (bf16[256,256]{1,0:T(8,128)(2,1)S(1)}, bf16[256,256]{1,0:T(8,128)(2,1)S(1)}, u32[]{:S(2)}, u32[]{:S(2)}) collective-permute-start(bf16[256,256]{1,0:T(8,128)(2,1)S(1)} %get-tuple-element.35), channel_id=1, source_target_pairs={{0,4},{1,13},{2,6},{3,15},{4,8},{5,1},{6,10},{7,3},{8,12},{9,5},{1... | collective-permute-start | bytes 393224 | tf_op jit(solution)/shard_map/ppermute | solution.py:49
  85.9 7.3 %collective-permute-start.17 = (bf16[256,256]{1,0:T(8,128)(2,1)S(1)}, bf16[256,256]{1,0:T(8,128)(2,1)S(1)}, u32[]{:S(2)}, u32[]{:S(2)}) collective-permute-start(bf16[256,256]{1,0:T(8,128)(2,1)S(1)} %get-tuple-element.36), channel_id=1, source_target_pairs={{0,14},{1,3},{2,0},{3,5},{4,2},{5,7},{6,4},{7,9},{8,6},{9,11},{10,... | collective-permute-start | bytes 393224 | tf_op jit(solution)/shard_map/ppermute | solution.py:49
  89.9 6.7 %collective-permute-start.25 = (bf16[256,256]{1,0:T(8,128)(2,1)S(1)}, bf16[256,256]{1,0:T(8,128)(2,1)S(1)}, u32[]{:S(2)}, u32[]{:S(2)}) collective-permute-start(bf16[256,256]{1,0:T(8,128)(2,1)S(1)} %get-tuple-element.46), channel_id=1, source_target_pairs={{0,2},{1,15},{2,4},{3,1},{4,6},{5,3},{6,8},{7,5},{8,10},{9,7},{10,... | collective-permute-start | bytes 393224 | tf_op jit(solution)/shard_map/ppermute | solution.py:49
  91.3 6.1 %collective-permute-start.26 = (bf16[256,256]{1,0:T(8,128)(2,1)S(1)}, bf16[256,256]{1,0:T(8,128)(2,1)S(1)}, u32[]{:S(2)}, u32[]{:S(2)}) collective-permute-start(bf16[256,256]{1,0:T(8,128)(2,1)S(1)} %get-tuple-element.47), channel_id=1, source_target_pairs={{0,14},{1,3},{2,0},{3,5},{4,2},{5,7},{6,4},{7,9},{8,6},{9,11},{10,... | collective-permute-start | bytes 393224 | tf_op jit(solution)/shard_map/ppermute | solution.py:49
  93.3 6.8 %collective-permute-start.18 = (bf16[256,256]{1,0:T(8,128)(2,1)S(1)}, bf16[256,256]{1,0:T(8,128)(2,1)S(1)}, u32[]{:S(2)}, u32[]{:S(2)}) collective-permute-start(bf16[256,256]{1,0:T(8,128)(2,1)S(1)} %get-tuple-element.37), channel_id=1, source_target_pairs={{0,2},{1,15},{2,4},{3,1},{4,6},{5,3},{6,8},{7,5},{8,10},{9,7},{10,... | collective-permute-start | bytes 393224 | tf_op jit(solution)/shard_map/ppermute | solution.py:49
  94.8 5.4 %collective-permute-start.19 = (bf16[256,256]{1,0:T(8,128)(2,1)S(1)}, bf16[256,256]{1,0:T(8,128)(2,1)S(1)}, u32[]{:S(2)}, u32[]{:S(2)}) collective-permute-start(bf16[256,256]{1,0:T(8,128)(2,1)S(1)} %get-tuple-element.38), channel_id=1, source_target_pairs={{0,14},{1,3},{2,0},{3,5},{4,2},{5,7},{6,4},{7,9},{8,6},{9,11},{10,... | collective-permute-start | bytes 393224 | tf_op jit(solution)/shard_map/ppermute | solution.py:49
